TPU v7x, 256 devices: a whole 4x4x8 slice. The times are simulated.
256 devices in a mesh: space: 16 (over x_lo, z), mode: 16 (over y, x_hi, core).
Axes of the slice: x: 4 (x_hi: 2, x_lo: 2; x = x_hi * 2 + x_lo), y: 4, z: 8, core: 2. Of those that a mesh axis runs over, the one named last changes fastest.
Arguments:
- pressure: float32 [176, 176, 32, 128], P('mode', 'space'), may hold values from -6 to 6
- source: float32 [176, 176, 32, 128], P('mode', 'space'), may hold values from -6 to 6
- concentration: float32 [176, 176, 32, 128], P('mode', 'space'), may hold values from -6 to 6
- mean_cond: float32 [176, 32, 128], P('space'), may hold values from 1 to 10
- kl_cond: float32 [8, 176, 32, 128], P(None, 'space'), may hold values from -4 to 4
- mode_table: int32 [176, 8], replicated, may hold values from -1 to 3, as said below
Outputs:
- pressure_next: float32 [176, 176, 32, 128], P('mode', 'space')
- concentration_next: float32 [176, 176, 32, 128], P('mode', 'space')
Inputs may be any that keep to these rules, and one draw needn't show every extreme that they name: `mode_table`: each row is either a multi-index of 8 degrees with total at most 3, or all -1; every such multi-index is exactly one row, in a shuffled order.
All inputs are finite; a program needn't handle non-finite values.
Results may differ from a plain program's by a relative error of at most 0.0036.
Values may be sent and summed in bfloat16 or wider, within the bound.
No kernel may reach another device: no remote copies, remote signals or barrier semaphores. Data moves between devices by JAX's collectives and lax.ppermute only.
A program may use at most 192 MiB of HBM per device.

v0:
```python
import jax
import jax.numpy as jnp
from jax import lax
from jax.sharding import PartitionSpec as P

OMEGA = 0.8
DISPERSION = 0.01
STEP = 0.05


def with_halo(cells, sides, width):
    for axis, dim in sides:
        count = lax.axis_size(axis)
        ends = count - 1
        head = lax.slice_in_dim(cells, 0, width, axis=dim)
        tail = lax.slice_in_dim(cells, cells.shape[dim] - width, cells.shape[dim], axis=dim)
        cells = jnp.concatenate(
            [
                lax.ppermute(tail, axis, [(i, (i + 1) % count) for i in range(ends)]),
                cells,
                lax.ppermute(head, axis, [((i + 1) % count, i) for i in range(ends)]),
            ],
            axis=dim,
        )
    return cells


def spread(block, axis, owner):
    block = jnp.where(lax.axis_index(axis) == owner, block, jnp.zeros_like(block))
    return lax.psum(block, axis)


def coupling(mode_table):
    is_valid = mode_table[:, 0] >= 0
    both_valid = is_valid[:, None] & is_valid[None, :]
    distance = jnp.abs(mode_table[:, None, :] - mode_table[None, :, :])
    total_gap = jnp.sum(distance, axis=2)
    larger = jnp.maximum(mode_table[:, None, :], mode_table[None, :, :]).astype(jnp.float32)
    mean_part = jnp.where(both_valid & (total_gap == 0), 1.0, 0.0).astype(jnp.float32)
    kl_terms = jnp.where(
        (both_valid & (total_gap == 1))[:, :, None] & (distance == 1),
        jnp.sqrt(jnp.maximum(larger, 1.0)),
        0.0,
    )
    tensor = jnp.concatenate([mean_part[:, None, :], jnp.transpose(kl_terms, (0, 2, 1))], axis=1)
    return tensor.astype(jnp.bfloat16)


def laplace(extended):
    centre = extended[:, 1:-1]
    padded = jnp.pad(centre, ((0, 0), (0, 0), (1, 1), (1, 1)))
    beside_all = extended[:, 2:] + extended[:, :-2]
    beside_all = beside_all + padded[:, :, 2:, 1:-1] + padded[:, :, :-2, 1:-1]
    beside_all = beside_all + padded[:, :, 1:-1, 2:] + padded[:, :, 1:-1, :-2]
    return 6.0 * centre - beside_all


def gradients(extended):
    centre = extended[:, 1:-1]
    padded = jnp.pad(centre, ((0, 0), (0, 0), (1, 1), (1, 1)))
    along_x = 0.5 * (extended[:, 2:] - extended[:, :-2])
    along_y = 0.5 * (padded[:, :, 2:, 1:-1] - padded[:, :, :-2, 1:-1])
    along_z = 0.5 * (padded[:, :, 1:-1, 2:] - padded[:, :, 1:-1, :-2])
    return (along_x, along_y, along_z)


def weighted(products, mean_cond, kl_cond):
    result = mean_cond[None] * products[0]
    for kl_index in range(kl_cond.shape[0]):
        result = result + kl_cond[kl_index][None] * products[kl_index + 1]
    return result


def local(pressure, source, concentration, mean_cond, kl_cond, mode_table):
    local_modes = pressure.shape[0]
    tensor = coupling(mode_table)
    both_fields = jnp.concatenate([pressure, concentration], axis=0)
    extended = with_halo(both_fields, (("space", 1),), 1)
    lap_all = laplace(extended).astype(jnp.bfloat16)
    lap_press = lap_all[:local_modes]
    lap_conc = lap_all[local_modes:]
    mode_rank = lax.axis_index("mode")
    columns = lax.dynamic_slice_in_dim(tensor, mode_rank * local_modes, local_modes, 2)
    whole_press, whole_conc = (
        lax.all_gather(lap_press, "mode", axis=0, tiled=True),
        lax.all_gather(lap_conc, "mode", axis=0, tiled=True),
    )
    prod_press = jnp.einsum(
        "jxyz,jtk->tkxyz", whole_press, columns, preferred_element_type=jnp.float32
    )
    galerkin_press = weighted(prod_press, mean_cond, kl_cond)
    prod_conc = jnp.einsum(
        "jxyz,jtk->tkxyz", whole_conc, columns, preferred_element_type=jnp.float32
    )
    galerkin_conc = weighted(prod_conc, mean_cond, kl_cond)
    pressure_next = pressure + OMEGA * (source - galerkin_press) / (6.0 * mean_cond[None])
    is_mean = (jnp.sum(jnp.abs(mode_table), axis=1) == 0).astype(jnp.int32)
    mean_row = jnp.argmax(is_mean)
    owner_rank = mean_row // local_modes
    head_plane = lax.dynamic_slice_in_dim(pressure_next, mean_row % local_modes, 1, 0)
    head_plane = spread(head_plane, "mode", owner_rank)
    head_ext = with_halo(head_plane, (("space", 1),), 1)
    head_x, head_y, head_z = gradients(head_ext)
    vel_x = -mean_cond[None] * head_x
    vel_y = -mean_cond[None] * head_y
    vel_z = -mean_cond[None] * head_z
    conc_x, conc_y, conc_z = gradients(extended[local_modes:])
    advection = vel_x * conc_x + vel_y * conc_y + vel_z * conc_z
    concentration_next = concentration - DISPERSION * galerkin_conc - STEP * advection
    return (pressure_next, concentration_next)


def solution(mesh):
    return jax.shard_map(
        local,
        mesh=mesh,
        in_specs=(
            P("mode", "space", None, None),
            P("mode", "space", None, None),
            P("mode", "space", None, None),
            P("space", None, None),
            P(None, "space", None, None),
            P(),
        ),
        out_specs=(P("mode", "space", None, None), P("mode", "space", None, None)),
        check_vma=False,
    )
```

profile of v0, /device:TPU:2, one launch (start us, length us, event | category | flops | bytes accessed | tf_op | source)
XLA Modules:
  0.0 482.6 jit_solution(284276370086791266)
XLA Ops:
  7.2 0.0 all-gather.3.cloned.1.call-start
  7.2 0.0 copy-start.3
  7.2 3.0 copy.36
  10.2 0.0 copy-done.3
  10.2 1.3 copy.40
  11.5 0.1 fusion.62
  11.6 7.7 %collective-permute-start = (f32[22,1,32,128]{3,0,2,1:T(8,128)S(1)}, f32[22,1,32,128]{3,0,2,1:T(8,128)S(1)}, u32[]{:S(2)}, u32[]{:S(2)}) collective-permute-start(f32[22,1,32,128]{3,0,2,1:T(8,128)S(1)} %get-tuple-element.12), channel_id=1, source_target_pairs={{16,0},{32,16},{48,32},{64,48},{80,64},{96,80},{112,96},{128,112},... | collective-permute-start | bytes 1081352 | tf_op jit(solution)/shard_map/ppermute | solution.py:21
  19.4 1.9 collective-permute-start.1
  21.3 0.5 pad_maximum_fusion
  21.8 5.9 %collective-permute-done = f32[22,1,32,128]{3,0,2,1:T(8,128)S(1)} collective-permute-done((f32[22,1,32,128]{3,0,2,1:T(8,128)S(1)}, f32[22,1,32,128]{3,0,2,1:T(8,128)S(1)}, u32[]{:S(2)}, u32[]{:S(2)}) %collective-permute-start) | collective-permute-done | bytes 360480 | tf_op jit(solution)/shard_map/ppermute | solution.py:21
  27.7 6.2 %collective-permute-done.1 = f32[22,1,32,128]{3,0,2,1:T(8,128)S(1)} collective-permute-done((f32[22,1,32,128]{3,0,2,1:T(8,128)S(1)}, f32[22,1,32,128]{3,0,2,1:T(8,128)S(1)}, u32[]{:S(2)}, u32[]{:S(2)}) %collective-permute-start.1) | collective-permute-done | bytes 360480 | tf_op jit(solution)/shard_map/ppermute | solution.py:19
  33.9 1.2 pad_maximum_fusion.1
  35.2 0.0 copy-start
  35.2 0.0 copy-start.1
  35.2 2.6 fusion.11
  37.8 0.0 copy-done
  37.8 0.9 copy-done.1
  38.7 1.8 fusion.72
  40.5 0.0 copy-start.7
  40.5 0.0 copy-start.4
  40.5 1.2 copy.37
  41.7 0.0 all-gather.3.cloned.1.call-update
  41.7 0.2 all-reduce.5.cloned.1.call-start
  41.9 0.0 copy-done.7
  41.9 0.1 copy.32
  42.1 0.7 fusion.69
  44.9 0.6 abs_reduce_fusion
  45.5 0.1 copy.33
  45.7 0.1 compare_and_fusion
  45.8 0.1 copy.34
  45.9 0.1 select_convert_fusion.1
  46.0 0.0 copy-done.4
  46.1 0.8 fusion.74
  46.8 1.9 select_convert_fusion
  48.7 2.4 slice_bitcast_fusion.25
  51.2 96.4 %all-gather.3.cloned.1.call-done = bf16[176,11,32,128]{3,2,1,0:T(8,128)(2,1)} async-done(((bf16[11,11,32,128]{3,2,1,0:T(8,128)(2,1)}), bf16[176,11,32,128]{3,2,1,0:T(8,128)(2,1)}) %all-gather.3.cloned.1.call-update) | async-done | bytes 15859728 | tf_op jit(solution)/shard_map/all_gather | solution.py:85
  147.5 21.1 %fusion.2 = f32[9,11,11,32,128]{4,1,3,2,0:T(8,128)} fusion(bf16[176,11,32,128]{3,2,1,0:T(8,128)(2,1)} %all-gather.3.cloned.1.call-done, s32[]{:T(128)S(6)} %select_n.47, bf16[176,1,176]{0,2,1:T(8,128)(2,1)S(1)} %select_convert_fusion.1, bf16[176,8,176]{0,2,1:T(8,128)(2,1)} %select_convert_fusion), kind=kOutput, calls=%fused_computation.2 | convolution fusion | flops 1570181120 | bytes 34259460 | tf_op jit(solution)/shard_map/jxyz,jtk->tkxyz/dot_general | solution.py:88
  168.6 13.1 %fusion.45 = f32[11,11,32,128]{3,0,2,1:T(8,128)S(1)} fusion(f32[9,11,11,32,128]{4,1,3,2,0:T(8,128)} %fusion.2, f32[11,11,32,128]{3,2,1,0:T(8,128)} %param.7, f32[11,32,128]{2,1,0:T(8,128)} %get-tuple-element.30, f32[11,32,128]{2,1,0:T(8,128)} %get-tuple-element.22, f32[11,32,128]{2,1,0:T(8,128)} %get-tuple-element.23, ...), kind=kLoop, calls=%fused_computation.72 | loop fusion | flops 10407936 | bytes 25591808 | tf_op jit(solution)/shard_map/add | solution.py:96
  181.7 0.0 copy-start.2
  181.7 1.6 copy-done.2
  183.3 0.9 broadcast_select_fusion
  184.2 0.0 all-reduce.5.cloned.1.call-update
  184.2 0.0 all-gather.5.cloned.1.call-start
  184.3 2.6 copy.41
  186.8 0.0 all-gather.5.cloned.1.call-update
  186.9 132.3 %all-reduce.5.cloned.1.call-done = f32[1,11,32,128]{3,0,2,1:T(1,128)} async-done(((f32[1,11,32,128]{3,0,2,1:T(1,128)}), f32[1,11,32,128]{3,0,2,1:T(1,128)}) %all-reduce.5.cloned.1.call-update) | async-done | bytes 180240 | tf_op jit(solution)/shard_map/psum | solution.py:30
  319.2 1.3 fusion.73
  320.6 5.2 %collective-permute-start.2 = (f32[1,1,32,128]{3,0,2,1:T(1,128)}, f32[1,1,32,128]{3,0,2,1:T(1,128)S(1)}, u32[]{:S(2)}, u32[]{:S(2)}) collective-permute-start(f32[1,1,32,128]{3,0,2,1:T(1,128)} %get-tuple-element.27), channel_id=1, source_target_pairs={{16,0},{32,16},{48,32},{64,48},{80,64},{96,80},{112,96},{128,112},... | collective-permute-start | bytes 49160 | tf_op jit(solution)/shard_map/ppermute | solution.py:21
  325.8 2.1 collective-permute-start.3
  327.9 102.3 %all-gather.5.cloned.1.call-done = bf16[176,11,32,128]{3,2,1,0:T(8,128)(2,1)} async-done(((bf16[11,11,32,128]{3,2,1,0:T(8,128)(2,1)}), bf16[176,11,32,128]{3,2,1,0:T(8,128)(2,1)}) %all-gather.5.cloned.1.call-update) | async-done | bytes 15859728 | tf_op jit(solution)/shard_map/all_gather | solution.py:86
  430.2 21.1 %fusion = f32[9,11,11,32,128]{4,1,3,2,0:T(8,128)} fusion(bf16[176,11,32,128]{3,2,1,0:T(8,128)(2,1)} %all-gather.5.cloned.1.call-done, s32[]{:T(128)S(6)} %select_n.47, bf16[176,1,176]{0,2,1:T(8,128)(2,1)S(1)} %select_convert_fusion.1, bf16[176,8,176]{0,2,1:T(8,128)(2,1)} %select_convert_fusion), kind=kOutput, calls=%fused_computation | convolution fusion | flops 1570181120 | bytes 34259460 | tf_op jit(solution)/shard_map/jxyz,jtk->tkxyz/dot_general | solution.py:92
  451.3 0.0 copy-start.5
  451.3 0.0 copy-start.6
  451.3 3.8 copy.45
  455.1 0.0 collective-permute-done.2
  455.1 0.0 collective-permute-done.3
  455.1 0.0 copy-done.5
  455.1 0.0 copy-done.6
  455.1 1.6 multiply_multiply_fusion.2
  456.7 15.7 %fusion.17 = f32[11,11,32,128]{3,0,2,1:T(8,128)} fusion(f32[11,11,32,128]{3,0,2,1:T(8,128)S(1)} %copy.36, f32[22,12,32,128]{3,0,2,1:T(8,128)} %copy-done.1, f32[22,12,32,128]{3,0,2,1:T(8,128)} %copy-done, f32[9,11,11,32,128]{4,1,3,2,0:T(8,128)} %fusion, f32[11,32,128]{2,1,0:T(8,128)} %bitcast.189, f32[11,32,128]{2,1,0:T(8,128)} %bitcast.190, ...), kind=kLoop, calls=%fused_computation.33 | loop fusion | flops 14372864 | bytes 27934720 | tf_op jit(solution)/shard_map/sub | solution.py:109
  472.4 3.7 copy.46
  (2 shorter events, 0.0 us)
Async XLA Ops:
  7.2 140.4 %all-gather.3.cloned.1.call-start = ((), (), s32[]{:S(2)}) async-start(), calls=%async_computation | async-start | bytes 16850944 | tf_op jit(solution)/shard_map/all_gather | solution.py:85
  7.2 3.0 copy-start.3
  11.6 16.1 %collective-permute-start = (f32[22,1,32,128]{3,0,2,1:T(8,128)S(1)}, f32[22,1,32,128]{3,0,2,1:T(8,128)S(1)}, u32[]{:S(2)}, u32[]{:S(2)}) collective-permute-start(f32[22,1,32,128]{3,0,2,1:T(8,128)S(1)} %get-tuple-element.12), channel_id=1, source_target_pairs={{16,0},{32,16},{48,32},{64,48},{80,64},{96,80},{112,96},{128,112},... | collective-permute-start | bytes 1081352 | tf_op jit(solution)/shard_map/ppermute | solution.py:21
  19.4 14.6 %collective-permute-start.1 = (f32[22,1,32,128]{3,0,2,1:T(8,128)S(1)}, f32[22,1,32,128]{3,0,2,1:T(8,128)S(1)}, u32[]{:S(2)}, u32[]{:S(2)}) collective-permute-start(f32[22,1,32,128]{3,0,2,1:T(8,128)S(1)} %get-tuple-element.13), channel_id=1, source_target_pairs={{0,16},{16,32},{32,48},{48,64},{64,80},{80,96},{96,112},{112,128},... | collective-permute-start | bytes 1081352 | tf_op jit(solution)/shard_map/ppermute | solution.py:19
  35.2 2.6 copy-start
  35.2 3.5 copy-start.1
  40.5 1.5 copy-start.7
  40.5 5.6 %copy-start.4 = (f32[11,32,128]{2,1,0:T(8,128)S(1)}, f32[11,32,128]{2,1,0:T(8,128)}, u32[]{:S(2)}) copy-start(f32[11,32,128]{2,1,0:T(8,128)} %param.9) | copy-start | bytes 540676
  41.7 277.5 %all-reduce.5.cloned.1.call-start = ((), (), s32[]{:S(2)}) async-start(), calls=%async_computation.2 | async-start | bytes 360448 | tf_op jit(solution)/shard_map/psum | solution.py:30
  181.7 1.6 copy-start.2
  184.2 246.0 %all-gather.5.cloned.1.call-start = ((), (), s32[]{:S(2)}) async-start(), calls=%async_computation.1 | async-start | bytes 16850944 | tf_op jit(solution)/shard_map/all_gather | solution.py:86
  320.6 134.5 %collective-permute-start.2 = (f32[1,1,32,128]{3,0,2,1:T(1,128)}, f32[1,1,32,128]{3,0,2,1:T(1,128)S(1)}, u32[]{:S(2)}, u32[]{:S(2)}) collective-permute-start(f32[1,1,32,128]{3,0,2,1:T(1,128)} %get-tuple-element.27), channel_id=1, source_target_pairs={{16,0},{32,16},{48,32},{64,48},{80,64},{96,80},{112,96},{128,112},... | collective-permute-start | bytes 49160 | tf_op jit(solution)/shard_map/ppermute | solution.py:21
  325.8 129.3 %collective-permute-start.3 = (f32[1,1,32,128]{3,0,2,1:T(1,128)}, f32[1,1,32,128]{3,0,2,1:T(1,128)S(1)}, u32[]{:S(2)}, u32[]{:S(2)}) collective-permute-start(f32[1,1,32,128]{3,0,2,1:T(1,128)} %get-tuple-element.28), channel_id=1, source_target_pairs={{0,16},{16,32},{32,48},{48,64},{64,80},{80,96},{96,112},{112,128},... | collective-permute-start | bytes 49160 | tf_op jit(solution)/shard_map/ppermute | solution.py:19
  451.3 3.8 copy-start.5
  451.3 3.8 copy-start.6
Sparse Core Ops, SparseCore 0:
  41.8 105.6 all-gather.2
  184.3 134.8 all-reduce.4
  322.9 107.2 all-gather.4
where the time goes:
time: 485 us; the launch traced here: 483 us
  waiting for transfers between devices  343 us (71%)
  matrix products  42.1 us (9%)
  other arithmetic  39.9 us (8%)
  local copies, waits for them, and re-layouts  24 us (5%)
  starting transfers between devices  17.3 us (4%)
  between operations  16.1 us (3%)
    psum x1, waiting for transfers between devices, spread(): return lax.psum(block, axis)  132 us
    all_gather x1, waiting for transfers between devices, local(): lax.all_gather(lap_conc, 'mode', axis=0, tiled=True)  102 us
    all_gather x1, waiting for transfers between devices, local(): lax.all_gather(lap_press, 'mode', axis=0, tiled=True)  96.4 us
    dot_general x1, matrix products, local(): jnp.einsum('jxyz,jtk->tkxyz', whole_conc, columns, preferred_element_type...  21.1 us
    dot_general x1, matrix products, local(): jnp.einsum('jxyz,jtk->tkxyz', whole_press, columns, preferred_element_typ...  21.1 us
    sub x1, other arithmetic, local(): concentration - DISPERSION * galerkin_conc - STEP * advection  15.7 us
    unnamed x21, local copies, waits for them, and re-layouts  14.4 us
    add x1, other arithmetic, local(): pressure + OMEGA * (source - galerkin_press) / (6.0 * mean_cond[None])  13.1 us
  transfers between devices with their start and end apart: 7, of which 5 were waited for; matrix products, arithmetic and copies ran while one was open for 8% of the time, Pallas kernels for 0%

commit v1 on v0

v1 whole, which is shorter than its diff:
```python
import functools

import jax
import jax.numpy as jnp
from jax import lax
from jax.experimental import pallas as pl
from jax.experimental.pallas import tpu as pltpu
from jax.sharding import PartitionSpec as P

OMEGA = 0.8
DISPERSION = 0.01
STEP = 0.05

F32 = jnp.float32
BF16 = jnp.bfloat16

RANKS = 16
MODES = 11
PLANES = 11
CY = 32
CZ = 128
KL = 8
ALL = RANKS * MODES
HALVES = CY // RANKS
SPOTS = PLANES * HALVES
BODY = SPOTS * MODES
HIGH = BODY
LOW = BODY + SPOTS
ROWS_HEAD = 288
ROWS = 256
VMEM_LIMIT = 48 * 1024 * 1024


def vmem():
    return pl.BlockSpec(memory_space=pltpu.VMEM)


def smem():
    return pl.BlockSpec(memory_space=pltpu.SMEM)


def call(kernel, outs, ins, scratch, name, flops, moved):
    return pl.pallas_call(
        kernel,
        out_shape=outs,
        in_specs=ins,
        out_specs=jax.tree.map(lambda _: vmem(), outs),
        scratch_shapes=scratch,
        compiler_params=pltpu.CompilerParams(vmem_limit_bytes=VMEM_LIMIT),
        cost_estimate=pl.CostEstimate(flops=flops, bytes_accessed=moved, transcendentals=0),
        name=name,
    )


def coupling_kernel(column_ref, row_ref, out_ref):
    for block in range(ALL // 16):
        rows = pl.ds(block * 16, 16)
        columns = column_ref[rows, :]
        gap = jnp.zeros((16, 256), jnp.int32)
        steps = []
        for d in range(KL):
            column = columns[:, d : d + 1]
            row = row_ref[d : d + 1, :]
            step = jnp.abs(column - row)
            gap = gap + step
            steps.append((step, jnp.maximum(column, row)))
        valid = (columns[:, 0:1] >= 0) & (row_ref[0:1, :] >= 0)
        beside = valid & (gap == 1)
        for d in range(KL):
            step, larger = steps[d]
            root = jnp.sqrt(jnp.maximum(larger, 1).astype(F32))
            out_ref[d, rows, :] = jnp.where(beside & (step == 1), root, 0.0).astype(BF16)


def edge_masks():
    row = lax.broadcasted_iota(jnp.int32, (CY, CZ), 0)
    lane = lax.broadcasted_iota(jnp.int32, (CY, CZ), 1)
    return row == 0, row == CY - 1, lane == 0, lane == CZ - 1


def beside(tile, masks):
    first_row, last_row, first_lane, last_lane = masks
    y_less = jnp.where(first_row, 0.0, pltpu.roll(tile, 1, 0))
    y_more = jnp.where(last_row, 0.0, pltpu.roll(tile, CY - 1, 0))
    z_less = jnp.where(first_lane, 0.0, pltpu.roll(tile, 1, 1))
    z_more = jnp.where(last_lane, 0.0, pltpu.roll(tile, CZ - 1, 1))
    return y_less, y_more, z_less, z_more


def spread_rows(scratch, rows, row, tile):
    for half in range(HALVES):
        scratch[pl.ds(row + half * MODES, RANKS, stride=rows), :] = tile[half * RANKS : (half + 1) * RANKS]


def gather_rows(scratch, rows, row, gap):
    return jnp.concatenate(
        [scratch[pl.ds(row + half * gap, RANKS, stride=rows), :] for half in range(HALVES)], axis=0
    )


def pack(scratch, rows, out_ref):
    def one(rank, carry):
        for block in range(rows // 16):
            start = pl.multiple_of(rank * rows + block * 16, 16)
            out_ref[rank, pl.ds(block * 16, 16), :] = scratch[pl.ds(start, 16), :].astype(BF16)
        return carry

    lax.fori_loop(0, RANKS, one, 0)


def unpack(in_ref, rows, scratch):
    def one(rank, carry):
        for block in range(rows // 16):
            start = pl.multiple_of(rank * rows + block * 16, 16)
            scratch[pl.ds(start, 16), :] = in_ref[rank, pl.ds(block * 16, 16), :].astype(F32)
        return carry

    lax.fori_loop(0, RANKS, one, 0)


def laplace_rows(field_ref, low_ref, high_ref, offset, scratch, rows, finish):
    masks = edge_masks()

    def one_mode(m, carry):
        for x in range(PLANES):
            tile = field_ref[m, x]
            below = field_ref[m, x - 1] if x > 0 else low_ref[offset + m].astype(F32)
            above = field_ref[m, x + 1] if x < PLANES - 1 else high_ref[offset + m].astype(F32)
            y_less, y_more, z_less, z_more = beside(tile, masks)
            total = ((above + below) + (y_more + y_less)) + (z_more + z_less)
            image = (6.0 * tile - total).astype(BF16).astype(F32)
            for half in range(HALVES):
                scratch[pl.ds((x * HALVES + half) * MODES + m, RANKS, stride=rows), :] = image[
                    half * RANKS : (half + 1) * RANKS
                ]
            finish(m, x, tile, image)
        return carry

    lax.fori_loop(0, MODES, one_mode, 0)


def pressure_kernel(
    facts, field_ref, source_ref, low_ref, high_ref, mean_ref, send_ref, base_ref, scratch, scale
):
    rows = ROWS_HEAD
    scale[...] = OMEGA / (6.0 * mean_ref[...])

    def finish(m, x, tile, image):
        own = facts[4 + m].astype(F32)
        rest = source_ref[m, x] - own * (mean_ref[x] * image)
        base_ref[m, x] = tile + scale[x] * rest

    laplace_rows(field_ref, low_ref, high_ref, 0, scratch, rows, finish)
    slot = facts[2]
    for x in range(PLANES):
        head = field_ref[slot, x] + scale[x] * source_ref[slot, x]
        high = head.astype(BF16).astype(F32)
        for half in range(HALVES):
            part = slice(half * RANKS, (half + 1) * RANKS)
            scratch[pl.ds(HIGH + x * HALVES + half, RANKS, stride=rows), :] = high[part]
            scratch[pl.ds(LOW + x * HALVES + half, RANKS, stride=rows), :] = (head - high)[part]
    for rank in range(RANKS):
        start = rank * rows + LOW + SPOTS
        scratch[start : (rank + 1) * rows, :] = jnp.zeros((rows - LOW - SPOTS, CZ), F32)
    pack(scratch, rows, send_ref)


def concentration_kernel(
    facts, field_ref, low_ref, high_ref, mean_ref, send_ref, base_ref, scratch
):
    rows = ROWS

    def finish(m, x, tile, image):
        own = facts[4 + m].astype(F32) * DISPERSION
        base_ref[m, x] = tile - own * (mean_ref[x] * image)

    laplace_rows(field_ref, low_ref, high_ref, MODES, scratch, rows, finish)
    for rank in range(RANKS):
        scratch[rank * rows + BODY : (rank + 1) * rows, :] = jnp.zeros((rows - BODY, CZ), F32)
    pack(scratch, rows, send_ref)


def contract_kernel(with_head, facts, recv_ref, tensor_ref, kl_ref, mean_ref, send_ref, images, block, sums, outs):
    rows = ROWS_HEAD if with_head else ROWS
    unpack(recv_ref, rows, images)

    def one_plane(x, carry):
        for rank in range(RANKS):
            for half in range(HALVES):
                start = rank * rows + (x * HALVES + half) * MODES
                block[rank * 16 : (rank + 1) * 16, half * CZ : (half + 1) * CZ] = images[
                    pl.ds(start, 16), :
                ].astype(BF16)
        values = block[...]
        weights = kl_ref[x]
        total = jnp.zeros((ALL, HALVES * CZ), F32)
        for d in range(KL):
            product = jnp.dot(tensor_ref[d], values, preferred_element_type=F32)
            total = total + weights[d : d + 1] * product
        for half in range(HALVES):
            spot = x * HALVES + half
            sums[pl.ds(pl.multiple_of(spot * ALL, 8), ALL), :] = total[:, half * CZ : (half + 1) * CZ]
        for half in range(HALVES):
            spot = x * HALVES + half
            for rank in range(RANKS):
                outs[pl.ds(rank * rows + spot * MODES, 16), :] = sums[pl.ds(spot * ALL + rank * MODES, 16), :]
        return carry

    lax.fori_loop(0, PLANES, one_plane, 0)
    if with_head:
        owner, row, slot = facts[0], facts[1], facts[2]
        start = owner * rows
        known = images[pl.ds(start + HIGH, SPOTS), :] + images[pl.ds(start + LOW, SPOTS), :]
        image = images[pl.ds(start + slot, SPOTS, stride=MODES), :]
        total = sums[pl.ds(row, SPOTS, stride=ALL), :]
        mean = mean_ref[...]
        head = known - OMEGA * (mean * image + total) / (6.0 * mean)
        high = head.astype(BF16).astype(F32)
        for rank in range(RANKS):
            outs[rank * rows + HIGH : rank * rows + LOW, :] = high
            outs[rank * rows + LOW : rank * rows + LOW + SPOTS, :] = head - high
    pack(outs, rows, send_ref)


def pressure_result_kernel(recv_ref, base_ref, mean_ref, out_ref, head_ref, sums, scale):
    rows = ROWS_HEAD
    unpack(recv_ref, rows, sums)
    scale[...] = OMEGA / (6.0 * mean_ref[...])
    for x in range(PLANES):
        head_ref[x] = gather_rows(sums, rows, HIGH + x * HALVES, 1) + gather_rows(sums, rows, LOW + x * HALVES, 1)

    def one_mode(m, carry):
        for x in range(PLANES):
            total = gather_rows(sums, rows, x * HALVES * MODES + m, MODES)
            out_ref[m, x] = base_ref[m, x] - scale[x] * total
        return carry

    lax.fori_loop(0, MODES, one_mode, 0)


def advection_kernel(field_ref, low_ref, high_ref, base_ref, mean_ref, head_ref, head_low, head_high, out_ref, speed):
    masks = edge_masks()
    for x in range(PLANES):
        head = head_ref[x]
        below = head_ref[x - 1] if x > 0 else head_low[0]
        above = head_ref[x + 1] if x < PLANES - 1 else head_high[0]
        y_less, y_more, z_less, z_more = beside(head, masks)
        factor = (0.25 * STEP) * mean_ref[x]
        speed[0, x] = factor * (above - below)
        speed[1, x] = factor * (y_more - y_less)
        speed[2, x] = factor * (z_more - z_less)

    def one_mode(m, carry):
        for x in range(PLANES):
            tile = field_ref[m, x]
            below = field_ref[m, x - 1] if x > 0 else low_ref[MODES + m].astype(F32)
            above = field_ref[m, x + 1] if x < PLANES - 1 else high_ref[MODES + m].astype(F32)
            y_less, y_more, z_less, z_more = beside(tile, masks)
            moved = speed[0, x] * (above - below) + speed[1, x] * (y_more - y_less) + speed[2, x] * (z_more - z_less)
            out_ref[m, x] = base_ref[m, x] + moved
        return carry

    lax.fori_loop(0, MODES, one_mode, 0)


def concentration_result_kernel(recv_ref, base_ref, out_ref, sums):
    rows = ROWS
    unpack(recv_ref, rows, sums)

    def one_mode(m, carry):
        for x in range(PLANES):
            total = gather_rows(sums, rows, x * HALVES * MODES + m, MODES)
            out_ref[m, x] = base_ref[m, x] - DISPERSION * total
        return carry

    lax.fori_loop(0, MODES, one_mode, 0)


def local(pressure, source, concentration, mean_cond, kl_cond, mode_table):
    spaces = lax.axis_size("space")
    up = [(i, i + 1) for i in range(spaces - 1)]
    down = [(i + 1, i) for i in range(spaces - 1)]
    rank = lax.axis_index("mode")

    last = jnp.concatenate([pressure[:, -1], concentration[:, -1]], axis=0).astype(BF16)
    first = jnp.concatenate([pressure[:, 0], concentration[:, 0]], axis=0).astype(BF16)
    low = lax.ppermute(last, "space", up)
    high = lax.ppermute(first, "space", down)

    is_mean = jnp.sum(jnp.abs(mode_table), axis=1) == 0
    row = jnp.argmax(is_mean.astype(jnp.int32)).astype(jnp.int32)
    valid = lax.dynamic_slice_in_dim((mode_table[:, 0] >= 0).astype(jnp.int32), rank * MODES, MODES, 0)
    facts = jnp.concatenate(
        [jnp.stack([row // MODES, row, row % MODES, rank.astype(jnp.int32)]), valid, jnp.zeros((1,), jnp.int32)]
    )

    ordered = jnp.pad(
        mode_table.T.reshape(KL, RANKS, MODES), ((0, 0), (0, 0), (0, 16 - MODES)), constant_values=-1
    ).reshape(KL, RANKS * 16)
    tensor = call(
        coupling_kernel,
        jax.ShapeDtypeStruct((KL, ALL, 256), BF16),
        [vmem(), vmem()],
        [],
        "coupling",
        8 * ALL * 256 * 8,
        KL * ALL * 256 * 2,
    )(mode_table, ordered)

    own_kl = lax.dynamic_index_in_dim(kl_cond.reshape(KL, PLANES, HALVES, RANKS, CZ), rank, 3, keepdims=False)
    own_kl = jnp.swapaxes(own_kl.reshape(KL, PLANES, HALVES * CZ), 0, 1)
    own_mean = lax.dynamic_index_in_dim(mean_cond.reshape(SPOTS, RANKS, CZ), rank, 1, keepdims=False)

    field = jax.ShapeDtypeStruct(pressure.shape, F32)

    def message(rows):
        return jax.ShapeDtypeStruct((RANKS, rows, CZ), BF16)

    def exchange(rows_of):
        return lax.all_to_all(rows_of, "mode", 0, 0, tiled=True)

    size = pressure.size
    send_p, base_p = call(
        pressure_kernel,
        (message(ROWS_HEAD), field),
        [smem()] + [vmem()] * 5,
        [pltpu.VMEM((RANKS * ROWS_HEAD, CZ), F32), pltpu.VMEM((PLANES, CY, CZ), F32)],
        "pressure_images",
        size * 20,
        size * 14,
    )(facts, pressure, source, low, high, mean_cond)
    recv_p = exchange(send_p)
    send_c, base_c = call(
        concentration_kernel,
        (message(ROWS), field),
        [smem()] + [vmem()] * 4,
        [pltpu.VMEM((RANKS * ROWS, CZ), F32)],
        "concentration_images",
        size * 20,
        size * 10,
    )(facts, concentration, low, high, mean_cond)
    recv_c = exchange(send_c)

    def contract(with_head, received):
        rows = ROWS_HEAD if with_head else ROWS
        return call(
            functools.partial(contract_kernel, with_head),
            message(rows),
            [smem()] + [vmem()] * 4,
            [
                pltpu.VMEM((RANKS * rows + 16, CZ), F32),
                pltpu.VMEM((256, HALVES * CZ), BF16),
                pltpu.VMEM((SPOTS * ALL + 16, CZ), F32),
                pltpu.VMEM((RANKS * rows + 16, CZ), F32),
            ],
            "contract_pressure" if with_head else "contract_concentration",
            2 * KL * ALL * 256 * SPOTS * CZ,
            RANKS * rows * CZ * 4,
        )(facts, received, tensor, own_kl, own_mean)

    back_p = exchange(contract(True, recv_p))
    back_c = exchange(contract(False, recv_c))

    pressure_next, head = call(
        pressure_result_kernel,
        (field, jax.ShapeDtypeStruct(mean_cond.shape, F32)),
        [vmem()] * 3,
        [pltpu.VMEM((RANKS * ROWS_HEAD, CZ), F32), pltpu.VMEM((PLANES, CY, CZ), F32)],
        "pressure_result",
        size * 4,
        size * 10,
    )(back_p, base_p, mean_cond)
    head_low = lax.ppermute(head[-1:], "space", up)
    head_high = lax.ppermute(head[:1], "space", down)
    moved = call(
        advection_kernel,
        field,
        [vmem()] * 8,
        [pltpu.VMEM((3, PLANES, CY, CZ), F32)],
        "advection",
        size * 20,
        size * 12,
    )(concentration, low, high, base_c, mean_cond, head, head_low, head_high)
    concentration_next = call(
        concentration_result_kernel,
        field,
        [vmem()] * 2,
        [pltpu.VMEM((RANKS * ROWS, CZ), F32)],
        "concentration_result",
        size * 4,
        size * 10,
    )(back_c, moved)
    return (pressure_next, concentration_next)


def solution(mesh):
    return jax.shard_map(
        local,
        mesh=mesh,
        in_specs=(
            P("mode", "space", None, None),
            P("mode", "space", None, None),
            P("mode", "space", None, None),
            P("space", None, None),
            P(None, "space", None, None),
            P(),
        ),
        out_specs=(P("mode", "space", None, None), P("mode", "space", None, None)),
        check_vma=False,
    )
```

time: 485 us -> 134 us (0.28)
  waiting for transfers between devices: 343 us -> 28.1 us
  matrix products: 42.1 us -> 0 us
  other arithmetic: 39.9 us -> 1.48 us
  Pallas kernels: 0 us -> 34.1 us
  starting transfers between devices: 17.3 us -> 37.3 us
  between operations: 16.1 us -> 2.92 us
    all_gather x2 -> x0, waiting for transfers between devices: 199 us -> none  [the longest x1 102 us: local(): lax.all_gather(lap_conc, 'mode', axis=0, tiled=True)]
    psum x1 -> x0, waiting for transfers between devices: 132 us -> none  [spread(): return lax.psum(block, axis)]
    dot_general x2 -> x0, matrix products: 42.1 us -> none  [the longest x1 21.1 us: local(): jnp.einsum('jxyz,jtk->tkxyz', whole_conc, columns, preferred_element_type...]
    pallas_call x0 -> x8, Pallas kernels: none -> 34.1 us  [the longest x2 12 us: contract(): call(functools.partial(contract_kernel, with_head), message(rows), [smem(...]
    all_to_all x0 -> x4, waiting for transfers between devices: none -> 26.7 us  [exchange(): return lax.all_to_all(rows_of, 'mode', 0, 0, tiled=True)]
    all_to_all x0 -> x4, starting transfers between devices: none -> 19.7 us  [exchange(): return lax.all_to_all(rows_of, 'mode', 0, 0, tiled=True)]
    sub x1 -> x0, other arithmetic: 15.7 us -> none  [local(): concentration - DISPERSION * galerkin_conc - STEP * advection]
    add x1 -> x0, other arithmetic: 13.1 us -> none  [local(): pressure + OMEGA * (source - galerkin_press) / (6.0 * mean_cond[None])]
  transfers between devices with their start and end apart: 7 -> 8, of which waited for: 5 -> 4; matrix products, arithmetic and copies ran while one was open for 8% -> 5% of each run, Pallas kernels for 0% -> 19%
where the time goes in v1:
time: 134 us; the launch traced here: 131 us
  starting transfers between devices  37.3 us (28%)
  Pallas kernels  34.1 us (25%)
  waiting for transfers between devices  28.1 us (21%)
  local copies, waits for them, and re-layouts  27.5 us (21%)
  between operations  2.92 us (2%)
  other arithmetic  1.48 us (1%)
    all_to_all x4, waiting for transfers between devices, exchange(): return lax.all_to_all(rows_of, 'mode', 0, 0, tiled=True)  26.7 us
    unnamed x55, local copies, waits for them, and re-layouts  20.5 us
    all_to_all x4, starting transfers between devices, exchange(): return lax.all_to_all(rows_of, 'mode', 0, 0, tiled=True)  19.7 us
    pallas_call x2, Pallas kernels, contract(): call(functools.partial(contract_kernel, with_head), message(rows), [smem(...  12 us
    ppermute x1, starting transfers between devices, local(): head_high = lax.ppermute(head[:1], 'space', down)  6.03 us
    ppermute x1, starting transfers between devices, local(): high = lax.ppermute(first, 'space', down)  5.83 us
    pallas_call x1, Pallas kernels, local(): call(pressure_kernel, (message(ROWS_HEAD), field), [smem()] + [vmem()] *...  5.25 us
    pallas_call x1, Pallas kernels, local(): call(pressure_result_kernel, (field, jax.ShapeDtypeStruct(mean_cond.shape...  4.36 us
  transfers between devices with their start and end apart: 8, of which 4 were waited for; matrix products, arithmetic and copies ran while one was open for 5% of the time, Pallas kernels for 19%

profile of v1, /device:TPU:2, one launch (start us, length us, event | category | flops | bytes accessed | tf_op | source)
XLA Modules:
  0.0 131.4 jit_solution(7585982401326726139)
XLA Ops:
  0.6 0.0 copy-start
  0.6 1.4 %slice_bitcast_fusion = (bf16[11,32,128]{2,1,0:T(8,128)(2,1)S(1)}, bf16[11,32,128]{2,1,0:T(8,128)(2,1)S(1)}, bf16[11,32,128]{2,1,0:T(8,128)(2,1)S(1)}, bf16[11,32,128]{2,1,0:T(8,128)(2,1)S(1)}) fusion(f32[11,11,32,128]{3,2,1,0:T(8,128)} %field_ref.3, f32[11,11,32,128]{3,2,1,0:T(8,128)} %field_ref.5), kind=kLoop, calls=%fused_computation.4 | loop fusion | bytes 720896 | tf_op jit(solution)/shard_map/squeeze | solution.py:286
  2.0 3.8 %collective-permute-start = (bf16[22,32,128]{2,1,0:T(8,128)(2,1)S(1)}, bf16[22,32,128]{2,1,0:T(8,128)(2,1)S(1)}, u32[]{:S(2)}, u32[]{:S(2)}) collective-permute-start(bf16[22,32,128]{2,1,0:T(8,128)(2,1)S(1)} %pad_maximum_fusion), channel_id=1, source_target_pairs={{0,16},{16,32},{32,48},{48,64},{64,80},{80,96},{96,112},{112,128},... | collective-permute-start | bytes 540680 | tf_op jit(solution)/shard_map/ppermute | solution.py:287
  5.9 5.8 %collective-permute-start.1 = (bf16[22,32,128]{2,1,0:T(8,128)(2,1)S(1)}, bf16[22,32,128]{2,1,0:T(8,128)(2,1)S(1)}, u32[]{:S(2)}, u32[]{:S(2)}) collective-permute-start(bf16[22,32,128]{2,1,0:T(8,128)(2,1)S(1)} %pad_maximum_fusion.1), channel_id=1, source_target_pairs={{16,0},{32,16},{48,32},{64,48},{80,64},{96,80},{112,96},{128,112},... | collective-permute-start | bytes 540680 | tf_op jit(solution)/shard_map/ppermute | solution.py:288
  11.7 0.7 abs_reduce_fusion
  12.4 0.7 fusion
  15.1 0.7 slice.25
  15.8 0.1 fusion.1
  15.8 0.7 concatenate.11.facts
  16.6 0.0 collective-permute-done.low_ref
  16.6 0.0 collective-permute-done.1.high_ref
  16.6 0.0 copy-start.4
  16.6 0.9 copy-done.4
  17.5 1.5 %copy-done.7 = f32[11,11,32,128]{3,2,1,0:T(8,128)S(1)} copy-done((f32[11,11,32,128]{3,2,1,0:T(8,128)S(1)}, f32[11,11,32,128]{3,2,1,0:T(8,128)}, u32[]{:S(2)}) %copy-start.7) | copy-done | bytes 1982488
  19.1 5.3 %pressure_images.1 = (bf16[16,288,128]{2,1,0:T(8,128)(2,1)S(1)}, f32[11,11,32,128]{3,2,1,0:T(8,128)S(1)}) custom-call(s32[16]{0:T(128)S(1)} %concatenate.11.facts, f32[11,11,32,128]{3,2,1,0:T(8,128)S(1)} %copy-done.7, f32[11,11,32,128]{3,2,1,0:T(8,128)} %source_ref.1, bf16[22,32,128]{2,1,0:T(8,128)(2,1)S(1)} %collective-permute-done.low_ref, ...), custom_call_target="tpu_custom_call" | custom-call | flops 9912320 | bytes 6938624 | tf_op jit(solution)/shard_map/pressure_images/pallas_call | solution.py:323
  24.3 0.0 copy-start.9
  24.3 1.3 copy-done.9
  25.6 0.7 copy-done.11
  26.3 0.7 copy-done.14
  26.9 1.0 copy-done.18
  27.9 6.6 %all-to-all-start = ((bf16[16,288,128]{2,1,0:T(8,128)(2,1)}), bf16[16,288,128]{2,1,0:T(8,128)(2,1)}, u32[]{:S(2)}, u32[]{:S(2)}) async-start(bf16[16,288,128]{2,1,0:T(8,128)(2,1)} %copy-done.18), calls=%async_computation | async-start | bytes 2359296 | tf_op jit(solution)/shard_map/all_to_all | solution.py:320
  34.6 0.0 copy-start.5
  34.6 0.9 copy-done.5
  35.5 0.9 copy-done.12
  36.4 0.9 copy-done.15
  37.3 3.9 %concentration_images.1 = (bf16[16,256,128]{2,1,0:T(8,128)(2,1)S(1)}, f32[11,11,32,128]{3,2,1,0:T(8,128)S(1)}) custom-call(s32[16]{0:T(128)S(1)} %concatenate.11.facts, f32[11,11,32,128]{3,2,1,0:T(8,128)S(1)} %copy-done.1, bf16[22,32,128]{2,1,0:T(8,128)(2,1)S(1)} %copy-done.12, bf16[22,32,128]{2,1,0:T(8,128)(2,1)S(1)} %copy-done.15, f32[11,32,128]{2,1,0:T(8,128)S(1)} %copy-done.5), custom_call_target="tpu_custom_call" | custom-call | flops 9912320 | bytes 4956160 | tf_op jit(solution)/shard_map/concentration_images/pallas_call | solution.py:333
  41.2 1.3 copy-done.8
  42.5 1.0 copy-done.20
  43.5 10.6 %all-to-all-done.recv_ref = bf16[16,288,128]{2,1,0:T(8,128)(2,1)} async-done(((bf16[16,288,128]{2,1,0:T(8,128)(2,1)}), bf16[16,288,128]{2,1,0:T(8,128)(2,1)}, u32[]{:S(2)}, u32[]{:S(2)}) %all-to-all-start) | async-done | bytes 1179680 | tf_op jit(solution)/shard_map/all_to_all | solution.py:320
  54.1 4.3 %all-to-all-start.2 = ((bf16[16,256,128]{2,1,0:T(8,128)(2,1)}), bf16[16,256,128]{2,1,0:T(8,128)(2,1)}, u32[]{:S(2)}, u32[]{:S(2)}) async-start(bf16[16,256,128]{2,1,0:T(8,128)(2,1)} %copy-done.20), calls=%async_computation.2 | async-start | bytes 2097152 | tf_op jit(solution)/shard_map/all_to_all | solution.py:320
  58.5 0.1 copy.15.column_ref
  58.6 0.7 reshape.24
  59.3 1.5 %pad.4 = s32[8,16,16]{2,1,0:T(8,128)} pad(s32[8,16,11]{2,1,0:T(8,128)} %reshape.24, s32[]{:T(128)} %constant.39.clone.1), padding=0_0x0_0x0_5 | pad | bytes 13828 | tf_op jit(solution)/shard_map/jit(_pad)/pad | solution.py:297
  60.8 0.9 reshape.25.row_ref
  61.7 0.0 copy-done
  61.7 0.1 constant_dynamic-slice_fusion.1
  61.8 0.9 constant_dynamic-slice_fusion
  62.8 1.0 coupling.1.tensor_ref
  63.9 6.1 %contract_pressure.1 = bf16[16,288,128]{2,1,0:T(8,128)(2,1)S(1)} custom-call(s32[16]{0:T(128)S(1)} %concatenate.11.facts, bf16[16,288,128]{2,1,0:T(8,128)(2,1)} %all-to-all-done.recv_ref, bf16[8,176,256]{2,1,0:T(8,128)(2,1)S(1)} %coupling.1.tensor_ref, f32[11,8,256]{2,1,0:T(8,128)S(1)} %bitcast.27, f32[22,128]{1,0:T(8,128)S(1)} %bitcast.29), custom_call_target="tpu_custom_call" | custom-call | flops 2030043136 | bytes 2359296 | tf_op jit(solution)/shard_map/contract_pressure/pallas_call | solution.py:346
  69.9 0.0 copy-start.17
  69.9 1.0 copy-done.17
  70.9 0.9 copy-done.21
  71.8 4.7 %all-to-all-done.2.recv_ref = bf16[16,256,128]{2,1,0:T(8,128)(2,1)} async-done(((bf16[16,256,128]{2,1,0:T(8,128)(2,1)}), bf16[16,256,128]{2,1,0:T(8,128)(2,1)}, u32[]{:S(2)}, u32[]{:S(2)}) %all-to-all-start.2) | async-done | bytes 1048608 | tf_op jit(solution)/shard_map/all_to_all | solution.py:320
  76.5 4.4 %all-to-all-start.1 = ((bf16[16,288,128]{2,1,0:T(8,128)(2,1)}), bf16[16,288,128]{2,1,0:T(8,128)(2,1)}, u32[]{:S(2)}, u32[]{:S(2)}) async-start(bf16[16,288,128]{2,1,0:T(8,128)(2,1)} %copy-done.17), calls=%async_computation.1 | async-start | bytes 2359296 | tf_op jit(solution)/shard_map/all_to_all | solution.py:320
  80.9 0.0 copy-done.24
  80.9 1.1 copy-done.22
  82.0 5.9 %contract_concentration.1 = bf16[16,256,128]{2,1,0:T(8,128)(2,1)S(1)} custom-call(s32[16]{0:T(128)S(1)} %concatenate.11.facts, bf16[16,256,128]{2,1,0:T(8,128)(2,1)} %all-to-all-done.2.recv_ref, bf16[8,176,256]{2,1,0:T(8,128)(2,1)S(1)} %copy-done.22, f32[11,8,256]{2,1,0:T(8,128)S(1)} %bitcast.28, f32[22,128]{1,0:T(8,128)S(1)} %bitcast.30), custom_call_target="tpu_custom_call" | custom-call | flops 2030043136 | bytes 2097152 | tf_op jit(solution)/shard_map/contract_concentration/pallas_call | solution.py:346
  88.0 1.0 copy-done.19
  89.0 11.4 %all-to-all-done.1.recv_ref = bf16[16,288,128]{2,1,0:T(8,128)(2,1)} async-done(((bf16[16,288,128]{2,1,0:T(8,128)(2,1)}), bf16[16,288,128]{2,1,0:T(8,128)(2,1)}, u32[]{:S(2)}, u32[]{:S(2)}) %all-to-all-start.1) | async-done | bytes 1179680 | tf_op jit(solution)/shard_map/all_to_all | solution.py:320
  100.4 4.3 %all-to-all-start.3 = ((bf16[16,256,128]{2,1,0:T(8,128)(2,1)}), bf16[16,256,128]{2,1,0:T(8,128)(2,1)}, u32[]{:S(2)}, u32[]{:S(2)}) async-start(bf16[16,256,128]{2,1,0:T(8,128)(2,1)} %copy-done.19), calls=%async_computation.3 | async-start | bytes 2097152 | tf_op jit(solution)/shard_map/all_to_all | solution.py:320
  104.8 0.0 copy-start.6
  104.8 0.9 copy-done.6
  105.7 1.5 %copy-done.10 = f32[11,11,32,128]{3,2,1,0:T(8,128)S(1)} copy-done((f32[11,11,32,128]{3,2,1,0:T(8,128)S(1)}, f32[11,11,32,128]{3,2,1,0:T(8,128)}, u32[]{:S(2)}) %copy-start.10) | copy-done | bytes 1982488
  107.2 4.4 %pressure_result.1 = (f32[11,11,32,128]{3,2,1,0:T(8,128)}, f32[11,32,128]{2,1,0:T(8,128)S(1)}) custom-call(bf16[16,288,128]{2,1,0:T(8,128)(2,1)} %all-to-all-done.1.recv_ref, f32[11,11,32,128]{3,2,1,0:T(8,128)S(1)} %copy-done.10, f32[11,32,128]{2,1,0:T(8,128)S(1)} %copy-done.6), custom_call_target="tpu_custom_call" | custom-call | flops 1982464 | bytes 4956160 | tf_op jit(solution)/shard_map/pressure_result/pallas_call | solution.py:364
  111.6 1.9 %collective-permute-start.2 = (f32[1,32,128]{2,1,0:T(8,128)S(1)}, f32[1,32,128]{2,1,0:T(8,128)S(1)}, u32[]{:S(2)}, u32[]{:S(2)}) collective-permute-start(f32[1,32,128]{2,1,0:T(8,128)S(1)} %get-tuple-element.21), channel_id=1, source_target_pairs={{0,16},{16,32},{32,48},{48,64},{64,80},{80,96},{96,112},{112,128},... | collective-permute-start | bytes 49160 | tf_op jit(solution)/shard_map/ppermute | solution.py:373
  113.5 6.0 %collective-permute-start.3 = (f32[1,32,128]{2,1,0:T(8,128)S(1)}, f32[1,32,128]{2,1,0:T(8,128)S(1)}, u32[]{:S(2)}, u32[]{:S(2)}) collective-permute-start(f32[1,32,128]{2,1,0:T(8,128)S(1)} %get-tuple-element.20), channel_id=1, source_target_pairs={{16,0},{32,16},{48,32},{64,48},{80,64},{96,80},{112,96},{128,112},... | collective-permute-start | bytes 49160 | tf_op jit(solution)/shard_map/ppermute | solution.py:374
  119.6 0.0 collective-permute-done.2.head_low
  119.6 1.4 %collective-permute-done.3.head_high = f32[1,32,128]{2,1,0:T(8,128)S(1)} collective-permute-done((f32[1,32,128]{2,1,0:T(8,128)S(1)}, f32[1,32,128]{2,1,0:T(8,128)S(1)}, u32[]{:S(2)}, u32[]{:S(2)}) %collective-permute-start.3) | collective-permute-done | bytes 16416 | tf_op jit(solution)/shard_map/ppermute | solution.py:374
  121.0 3.5 %advection.1.base_ref = f32[11,11,32,128]{3,2,1,0:T(8,128)S(1)} custom-call(f32[11,11,32,128]{3,2,1,0:T(8,128)S(1)} %copy-done.1, bf16[22,32,128]{2,1,0:T(8,128)(2,1)S(1)} %copy-done.13, bf16[22,32,128]{2,1,0:T(8,128)(2,1)S(1)} %copy-done.16, f32[11,11,32,128]{3,2,1,0:T(8,128)} %copy-done.8, f32[11,32,128]{2,1,0:T(8,128)S(1)} %copy-done.6, ...), custom_call_target="tpu_custom_call" | custom-call | flops 9912320 | bytes 5947392 | tf_op jit(solution)/shard_map/advection/pallas_call | solution.py:375
  124.5 0.0 copy-start.2
  124.5 1.3 copy-done.2
  125.8 0.0 all-to-all-done.3.recv_ref
  125.8 1.6 %copy-done.3 = f32[11,11,32,128]{3,2,1,0:T(8,128)S(1)} copy-done((f32[11,11,32,128]{3,2,1,0:T(8,128)S(1)}, f32[11,11,32,128]{3,2,1,0:T(8,128)}, u32[]{:S(2)}) %copy-start.3) | copy-done | bytes 1982488
  127.3 4.0 %concentration_result.1 = f32[11,11,32,128]{3,2,1,0:T(8,128)} custom-call(bf16[16,256,128]{2,1,0:T(8,128)(2,1)} %all-to-all-done.3.recv_ref, f32[11,11,32,128]{3,2,1,0:T(8,128)S(1)} %copy-done.3), custom_call_target="tpu_custom_call" | custom-call | flops 1982464 | bytes 4956160 | tf_op jit(solution)/shard_map/concentration_result/pallas_call | solution.py:384
  (29 shorter events, 0.1 us)
Async XLA Ops:
  0.6 61.1 %copy-start = (f32[8,11,32,128]{3,2,1,0:T(8,128)S(1)}, f32[8,11,32,128]{3,2,1,0:T(8,128)}, u32[]{:S(2)}) copy-start(f32[8,11,32,128]{3,2,1,0:T(8,128)} %param.10) | copy-start | bytes 4325380
  2.0 14.5 %collective-permute-start = (bf16[22,32,128]{2,1,0:T(8,128)(2,1)S(1)}, bf16[22,32,128]{2,1,0:T(8,128)(2,1)S(1)}, u32[]{:S(2)}, u32[]{:S(2)}) collective-permute-start(bf16[22,32,128]{2,1,0:T(8,128)(2,1)S(1)} %pad_maximum_fusion), channel_id=1, source_target_pairs={{0,16},{16,32},{32,48},{48,64},{64,80},{80,96},{96,112},{112,128},... | collective-permute-start | bytes 540680 | tf_op jit(solution)/shard_map/ppermute | solution.py:287
  5.9 10.7 %collective-permute-start.1 = (bf16[22,32,128]{2,1,0:T(8,128)(2,1)S(1)}, bf16[22,32,128]{2,1,0:T(8,128)(2,1)S(1)}, u32[]{:S(2)}, u32[]{:S(2)}) collective-permute-start(bf16[22,32,128]{2,1,0:T(8,128)(2,1)S(1)} %pad_maximum_fusion.1), channel_id=1, source_target_pairs={{16,0},{32,16},{48,32},{64,48},{80,64},{96,80},{112,96},{128,112},... | collective-permute-start | bytes 540680 | tf_op jit(solution)/shard_map/ppermute | solution.py:288
  16.6 0.9 copy-start.4
  17.5 1.6 %copy-start.7 = (f32[11,11,32,128]{3,2,1,0:T(8,128)S(1)}, f32[11,11,32,128]{3,2,1,0:T(8,128)}, u32[]{:S(2)}) copy-start(f32[11,11,32,128]{3,2,1,0:T(8,128)} %field_ref.3) | copy-start | bytes 5947396
  24.3 1.3 copy-start.9
  25.6 0.7 copy-start.11
  26.3 0.7 copy-start.14
  26.9 1.0 copy-start.18
  27.9 6.6 %copy-start.1 = (f32[11,11,32,128]{3,2,1,0:T(8,128)S(1)}, f32[11,11,32,128]{3,2,1,0:T(8,128)}, u32[]{:S(2)}) copy-start(f32[11,11,32,128]{3,2,1,0:T(8,128)} %field_ref.5) | copy-start | bytes 5947396
  27.9 26.1 %all-to-all-start = ((bf16[16,288,128]{2,1,0:T(8,128)(2,1)}), bf16[16,288,128]{2,1,0:T(8,128)(2,1)}, u32[]{:S(2)}, u32[]{:S(2)}) async-start(bf16[16,288,128]{2,1,0:T(8,128)(2,1)} %copy-done.18), calls=%async_computation | async-start | bytes 2359296 | tf_op jit(solution)/shard_map/all_to_all | solution.py:320
  34.6 0.9 copy-start.5
  35.5 0.9 copy-start.12
  36.4 0.9 copy-start.15
  37.3 21.1 %copy-start.25 = (s32[176,8]{0,1:T(8,128)S(1)}, s32[176,8]{0,1:T(8,128)}, u32[]{:S(2)}) copy-start(s32[176,8]{0,1:T(8,128)} %param.11) | copy-start | bytes 16900
  41.2 1.3 copy-start.8
  42.5 1.0 copy-start.20
  54.1 22.4 %all-to-all-start.2 = ((bf16[16,256,128]{2,1,0:T(8,128)(2,1)}), bf16[16,256,128]{2,1,0:T(8,128)(2,1)}, u32[]{:S(2)}, u32[]{:S(2)}) async-start(bf16[16,256,128]{2,1,0:T(8,128)(2,1)} %copy-done.20), calls=%async_computation.2 | async-start | bytes 2097152 | tf_op jit(solution)/shard_map/all_to_all | solution.py:320
  61.8 2.0 %copy-start.23 = (f32[8,11,2,1,128]{4,0,2,1,3:T(8,128)}, f32[8,11,2,1,128]{4,0,2,1,3:T(8,128)S(1)}, u32[]{:S(2)}) copy-start(f32[8,11,2,1,128]{4,0,2,1,3:T(8,128)S(1)} %copy.30) | copy-start | bytes 270340
  69.9 1.0 copy-start.17
  70.9 0.9 copy-start.21
  71.8 9.1 %copy-start.24 = (f32[8,11,2,1,128]{4,0,2,1,3:T(8,128)S(1)}, f32[8,11,2,1,128]{4,0,2,1,3:T(8,128)}, u32[]{:S(2)}) copy-start(f32[8,11,2,1,128]{4,0,2,1,3:T(8,128)} %copy-done.23) | copy-start | bytes 270340
  76.5 23.9 %all-to-all-start.1 = ((bf16[16,288,128]{2,1,0:T(8,128)(2,1)}), bf16[16,288,128]{2,1,0:T(8,128)(2,1)}, u32[]{:S(2)}, u32[]{:S(2)}) async-start(bf16[16,288,128]{2,1,0:T(8,128)(2,1)} %copy-done.17), calls=%async_computation.1 | async-start | bytes 2359296 | tf_op jit(solution)/shard_map/all_to_all | solution.py:320
  80.9 1.1 copy-start.22
  88.0 1.0 copy-start.19
  100.4 25.4 %all-to-all-start.3 = ((bf16[16,256,128]{2,1,0:T(8,128)(2,1)}), bf16[16,256,128]{2,1,0:T(8,128)(2,1)}, u32[]{:S(2)}, u32[]{:S(2)}) async-start(bf16[16,256,128]{2,1,0:T(8,128)(2,1)} %copy-done.19), calls=%async_computation.3 | async-start | bytes 2097152 | tf_op jit(solution)/shard_map/all_to_all | solution.py:320
  104.8 0.9 copy-start.6
  105.7 1.6 %copy-start.10 = (f32[11,11,32,128]{3,2,1,0:T(8,128)S(1)}, f32[11,11,32,128]{3,2,1,0:T(8,128)}, u32[]{:S(2)}) copy-start(f32[11,11,32,128]{3,2,1,0:T(8,128)} %copy-done.9) | copy-start | bytes 5947396
  107.2 13.8 %copy-start.13 = (bf16[22,32,128]{2,1,0:T(8,128)(2,1)S(1)}, bf16[22,32,128]{2,1,0:T(8,128)(2,1)}, u32[]{:S(2)}) copy-start(bf16[22,32,128]{2,1,0:T(8,128)(2,1)} %copy-done.11) | copy-start | bytes 540676
  107.2 13.8 %copy-start.16 = (bf16[22,32,128]{2,1,0:T(8,128)(2,1)S(1)}, bf16[22,32,128]{2,1,0:T(8,128)(2,1)}, u32[]{:S(2)}) copy-start(bf16[22,32,128]{2,1,0:T(8,128)(2,1)} %copy-done.14) | copy-start | bytes 540676
  111.6 8.0 %collective-permute-start.2 = (f32[1,32,128]{2,1,0:T(8,128)S(1)}, f32[1,32,128]{2,1,0:T(8,128)S(1)}, u32[]{:S(2)}, u32[]{:S(2)}) collective-permute-start(f32[1,32,128]{2,1,0:T(8,128)S(1)} %get-tuple-element.21), channel_id=1, source_target_pairs={{0,16},{16,32},{32,48},{48,64},{64,80},{80,96},{96,112},{112,128},... | collective-permute-start | bytes 49160 | tf_op jit(solution)/shard_map/ppermute | solution.py:373
  113.5 7.5 %collective-permute-start.3 = (f32[1,32,128]{2,1,0:T(8,128)S(1)}, f32[1,32,128]{2,1,0:T(8,128)S(1)}, u32[]{:S(2)}, u32[]{:S(2)}) collective-permute-start(f32[1,32,128]{2,1,0:T(8,128)S(1)} %get-tuple-element.20), channel_id=1, source_target_pairs={{16,0},{32,16},{48,32},{64,48},{80,64},{96,80},{112,96},{128,112},... | collective-permute-start | bytes 49160 | tf_op jit(solution)/shard_map/ppermute | solution.py:374
  124.5 1.3 copy-start.2
  125.8 1.6 %copy-start.3 = (f32[11,11,32,128]{3,2,1,0:T(8,128)S(1)}, f32[11,11,32,128]{3,2,1,0:T(8,128)}, u32[]{:S(2)}) copy-start(f32[11,11,32,128]{3,2,1,0:T(8,128)} %copy-done.2) | copy-start | bytes 5947396

commit v2 on v0

v2 whole, which is shorter than its diff:
```python
import functools
import itertools

import jax
import jax.numpy as jnp
import numpy as np
from jax import lax
from jax.experimental import pallas as pl
from jax.experimental.pallas import tpu as pltpu
from jax.sharding import PartitionSpec as P

OMEGA = 0.8
DISPERSION = 0.01
STEP = 0.05
ORDER = 3

F32 = jnp.float32
BF16 = jnp.bfloat16

RANKS = 16
MODES = 11
PLANES = 11
CY = 32
CZ = 128
KL = 8
ALL = RANKS * MODES
SLAB = PLANES * CY
SHARE = SLAB // RANKS
FULL = 24
BODY = SHARE * MODES
PAD = 8
SPACED = SLAB + PAD

SENT_HIGH = 2 * BODY
SENT_LOW = SENT_HIGH + SHARE
SENT = SENT_LOW + SHARE
HIGH = BODY
LOW = BODY + SHARE
ROWS_HEAD = 288
ROWS = 256
STRIDE = SENT + PAD

EDGE_RANKS = (0, 1, RANKS - 2, RANKS - 1)
LIMIT = 60 * 1024 * 1024

INDICES = sorted(
    (t for t in itertools.product(range(ORDER + 1), repeat=KL) if sum(t) <= ORDER), key=lambda t: (sum(t), t)
)
PLACE = {t: i for i, t in enumerate(INDICES)}
NEIGHBOURS = [
    [
        (d, max(t[d], t[d] + step), PLACE[t[:d] + (t[d] + step,) + t[d + 1 :]])
        for d in range(KL)
        for step in (-1, 1)
        if t[:d] + (t[d] + step,) + t[d + 1 :] in PLACE
    ]
    for t in INDICES
]
VALID = len(INDICES)
POWERS = (ORDER + 1) ** np.arange(KL)
CODES = (np.array(INDICES) * POWERS).sum(axis=1).astype(np.int32)
OWNER = VALID


def vmem():
    return pl.BlockSpec(memory_space=pltpu.VMEM)


def smem():
    return pl.BlockSpec(memory_space=pltpu.SMEM)


def hbm():
    return pl.BlockSpec(memory_space=pltpu.HBM)


def call(kernel, outs, ins, scratch, name, flops, moved, aliases=None):
    return pl.pallas_call(
        kernel,
        out_shape=outs,
        in_specs=ins,
        out_specs=jax.tree.map(lambda _: hbm(), outs),
        scratch_shapes=scratch,
        input_output_aliases=aliases or {},
        compiler_params=pltpu.CompilerParams(vmem_limit_bytes=LIMIT),
        cost_estimate=pl.CostEstimate(flops=flops, bytes_accessed=moved, transcendentals=0),
        name=name,
    )


def start_all(sems, pairs):
    copies = [pltpu.make_async_copy(source, target, sems.at[i]) for i, (source, target) in enumerate(pairs)]
    for copy in copies:
        copy.start()
    return copies


def loop(first, last, work):
    def one(i, carry):
        work(i)
        return carry

    lax.fori_loop(first, last, one, 0)


def edge_masks():
    row = lax.broadcasted_iota(jnp.int32, (CY, CZ), 0)
    lane = lax.broadcasted_iota(jnp.int32, (CY, CZ), 1)
    return row == 0, row == CY - 1, lane == 0, lane == CZ - 1


def rows_of(ref, start):
    return ref[pl.ds(start, CY), :]


def beside(ref, start, tile, masks):
    first_row, last_row, first_lane, last_lane = masks
    y_less = jnp.where(first_row, 0.0, rows_of(ref, start - 1))
    y_more = jnp.where(last_row, 0.0, rows_of(ref, start + 1))
    z_less = jnp.where(first_lane, 0.0, pltpu.roll(tile, 1, 1))
    z_more = jnp.where(last_lane, 0.0, pltpu.roll(tile, CZ - 1, 1))
    return y_less, y_more, z_less, z_more


def laplace(ref, base, x, masks, outer=None):
    start = base + x * CY
    tile = rows_of(ref, start)
    y_less, y_more, z_less, z_more = beside(ref, start, tile, masks)
    total = (y_more + y_less) + (z_more + z_less)
    if x > 0:
        total = total + rows_of(ref, start - CY)
    if x < PLANES - 1:
        total = total + rows_of(ref, start + CY)
    if outer is not None:
        total = total + outer
    return tile, 6.0 * tile - total


def rounded(tile):
    return tile.astype(BF16).astype(F32)


def copy_share(target, to, source, start):
    for part in range(0, FULL, 8):
        target[pl.ds(to + part, 8), :] = source[pl.ds(start + part, 8), :]


def pack_rank(scratch, start, out_ref, slot, blocks):
    for block in range(blocks):
        out_ref[slot, pl.ds(block * 16, 16), :] = scratch[pl.ds(start + block * 16, 16), :].astype(BF16)


def unpack_rank(in_ref, rank, scratch, stride, blocks):
    for block in blocks:
        start = pl.multiple_of(rank * stride + block * 16, 8)
        scratch[pl.ds(start, 16), :] = in_ref[rank, pl.ds(block * 16, 16), :].astype(F32)


def inner_kernel(
    table_ref, mean_hbm, pressure_hbm, source_hbm, concentration_hbm, send_hbm, part_hbm,
    fields, source, mean, image, high, low, scratch, strip, sems, extra_sems, send_sems, part_sems,
):
    inputs = (pressure_hbm, concentration_hbm)

    def base_of(index, m):
        return pl.multiple_of(PAD + (index * MODES + m) * SPACED, 8)

    def fetch(index, m):
        target = fields.at[pl.ds(base_of(index, m), SLAB), :]
        return pltpu.make_async_copy(inputs[index].at[m], target, sems.at[index, m])

    for index in range(2):
        for m in range(MODES):
            fetch(index, m).start()
    total = jnp.sum(jnp.abs(table_ref[...]).astype(F32), axis=0, keepdims=True)
    place = lax.broadcasted_iota(jnp.int32, (1, ALL), 1).astype(F32)
    row = jnp.min(jnp.where(total == 0.0, place, float(ALL))).astype(jnp.int32)
    slot = lax.rem(row, MODES)
    extra = start_all(extra_sems, [(source_hbm.at[slot], source), (mean_hbm, mean)])
    masks = edge_masks()

    for index in range(2):

        def one_mode(m):
            fetch(index, m).wait()
            for x in range(PLANES):
                image[pl.ds(x * CY, CY), :] = laplace(fields, base_of(index, m), x, masks)[1]
            for rank in range(RANKS):
                copy_share(scratch, rank * STRIDE + (index * MODES + m) * SHARE, image, rank * SHARE)

        loop(0, MODES, one_mode)
    for copy in extra:
        copy.wait()
    for x in range(PLANES):
        rows = pl.ds(x * CY, CY)
        head = rows_of(fields, base_of(0, slot) + x * CY) + (OMEGA / (6.0 * mean[rows, :])) * source[rows, :]
        top = rounded(head)
        high[rows, :] = top
        low[rows, :] = head - top
    for rank in range(RANKS):
        copy_share(scratch, rank * STRIDE + SENT_HIGH, high, rank * SHARE)
        copy_share(scratch, rank * STRIDE + SENT_LOW, low, rank * SHARE)
    parts = start_all(
        part_sems,
        [(scratch.at[pl.ds(rank * STRIDE, SENT), :], part_hbm.at[i]) for i, rank in enumerate(EDGE_RANKS)],
    )

    def send(rank):
        return pltpu.make_async_copy(strip.at[rank], send_hbm.at[rank], send_sems.at[rank])

    def go(rank):
        pack_rank(scratch, pl.multiple_of(rank * STRIDE, 8), strip, rank, SENT // 16)
        send(rank).start()

    loop(2, RANKS - 2, go)
    for copy in parts:
        copy.wait()
    loop(2, RANKS - 2, lambda rank: send(rank).wait())


def outer_kernel(part_hbm, low_hbm, high_hbm, send_in, send_hbm, part, low, high, halo, strip, sems, send_sems):
    parts = [(part_hbm.at[i], part.at[pl.ds(i * STRIDE, SENT), :]) for i in range(4)]
    for copy in start_all(sems, parts + [(low_hbm, low), (high_hbm, high)]):
        copy.wait()

    def spread(mode):
        halo[pl.ds(0, CY), :] = low[mode].astype(F32)
        halo[pl.ds(CY, CY), :] = high[mode].astype(F32)
        row = mode * SHARE
        for i, at, of, count in (
            (0, 0, 0, SHARE),
            (1, 0, SHARE, CY - SHARE),
            (2, 2 * SHARE - CY, CY, CY - SHARE),
            (3, 0, 2 * CY - SHARE, SHARE),
        ):
            rows = pl.ds(i * STRIDE + row + at, count)
            part[rows, :] = part[rows, :] - halo[pl.ds(of, count), :]

    loop(0, 2 * MODES, spread)
    sends = []
    for i, rank in enumerate(EDGE_RANKS):
        pack_rank(part, i * STRIDE, strip, i, SENT // 16)
        send = pltpu.make_async_copy(strip.at[i], send_hbm.at[rank], send_sems.at[i])
        send.start()
        sends.append(send)
    for send in sends:
        send.wait()


def base_kernel(
    rank_ref, table_ref, pressure_hbm, source_hbm, concentration_hbm, mean_hbm, low_hbm, high_hbm,
    base_p_hbm, base_c_hbm,
    fields, source, mean, low, high, base_p, base_c, scale, sems, out_sems,
):
    copies = start_all(
        sems,
        [(mean_hbm, mean), (low_hbm, low), (high_hbm, high)]
        + [(pressure_hbm.at[m], fields.at[pl.ds(PAD + m * SPACED, SLAB), :]) for m in range(MODES)]
        + [(concentration_hbm.at[m], fields.at[pl.ds(PAD + (MODES + m) * SPACED, SLAB), :]) for m in range(MODES)]
        + [(source_hbm, source)],
    )
    for copy in copies:
        copy.wait()
    scale[...] = OMEGA / (6.0 * mean[...])
    masks = edge_masks()

    def one_mode(m):
        own = (table_ref[0, rank_ref[0] * MODES + m] >= 0).astype(F32)
        for index in range(2):
            base = pl.multiple_of(PAD + (index * MODES + m) * SPACED, 8)
            for x in range(PLANES):
                outer = None
                if x == 0:
                    outer = low[index * MODES + m].astype(F32)
                elif x == PLANES - 1:
                    outer = high[index * MODES + m].astype(F32)
                tile, image = laplace(fields, base, x, masks, outer)
                rows = pl.ds(x * CY, CY)
                term = own * (mean[rows, :] * rounded(image))
                if index == 0:
                    base_p[m, rows, :] = tile + scale[rows, :] * (source[m, rows, :] - term)
                else:
                    base_c[m, rows, :] = tile - DISPERSION * term

    loop(0, MODES, one_mode)
    for copy in start_all(out_sems, [(base_p, base_p_hbm), (base_c, base_c_hbm)]):
        copy.wait()


def contract_kernel(
    index, places, recv_hbm, kl_hbm, mean_hbm, send_hbm,
    recv, kl, mean, images, ordered, weights, outs, strip, recv_sems, sems, send_sems,
):
    rows = ROWS_HEAD if index == 0 else ROWS
    spans = ((0, 16), (30, 33)) if index == 0 else ((15, 31),)
    blocks = [block for first, last in spans for block in range(first, last)]

    def fetch(rank, part):
        first, last = spans[part]
        span = pl.ds(first * 16, (last - first) * 16)
        return pltpu.make_async_copy(recv_hbm.at[rank, span, :], recv.at[rank, span, :], recv_sems.at[part, rank])

    def begin(rank):
        for part in range(len(spans)):
            fetch(rank, part).start()

    loop(0, RANKS, begin)
    others = start_all(sems, [(kl_hbm, kl), (mean_hbm, mean)])

    def clear(rank):
        start = pl.multiple_of(rank * STRIDE, 8)
        outs[pl.ds(start, rows), :] = jnp.zeros((rows, CZ), F32)

    loop(0, RANKS, clear)
    for copy in others:
        copy.wait()
    for larger in range(ORDER):
        root = float(np.sqrt(np.float32(larger + 1)).astype(jnp.bfloat16))
        for d in range(KL):
            weights[larger * KL + d] = root * kl[d]

    def spread(rank):
        for part in range(len(spans)):
            fetch(rank, part).wait()
        unpack_rank(recv, rank, images, STRIDE, blocks)

    loop(0, RANKS, spread)
    for i in range(VALID):
        copy_share(ordered, i * FULL, images, places[i] + index * BODY)
    for part in range(0, FULL, 8):
        count = min(8, SHARE - part)
        held = [weights[i, pl.ds(part, 8), :] for i in range(ORDER * KL)]
        for i in range(VALID):
            total = None
            for d, larger, other in NEIGHBOURS[i]:
                term = held[(larger - 1) * KL + d] * ordered[pl.ds(other * FULL + part, 8), :]
                total = term if total is None else total + term
            outs[pl.ds(places[i] + part, count), :] = total[:count]
    if index == 0:
        start = places[OWNER]
        known = images[pl.ds(start + SENT_HIGH, SHARE), :] + images[pl.ds(start + SENT_LOW, SHARE), :]
        image = ordered[pl.ds(0, SHARE), :]
        total = outs[pl.ds(places[0], SHARE), :]
        here = mean[pl.ds(0, SHARE), :]
        head = known - OMEGA * (here * image + total) / (6.0 * here)
        top = rounded(head)
        for rank in range(RANKS):
            outs[pl.ds(rank * STRIDE + HIGH, SHARE), :] = top
            outs[pl.ds(rank * STRIDE + LOW, SHARE), :] = head - top

    def send(rank):
        return pltpu.make_async_copy(strip.at[rank], send_hbm.at[rank], send_sems.at[rank])

    def go(rank):
        pack_rank(outs, pl.multiple_of(rank * STRIDE, 8), strip, rank, rows // 16)
        send(rank).start()

    loop(0, RANKS, go)
    loop(0, RANKS, lambda rank: send(rank).wait())


def result_kernel(index, recv_hbm, base_hbm, mean_hbm, out_hbm, *rest):
    rows = ROWS if index else ROWS_HEAD
    stride = rows + PAD
    head_hbm = None if index else rest[0]
    recv, base, mean, scale, sums, head, out, recv_sems, base_sems, sems, extra_sems = rest[0 if index else 1 :]

    def fetch(rank):
        return pltpu.make_async_copy(recv_hbm.at[rank], recv.at[rank], recv_sems.at[rank])

    def fetch_base(m):
        target = base.at[pl.ds(pl.multiple_of(m * SPACED, 8), SLAB), :]
        return pltpu.make_async_copy(base_hbm.at[m], target, base_sems.at[m])

    def leave(m):
        source = out.at[pl.ds(pl.multiple_of(m * SPACED, 8), SLAB), :]
        return pltpu.make_async_copy(source, out_hbm.at[m], sems.at[m])

    loop(0, RANKS, lambda rank: fetch(rank).start())
    loop(0, MODES, lambda m: fetch_base(m).start())
    if index == 0:
        fetch_mean = pltpu.make_async_copy(mean_hbm, mean, extra_sems.at[0])
        fetch_mean.start()

    def spread(rank):
        fetch(rank).wait()
        unpack_rank(recv, rank, sums, stride, range(rows // 16))

    loop(0, RANKS, spread)
    if index == 0:
        fetch_mean.wait()
        scale[pl.ds(0, SLAB), :] = OMEGA / (6.0 * mean[...])
        for rank in range(RANKS):
            for part in range(0, FULL, 8):
                at = rank * stride + part
                head[pl.ds(rank * SHARE + part, 8), :] = sums[pl.ds(at + HIGH, 8), :] + sums[pl.ds(at + LOW, 8), :]
        head_out = pltpu.make_async_copy(head.at[pl.ds(0, SLAB), :], head_hbm, extra_sems.at[1])
        head_out.start()

    def one_mode(m):
        fetch_base(m).wait()
        for rank in range(RANKS):
            for part in range(0, FULL, 8):
                at = pl.ds(m * SPACED + rank * SHARE + part, 8)
                factor = DISPERSION if index else scale[pl.ds(rank * SHARE + part, 8), :]
                out[at, :] = base[at, :] - factor * sums[pl.ds(rank * stride + m * SHARE + part, 8), :]
        leave(m).start()

    loop(0, MODES, one_mode)
    if index == 0:
        head_out.wait()
    loop(0, MODES, lambda m: leave(m).wait())


def advection_kernel(
    field_hbm, low_hbm, high_hbm, base_hbm, mean_hbm, head_hbm, head_low_hbm, head_high_hbm, out_hbm,
    field, low, high, base, mean, head, head_low, head_high, out, speed, sems, out_sems,
):
    copies = start_all(
        sems,
        [
            (head_hbm, head.at[pl.ds(PAD, SLAB), :]),
            (head_low_hbm, head_low),
            (head_high_hbm, head_high),
            (mean_hbm, mean),
            (low_hbm, low),
            (high_hbm, high),
            (base_hbm, base),
        ]
        + [(field_hbm.at[m], field.at[pl.ds(PAD + m * SLAB, SLAB), :]) for m in range(MODES)],
    )
    masks = edge_masks()

    def steps(ref, base, x, outer):
        start = base + x * CY
        below = rows_of(ref, start - CY) if x > 0 else outer(0)
        above = rows_of(ref, start + CY) if x < PLANES - 1 else outer(1)
        y_less, y_more, z_less, z_more = beside(ref, start, rows_of(ref, start), masks)
        return above - below, y_more - y_less, z_more - z_less

    for copy in copies[:4]:
        copy.wait()
    for x in range(PLANES):
        rows = pl.ds(x * CY, CY)
        factor = (0.25 * STEP) * mean[rows, :]
        for axis, step in enumerate(steps(head, PAD, x, lambda side: (head_low, head_high)[side][...])):
            speed[axis, rows, :] = factor * step
    for copy in copies[4:]:
        copy.wait()

    def leave(m):
        return pltpu.make_async_copy(out.at[m], out_hbm.at[m], out_sems.at[m])

    def one_mode(m):
        for x in range(PLANES):
            rows = pl.ds(x * CY, CY)
            along = steps(
                field, pl.multiple_of(PAD + m * SLAB, 8), x, lambda side: (low, high)[side][MODES + m].astype(F32)
            )
            moved = sum(speed[axis, rows, :] * step for axis, step in enumerate(along))
            out[m, rows, :] = base[m, rows, :] + moved
        leave(m).start()

    loop(0, MODES, one_mode)
    loop(0, MODES, lambda m: leave(m).wait())


def local(pressure, source, concentration, mean_cond, kl_cond, mode_table):
    shape = pressure.shape
    spaces = lax.axis_size("space")
    up = [(i, i + 1) for i in range(spaces - 1)]
    down = [(i + 1, i) for i in range(spaces - 1)]
    rank = lax.axis_index("mode").astype(jnp.int32)
    table = mode_table.T
    size = pressure.size
    last = jnp.concatenate([pressure[:, -1], concentration[:, -1]], axis=0).astype(BF16)
    first = jnp.concatenate([pressure[:, 0], concentration[:, 0]], axis=0).astype(BF16)
    low = lax.ppermute(last, "space", up)
    high = lax.ppermute(first, "space", down)

    pressure, source, concentration = (a.reshape(MODES, SLAB, CZ) for a in (pressure, source, concentration))
    mean_cond = mean_cond.reshape(SLAB, CZ)
    kl_cond = kl_cond.reshape(KL, SLAB, CZ)

    field = jax.ShapeDtypeStruct(pressure.shape, F32)
    plane = jax.ShapeDtypeStruct(mean_cond.shape, F32)
    dma = pltpu.SemaphoreType.DMA
    field_vmem = pltpu.VMEM(pressure.shape, F32)
    halo_vmem = pltpu.VMEM((2 * MODES, CY, CZ), BF16)
    edge_vmem = pltpu.VMEM((CY, CZ), F32)

    def rows_vmem(rows):
        return pltpu.VMEM((rows, CZ), F32)

    def message(rows):
        return jax.ShapeDtypeStruct((RANKS, rows, CZ), BF16)

    def message_vmem(rows):
        return pltpu.VMEM((RANKS, rows, CZ), BF16)

    def exchange(rows_of_ranks):
        return lax.all_to_all(rows_of_ranks, "mode", 0, 0, tiled=True)

    send, part = call(
        inner_kernel,
        (message(SENT), jax.ShapeDtypeStruct((4, SENT, CZ), F32)),
        [vmem()] + [hbm()] * 4,
        [rows_vmem(2 * MODES * SPACED + 2 * PAD), rows_vmem(SLAB), rows_vmem(SLAB)]
        + [rows_vmem(SLAB + PAD)] * 3
        + [rows_vmem(RANKS * STRIDE), message_vmem(SENT), dma((2, MODES)), dma((2,)), dma((RANKS,)), dma((4,))],
        "inner_images",
        size * 20,
        size * 14,
    )(table, mean_cond, pressure, source, concentration)
    send = call(
        outer_kernel,
        message(SENT),
        [hbm()] * 4,
        [
            rows_vmem(4 * STRIDE),
            halo_vmem,
            halo_vmem,
            rows_vmem(2 * CY),
            pltpu.VMEM((4, SENT, CZ), BF16),
            dma((6,)),
            dma((4,)),
        ],
        "outer_images",
        size,
        size,
        {3: 0},
    )(part, low, high, send)
    recv = exchange(send)

    base_p, base_c = call(
        base_kernel,
        (field, field),
        [smem(), smem()] + [hbm()] * 6,
        [rows_vmem(2 * MODES * SPACED + 2 * PAD), field_vmem, rows_vmem(SLAB), halo_vmem, halo_vmem]
        + [field_vmem, field_vmem, rows_vmem(SLAB), dma((4 + 2 * MODES,)), dma((2,))],
        "base",
        size * 60,
        size * 24,
    )(rank.reshape(1), table, pressure, source, concentration, mean_cond, low, high)

    recv, base_p, base_c = lax.optimization_barrier((recv, base_p, base_c))

    code = jnp.sum(table * POWERS.astype(np.int32)[:, None], axis=0)
    row = jnp.sum(jnp.where(code[None, :] == CODES[:, None], jnp.arange(ALL, dtype=jnp.int32)[None, :], 0), axis=1)
    places = row // MODES * STRIDE + row % MODES * SHARE
    places = jnp.concatenate([places, row[:1] // MODES * STRIDE])

    def share(rows):
        rows = lax.dynamic_slice_in_dim(rows, rank * SHARE, SHARE, rows.ndim - 2)
        return jnp.pad(rows, [(0, 0)] * (rows.ndim - 2) + [(0, FULL - SHARE), (0, 0)], constant_values=1.0)

    own_kl, own_mean = share(kl_cond), share(mean_cond)

    def contract(index):
        rows = ROWS if index else ROWS_HEAD
        return call(
            functools.partial(contract_kernel, index),
            message(rows),
            [smem()] + [hbm()] * 3,
            [
                message_vmem(SENT),
                pltpu.VMEM((KL, FULL, CZ), F32),
                rows_vmem(FULL),
                rows_vmem(RANKS * STRIDE),
                rows_vmem(VALID * FULL),
                pltpu.VMEM((ORDER * KL, FULL, CZ), F32),
                rows_vmem(RANKS * STRIDE),
                message_vmem(rows),
                dma((2, RANKS)),
                dma((2,)),
                dma((RANKS,)),
            ],
            "contract_concentration" if index else "contract_pressure",
            size * 40,
            size * 8,
        )(places, recv, own_kl, own_mean)

    back_p = exchange(contract(0))
    back_c = exchange(contract(1))

    def result(index, received, base):
        rows = ROWS if index else ROWS_HEAD
        return call(
            functools.partial(result_kernel, index),
            field if index else (field, plane),
            [hbm()] * 3,
            [message_vmem(rows), rows_vmem(MODES * SPACED), rows_vmem(SLAB), rows_vmem(SLAB + PAD)]
            + [rows_vmem(RANKS * (rows + PAD)), rows_vmem(SLAB + PAD), rows_vmem(MODES * SPACED)]
            + [dma((RANKS,)), dma((MODES,)), dma((MODES,)), dma((2,))],
            "concentration_result" if index else "pressure_result",
            size * 4,
            size * 10,
        )(received, base, mean_cond)

    pressure_next, head = result(0, back_p, base_p)
    head_low = lax.ppermute(head[-CY:], "space", up)
    head_high = lax.ppermute(head[:CY], "space", down)
    moved = call(
        advection_kernel,
        field,
        [hbm()] * 8,
        [rows_vmem(MODES * SLAB + 2 * PAD), halo_vmem, halo_vmem, field_vmem, rows_vmem(SLAB)]
        + [rows_vmem(SLAB + 2 * PAD), edge_vmem, edge_vmem, field_vmem, pltpu.VMEM((3, SLAB, CZ), F32)]
        + [dma((7 + MODES,)), dma((MODES,))],
        "advection",
        size * 20,
        size * 12,
    )(concentration, low, high, base_c, mean_cond, head, head_low, head_high)
    concentration_next = result(1, back_c, moved)
    return (pressure_next.reshape(shape), concentration_next.reshape(shape))


def solution(mesh):
    return jax.shard_map(
        local,
        mesh=mesh,
        in_specs=(
            P("mode", "space", None, None),
            P("mode", "space", None, None),
            P("mode", "space", None, None),
            P("space", None, None),
            P(None, "space", None, None),
            P(),
        ),
        out_specs=(P("mode", "space", None, None), P("mode", "space", None, None)),
        check_vma=False,
    )
```

time: 485 us -> 119 us (0.25)
  waiting for transfers between devices: 343 us -> 36.5 us
  matrix products: 42.1 us -> 0 us
  Pallas kernels: 0 us -> 40.4 us
  other arithmetic: 39.9 us -> 0.95 us
  local copies, waits for them, and re-layouts: 24 us -> 5.98 us
  between operations: 16.1 us -> 2.85 us
  starting transfers between devices: 17.3 us -> 30.5 us
    all_gather x2 -> x0, waiting for transfers between devices: 199 us -> none  [the longest x1 102 us: local(): lax.all_gather(lap_conc, 'mode', axis=0, tiled=True)]
    psum x1 -> x0, waiting for transfers between devices: 132 us -> none  [spread(): return lax.psum(block, axis)]
    dot_general x2 -> x0, matrix products: 42.1 us -> none  [the longest x1 21.1 us: local(): jnp.einsum('jxyz,jtk->tkxyz', whole_conc, columns, preferred_element_type...]
    pallas_call x0 -> x8, Pallas kernels: none -> 40.4 us  [the longest x2 9.14 us: contract(): call(functools.partial(contract_kernel, index), message(rows), [smem()] +...]
    all_to_all x0 -> x3, waiting for transfers between devices: none -> 30.7 us  [exchange(): return lax.all_to_all(rows_of_ranks, 'mode', 0, 0, tiled=True)]
    sub x1 -> x0, other arithmetic: 15.7 us -> none  [local(): concentration - DISPERSION * galerkin_conc - STEP * advection]
    all_to_all x0 -> x3, starting transfers between devices: none -> 14.7 us  [exchange(): return lax.all_to_all(rows_of_ranks, 'mode', 0, 0, tiled=True)]
    add x1, other arithmetic: 13.1 us -> 0.02 us  [local(): places = row // MODES * STRIDE + row % MODES * SHARE]
  transfers between devices with their start and end apart: 7 -> 7, of which waited for: 5 -> 3; matrix products, arithmetic and copies ran while one was open for 8% -> 4% of each run, Pallas kernels for 0% -> 26%
where the time goes in v2:
time: 119 us; the launch traced here: 117 us
  Pallas kernels  40.4 us (34%)
  waiting for transfers between devices  36.5 us (31%)
  starting transfers between devices  30.5 us (26%)
  local copies, waits for them, and re-layouts  5.98 us (5%)
  between operations  2.85 us (2%)
    all_to_all x3, waiting for transfers between devices, exchange(): return lax.all_to_all(rows_of_ranks, 'mode', 0, 0, tiled=True)  30.7 us
    all_to_all x3, starting transfers between devices, exchange(): return lax.all_to_all(rows_of_ranks, 'mode', 0, 0, tiled=True)  14.7 us
    pallas_call x2, Pallas kernels, contract(): call(functools.partial(contract_kernel, index), message(rows), [smem()] +...  9.14 us
    pallas_call x1, Pallas kernels, local(): call(base_kernel, (field, field), [smem(), smem()] + [hbm()] * 6, [rows_v...  9.09 us
    pallas_call x1, Pallas kernels, local(): call(inner_kernel, (message(SENT), jax.ShapeDtypeStruct((4, SENT, CZ), F3...  7.75 us
    pallas_call x2, Pallas kernels, result(): call(functools.partial(result_kernel, index), field if index else (field,...  6.74 us
    ppermute x1, starting transfers between devices, local(): high = lax.ppermute(first, 'space', down)  5.83 us
    ppermute x1, waiting for transfers between devices, local(): head_low = lax.ppermute(head[-CY:], 'space', up)  5.79 us
  transfers between devices with their start and end apart: 7, of which 3 were waited for; matrix products, arithmetic and copies ran while one was open for 4% of the time, Pallas kernels for 26%

profile of v2, /device:TPU:2, one launch (start us, length us, event | category | flops | bytes accessed | tf_op | source)
XLA Modules:
  0.0 117.2 jit_solution(334645690403440726)
XLA Ops:
  0.6 0.0 copy-start
  0.6 1.4 %slice_bitcast_fusion = (bf16[11,32,128]{2,1,0:T(8,128)(2,1)S(1)}, bf16[11,32,128]{2,1,0:T(8,128)(2,1)S(1)}, bf16[11,32,128]{2,1,0:T(8,128)(2,1)S(1)}, bf16[11,32,128]{2,1,0:T(8,128)(2,1)S(1)}) fusion(f32[11,11,32,128]{3,2,1,0:T(8,128)} %param.8, f32[11,11,32,128]{3,2,1,0:T(8,128)} %param.10), kind=kLoop, calls=%fused_computation.5 | loop fusion | bytes 720896 | tf_op jit(solution)/shard_map/squeeze | solution.py:477
  2.0 3.8 %collective-permute-start = (bf16[22,32,128]{2,1,0:T(8,128)(2,1)S(1)}, bf16[22,32,128]{2,1,0:T(8,128)(2,1)S(1)}, u32[]{:S(2)}, u32[]{:S(2)}) collective-permute-start(bf16[22,32,128]{2,1,0:T(8,128)(2,1)S(1)} %pad_maximum_fusion), channel_id=1, source_target_pairs={{0,16},{16,32},{32,48},{48,64},{64,80},{80,96},{96,112},{112,128},... | collective-permute-start | bytes 540680 | tf_op jit(solution)/shard_map/ppermute | solution.py:478
  5.9 5.8 %collective-permute-start.1 = (bf16[22,32,128]{2,1,0:T(8,128)(2,1)S(1)}, bf16[22,32,128]{2,1,0:T(8,128)(2,1)S(1)}, u32[]{:S(2)}, u32[]{:S(2)}) collective-permute-start(bf16[22,32,128]{2,1,0:T(8,128)(2,1)S(1)} %pad_maximum_fusion.1), channel_id=1, source_target_pairs={{16,0},{32,16},{48,32},{64,48},{80,64},{96,80},{112,96},{128,112},... | collective-permute-start | bytes 540680 | tf_op jit(solution)/shard_map/ppermute | solution.py:479
  11.7 7.8 %inner_images.1 = (bf16[16,528,128]{2,1,0:T(8,128)(2,1)}, f32[4,528,128]{2,1,0:T(8,128)}) custom-call(s32[8,176]{1,0:T(8,128)} %bitcast.33, f32[352,128]{1,0:T(8,128)} %bitcast.26, f32[11,352,128]{2,1,0:T(8,128)} %bitcast.22, f32[11,352,128]{2,1,0:T(8,128)} %bitcast.24, f32[11,352,128]{2,1,0:T(8,128)} %bitcast.19), custom_call_target="tpu_custom_call" | custom-call | flops 9912320 | bytes 6938624 | tf_op jit(solution)/shard_map/inner_images/pallas_call | solution.py:504
  19.5 0.0 collective-permute-done.low_hbm
  19.5 0.0 copy-start.2
  19.5 0.0 collective-permute-done.1.high_hbm
  19.5 0.0 copy-start.3
  19.5 0.6 copy-done.2
  20.2 0.1 copy-done.3
  20.3 2.4 %outer_images.1 = bf16[16,528,128]{2,1,0:T(8,128)(2,1)} custom-call(f32[4,528,128]{2,1,0:T(8,128)} %get-tuple-element.11.part_hbm, bf16[22,32,128]{2,1,0:T(8,128)(2,1)} %copy-done.2, bf16[22,32,128]{2,1,0:T(8,128)(2,1)} %copy-done.3, bf16[16,528,128]{2,1,0:T(8,128)(2,1)} %get-tuple-element.12.send_in), custom_call_target="tpu_custom_call", output_to_operand_aliasing={{}: (3, {})} | custom-call | flops 495616 | bytes 495616 | tf_op jit(solution)/shard_map/outer_images/pallas_call | solution.py:515
  22.7 0.0 copy-start.4
  22.7 0.0 copy-start.8
  22.7 0.0 copy-start.7
  22.8 6.6 %all-to-all-start = ((bf16[16,528,128]{2,1,0:T(8,128)(2,1)}), bf16[16,528,128]{2,1,0:T(8,128)(2,1)}, u32[]{:S(2)}, u32[]{:S(2)}) async-start(bf16[16,528,128]{2,1,0:T(8,128)(2,1)} %outer_images.1), calls=%async_computation | async-start | bytes 4325376 | tf_op jit(solution)/shard_map/all_to_all | solution.py:502
  29.4 0.0 copy-done.4
  29.4 0.0 copy-done.8
  29.4 0.1 multiply_reduce_fusion
  29.5 0.0 copy-done.7
  29.5 0.2 select_reduce_fusion
  29.7 0.5 slice.25
  32.2 0.7 constant_dynamic-slice_fusion
  32.9 0.6 pad.9.mean_hbm
  33.5 0.0 copy-done
  33.5 0.6 pad.8.kl_hbm
  34.2 0.6 pad_add_fusion.places
  34.8 9.1 %base.1 = (f32[11,352,128]{2,1,0:T(8,128)}, f32[11,352,128]{2,1,0:T(8,128)}) custom-call(s32[1]{0:T(128)} %bitcast.9.rank_ref, s32[8,176]{1,0:T(8,128)} %bitcast.34, f32[11,352,128]{2,1,0:T(8,128)} %bitcast.23, f32[11,352,128]{2,1,0:T(8,128)} %bitcast.25, f32[11,352,128]{2,1,0:T(8,128)} %bitcast.20, f32[352,128]{1,0:T(8,128)} %bitcast.28, ...), custom_call_target="tpu_custom_call" | custom-call | flops 29736960 | bytes 11894784 | tf_op jit(solution)/shard_map/base/pallas_call | solution.py:535
  43.9 15.9 %all-to-all-done.recv_hbm = bf16[16,528,128]{2,1,0:T(8,128)(2,1)} async-done(((bf16[16,528,128]{2,1,0:T(8,128)(2,1)}), bf16[16,528,128]{2,1,0:T(8,128)(2,1)}, u32[]{:S(2)}, u32[]{:S(2)}) %all-to-all-start) | async-done | bytes 2162720 | tf_op jit(solution)/shard_map/all_to_all | solution.py:502
  59.8 4.5 %contract_pressure.1 = bf16[16,288,128]{2,1,0:T(8,128)(2,1)} custom-call(s32[166]{0:T(256)} %pad_add_fusion.places, bf16[16,528,128]{2,1,0:T(8,128)(2,1)} %all-to-all-done.recv_hbm, f32[8,24,128]{2,1,0:T(8,128)} %pad.8.kl_hbm, f32[24,128]{1,0:T(8,128)} %pad.9.mean_hbm), custom_call_target="tpu_custom_call" | custom-call | flops 19824640 | bytes 3964928 | tf_op jit(solution)/shard_map/contract_pressure/pallas_call | solution.py:561
  64.3 3.7 %all-to-all-start.1 = ((bf16[16,288,128]{2,1,0:T(8,128)(2,1)}), bf16[16,288,128]{2,1,0:T(8,128)(2,1)S(1)}, u32[]{:S(2)}, u32[]{:S(2)}) async-start(bf16[16,288,128]{2,1,0:T(8,128)(2,1)} %contract_pressure.1), calls=%async_computation.1 | async-start | bytes 2359296 | tf_op jit(solution)/shard_map/all_to_all | solution.py:502
  68.0 4.6 %contract_concentration.1 = bf16[16,256,128]{2,1,0:T(8,128)(2,1)} custom-call(s32[166]{0:T(256)} %pad_add_fusion.places, bf16[16,528,128]{2,1,0:T(8,128)(2,1)} %all-to-all-done.recv_hbm, f32[8,24,128]{2,1,0:T(8,128)} %pad.8.kl_hbm, f32[24,128]{1,0:T(8,128)} %pad.9.mean_hbm), custom_call_target="tpu_custom_call" | custom-call | flops 19824640 | bytes 3964928 | tf_op jit(solution)/shard_map/contract_concentration/pallas_call | solution.py:561
  72.6 14.8 %all-to-all-done.1.recv_hbm = bf16[16,288,128]{2,1,0:T(8,128)(2,1)S(1)} async-done(((bf16[16,288,128]{2,1,0:T(8,128)(2,1)}), bf16[16,288,128]{2,1,0:T(8,128)(2,1)S(1)}, u32[]{:S(2)}, u32[]{:S(2)}) %all-to-all-start.1) | async-done | bytes 1179680 | tf_op jit(solution)/shard_map/all_to_all | solution.py:502
  87.4 0.0 copy-start.1
  87.4 4.3 %all-to-all-start.2 = ((bf16[16,256,128]{2,1,0:T(8,128)(2,1)}), bf16[16,256,128]{2,1,0:T(8,128)(2,1)}, u32[]{:S(2)}, u32[]{:S(2)}) async-start(bf16[16,256,128]{2,1,0:T(8,128)(2,1)} %contract_concentration.1), calls=%async_computation.2 | async-start | bytes 2097152 | tf_op jit(solution)/shard_map/all_to_all | solution.py:502
  91.8 0.0 copy-done.1
  91.8 3.7 %pressure_result.1 = (f32[11,352,128]{2,1,0:T(8,128)}, f32[352,128]{1,0:T(8,128)}) custom-call(bf16[16,288,128]{2,1,0:T(8,128)(2,1)} %copy-done.1, f32[11,352,128]{2,1,0:T(8,128)} %get-tuple-element.16.base_hbm, f32[352,128]{1,0:T(8,128)} %bitcast.29), custom_call_target="tpu_custom_call" | custom-call | flops 1982464 | bytes 4956160 | tf_op jit(solution)/shard_map/pressure_result/pallas_call | solution.py:588
  95.5 0.7 fusion.2
  96.3 4.2 %collective-permute-start.3 = (f32[32,128]{1,0:T(8,128)S(1)}, f32[32,128]{1,0:T(8,128)S(1)}, u32[]{:S(2)}, u32[]{:S(2)}) collective-permute-start(f32[32,128]{1,0:T(8,128)S(1)} %get-tuple-element.24), channel_id=1, source_target_pairs={{16,0},{32,16},{48,32},{64,48},{80,64},{96,80},{112,96},{128,112},... | collective-permute-start | bytes 49160 | tf_op jit(solution)/shard_map/ppermute | solution.py:602
  100.5 1.9 %collective-permute-start.2 = (f32[32,128]{1,0:T(8,128)S(1)}, f32[32,128]{1,0:T(8,128)S(1)}, u32[]{:S(2)}, u32[]{:S(2)}) collective-permute-start(f32[32,128]{1,0:T(8,128)S(1)} %get-tuple-element.25), channel_id=1, source_target_pairs={{0,16},{16,32},{32,48},{48,64},{64,80},{80,96},{96,112},{112,128},... | collective-permute-start | bytes 49160 | tf_op jit(solution)/shard_map/ppermute | solution.py:601
  102.4 0.0 collective-permute-done.3.head_high_hbm
  102.4 0.0 copy-start.5
  102.4 5.8 %collective-permute-done.2.head_low_hbm = f32[32,128]{1,0:T(8,128)S(1)} collective-permute-done((f32[32,128]{1,0:T(8,128)S(1)}, f32[32,128]{1,0:T(8,128)S(1)}, u32[]{:S(2)}, u32[]{:S(2)}) %collective-permute-start.2) | collective-permute-done | bytes 16416 | tf_op jit(solution)/shard_map/ppermute | solution.py:601
  108.2 0.0 copy-done.5
  108.2 0.0 copy-start.6
  108.2 0.6 copy-done.6
  108.8 5.3 %advection.1.base_hbm = f32[11,352,128]{2,1,0:T(8,128)} custom-call(f32[11,352,128]{2,1,0:T(8,128)} %bitcast.21, bf16[22,32,128]{2,1,0:T(8,128)(2,1)} %copy-done.2, bf16[22,32,128]{2,1,0:T(8,128)(2,1)} %copy-done.3, f32[11,352,128]{2,1,0:T(8,128)} %get-tuple-element.18.base_hbm, f32[352,128]{1,0:T(8,128)} %bitcast.30, ...), custom_call_target="tpu_custom_call" | custom-call | flops 9912320 | bytes 5947392 | tf_op jit(solution)/shard_map/advection/pallas_call | solution.py:603
  114.1 0.0 all-to-all-done.2.recv_hbm
  114.1 3.0 %concentration_result.1 = f32[11,352,128]{2,1,0:T(8,128)} custom-call(bf16[16,256,128]{2,1,0:T(8,128)(2,1)} %all-to-all-done.2.recv_hbm, f32[11,352,128]{2,1,0:T(8,128)} %advection.1.base_hbm, f32[352,128]{1,0:T(8,128)} %bitcast.31), custom_call_target="tpu_custom_call" | custom-call | flops 1982464 | bytes 4956160 | tf_op jit(solution)/shard_map/concentration_result/pallas_call | solution.py:588
  (4 shorter events, 0.1 us)
Async XLA Ops:
  0.6 32.9 %copy-start = (f32[8,11,32,128]{3,2,1,0:T(8,128)S(1)}, f32[8,11,32,128]{3,2,1,0:T(8,128)}, u32[]{:S(2)}) copy-start(f32[8,11,32,128]{3,2,1,0:T(8,128)} %param.12) | copy-start | bytes 4325380
  2.0 17.5 %collective-permute-start = (bf16[22,32,128]{2,1,0:T(8,128)(2,1)S(1)}, bf16[22,32,128]{2,1,0:T(8,128)(2,1)S(1)}, u32[]{:S(2)}, u32[]{:S(2)}) collective-permute-start(bf16[22,32,128]{2,1,0:T(8,128)(2,1)S(1)} %pad_maximum_fusion), channel_id=1, source_target_pairs={{0,16},{16,32},{32,48},{48,64},{64,80},{80,96},{96,112},{112,128},... | collective-permute-start | bytes 540680 | tf_op jit(solution)/shard_map/ppermute | solution.py:478
  5.9 13.6 %collective-permute-start.1 = (bf16[22,32,128]{2,1,0:T(8,128)(2,1)S(1)}, bf16[22,32,128]{2,1,0:T(8,128)(2,1)S(1)}, u32[]{:S(2)}, u32[]{:S(2)}) collective-permute-start(bf16[22,32,128]{2,1,0:T(8,128)(2,1)S(1)} %pad_maximum_fusion.1), channel_id=1, source_target_pairs={{16,0},{32,16},{48,32},{64,48},{80,64},{96,80},{112,96},{128,112},... | collective-permute-start | bytes 540680 | tf_op jit(solution)/shard_map/ppermute | solution.py:479
  19.5 0.7 copy-start.2
  19.5 0.7 copy-start.3
  22.7 6.7 %copy-start.4 = (s32[176,8]{0,1:T(8,128)S(1)}, s32[176,8]{0,1:T(8,128)}, u32[]{:S(2)}) copy-start(s32[176,8]{0,1:T(8,128)} %param.13) | copy-start | bytes 16900
  22.7 6.7 %copy-start.8 = (s32[8]{0:T(128)S(1)}, s32[8]{0:T(128)}, u32[]{:S(2)}) copy-start(s32[8]{0:T(128)} %constant.62) | copy-start | bytes 100
  22.7 6.8 %copy-start.7 = (s32[165]{0:T(256)S(1)}, s32[165]{0:T(256)}, u32[]{:S(2)}) copy-start(s32[165]{0:T(256)} %constant.63) | copy-start | bytes 1984
  22.8 37.0 %all-to-all-start = ((bf16[16,528,128]{2,1,0:T(8,128)(2,1)}), bf16[16,528,128]{2,1,0:T(8,128)(2,1)}, u32[]{:S(2)}, u32[]{:S(2)}) async-start(bf16[16,528,128]{2,1,0:T(8,128)(2,1)} %outer_images.1), calls=%async_computation | async-start | bytes 4325376 | tf_op jit(solution)/shard_map/all_to_all | solution.py:502
  64.3 23.2 %all-to-all-start.1 = ((bf16[16,288,128]{2,1,0:T(8,128)(2,1)}), bf16[16,288,128]{2,1,0:T(8,128)(2,1)S(1)}, u32[]{:S(2)}, u32[]{:S(2)}) async-start(bf16[16,288,128]{2,1,0:T(8,128)(2,1)} %contract_pressure.1), calls=%async_computation.1 | async-start | bytes 2359296 | tf_op jit(solution)/shard_map/all_to_all | solution.py:502
  87.4 4.4 %copy-start.1 = (bf16[16,288,128]{2,1,0:T(8,128)(2,1)}, bf16[16,288,128]{2,1,0:T(8,128)(2,1)S(1)}, u32[]{:S(2)}) copy-start(bf16[16,288,128]{2,1,0:T(8,128)(2,1)S(1)} %all-to-all-done.1.recv_hbm) | copy-start | bytes 3538948
  87.4 26.7 %all-to-all-start.2 = ((bf16[16,256,128]{2,1,0:T(8,128)(2,1)}), bf16[16,256,128]{2,1,0:T(8,128)(2,1)}, u32[]{:S(2)}, u32[]{:S(2)}) async-start(bf16[16,256,128]{2,1,0:T(8,128)(2,1)} %contract_concentration.1), calls=%async_computation.2 | async-start | bytes 2097152 | tf_op jit(solution)/shard_map/all_to_all | solution.py:502
  96.3 6.1 %collective-permute-start.3 = (f32[32,128]{1,0:T(8,128)S(1)}, f32[32,128]{1,0:T(8,128)S(1)}, u32[]{:S(2)}, u32[]{:S(2)}) collective-permute-start(f32[32,128]{1,0:T(8,128)S(1)} %get-tuple-element.24), channel_id=1, source_target_pairs={{16,0},{32,16},{48,32},{64,48},{80,64},{96,80},{112,96},{128,112},... | collective-permute-start | bytes 49160 | tf_op jit(solution)/shard_map/ppermute | solution.py:602
  100.5 7.7 %collective-permute-start.2 = (f32[32,128]{1,0:T(8,128)S(1)}, f32[32,128]{1,0:T(8,128)S(1)}, u32[]{:S(2)}, u32[]{:S(2)}) collective-permute-start(f32[32,128]{1,0:T(8,128)S(1)} %get-tuple-element.25), channel_id=1, source_target_pairs={{0,16},{16,32},{32,48},{48,64},{64,80},{80,96},{96,112},{112,128},... | collective-permute-start | bytes 49160 | tf_op jit(solution)/shard_map/ppermute | solution.py:601
  102.4 5.8 %copy-start.5 = (f32[32,128]{1,0:T(8,128)}, f32[32,128]{1,0:T(8,128)S(1)}, u32[]{:S(2)}) copy-start(f32[32,128]{1,0:T(8,128)S(1)} %collective-permute-done.3.head_high_hbm) | copy-start | bytes 49156
  108.2 0.6 copy-start.6

commit v3 on v2

--- a/solution.py
+++ b/solution.py
@@ -31,17 +31,11 @@
 PAD = 8
 SPACED = SLAB + PAD
 
-SENT_HIGH = 2 * BODY
-SENT_LOW = SENT_HIGH + SHARE
-SENT = SENT_LOW + SHARE
-HIGH = BODY
-LOW = BODY + SHARE
-ROWS_HEAD = 288
-ROWS = 256
+SENT = 496
 STRIDE = SENT + PAD
 
 EDGE_RANKS = (0, 1, RANKS - 2, RANKS - 1)
-LIMIT = 60 * 1024 * 1024
+LIMIT = 63 * 1024 * 1024
 
 INDICES = sorted(
     (t for t in itertools.product(range(ORDER + 1), repeat=KL) if sum(t) <= ORDER), key=lambda t: (sum(t), t)
@@ -59,7 +53,6 @@
 VALID = len(INDICES)
 POWERS = (ORDER + 1) ** np.arange(KL)
 CODES = (np.array(INDICES) * POWERS).sum(axis=1).astype(np.int32)
-OWNER = VALID
 
 
 def vmem():
@@ -157,8 +150,7 @@
 
 
 def inner_kernel(
-    table_ref, mean_hbm, pressure_hbm, source_hbm, concentration_hbm, send_hbm, part_hbm,
-    fields, source, mean, image, high, low, scratch, strip, sems, extra_sems, send_sems, part_sems,
+    pressure_hbm, concentration_hbm, send_hbm, part_hbm, fields, image, scratch, strip, sems, send_sems, part_sems
 ):
     inputs = (pressure_hbm, concentration_hbm)
 
@@ -172,11 +164,8 @@
     for index in range(2):
         for m in range(MODES):
             fetch(index, m).start()
-    total = jnp.sum(jnp.abs(table_ref[...]).astype(F32), axis=0, keepdims=True)
-    place = lax.broadcasted_iota(jnp.int32, (1, ALL), 1).astype(F32)
-    row = jnp.min(jnp.where(total == 0.0, place, float(ALL))).astype(jnp.int32)
-    slot = lax.rem(row, MODES)
-    extra = start_all(extra_sems, [(source_hbm.at[slot], source), (mean_hbm, mean)])
+    for rank in range(RANKS):
+        scratch[pl.ds(rank * STRIDE + 2 * BODY, SENT - 2 * BODY), :] = jnp.zeros((SENT - 2 * BODY, CZ), F32)
     masks = edge_masks()
 
     for index in range(2):
@@ -189,17 +178,6 @@
                 copy_share(scratch, rank * STRIDE + (index * MODES + m) * SHARE, image, rank * SHARE)
 
         loop(0, MODES, one_mode)
-    for copy in extra:
-        copy.wait()
-    for x in range(PLANES):
-        rows = pl.ds(x * CY, CY)
-        head = rows_of(fields, base_of(0, slot) + x * CY) + (OMEGA / (6.0 * mean[rows, :])) * source[rows, :]
-        top = rounded(head)
-        high[rows, :] = top
-        low[rows, :] = head - top
-    for rank in range(RANKS):
-        copy_share(scratch, rank * STRIDE + SENT_HIGH, high, rank * SHARE)
-        copy_share(scratch, rank * STRIDE + SENT_LOW, low, rank * SHARE)
     parts = start_all(
         part_sems,
         [(scratch.at[pl.ds(rank * STRIDE, SENT), :], part_hbm.at[i]) for i, rank in enumerate(EDGE_RANKS)],
@@ -287,129 +265,159 @@
         copy.wait()
 
 
+def head_kernel(
+    rank_ref, table_ref, pressure_hbm, source_hbm, mean_hbm, kl_hbm, low_hbm, high_hbm, out_hbm,
+    field, source, mean, kl, low, high, scale, out, sems, mean_sem, out_sem,
+):
+    fetch_mean = pltpu.make_async_copy(mean_hbm, mean, mean_sem)
+    fetch_mean.start()
+    out[...] = jnp.zeros((SLAB, CZ), F32)
+    fetch_mean.wait()
+    scale[...] = OMEGA / (6.0 * mean[...])
+    masks = edge_masks()
+
+    def one_mode(m):
+        row = rank_ref[0] * MODES + m
+        degree = table_ref[0, row]
+        which = 0
+        for d in range(1, KL):
+            degree = degree + table_ref[d, row]
+            which = which + d * table_ref[d, row]
+
+        @pl.when((degree >= 0) & (degree <= 1))
+        def _():
+            copies = start_all(
+                sems,
+                [
+                    (pressure_hbm.at[m], field.at[pl.ds(PAD, SLAB), :]),
+                    (source_hbm.at[m], source),
+                    (kl_hbm.at[which], kl),
+                    (low_hbm.at[m], low),
+                    (high_hbm.at[m], high),
+                ],
+            )
+            for copy in copies:
+                copy.wait()
+            is_mean = (degree == 0).astype(F32)
+            for x in range(PLANES):
+                outer = None
+                if x == 0:
+                    outer = low[...].astype(F32)
+                elif x == PLANES - 1:
+                    outer = high[...].astype(F32)
+                tile, image = laplace(field, PAD, x, masks, outer)
+                image = rounded(image)
+                rows = pl.ds(x * CY, CY)
+                own = tile + scale[rows, :] * (source[rows, :] - mean[rows, :] * image)
+                brought = scale[rows, :] * (kl[rows, :] * image)
+                out[rows, :] = out[rows, :] + (is_mean * own - (1.0 - is_mean) * brought)
+
+    loop(0, MODES, one_mode)
+    leave = pltpu.make_async_copy(out, out_hbm, out_sem)
+    leave.start()
+    leave.wait()
+
+
 def contract_kernel(
-    index, places, recv_hbm, kl_hbm, mean_hbm, send_hbm,
-    recv, kl, mean, images, ordered, weights, outs, strip, recv_sems, sems, send_sems,
+    places, recv_hbm, kl_hbm, send_hbm,
+    recv, kl, images, ordered, weights, outs, strip, recv_sems, kl_sem, send_sems,
 ):
-    rows = ROWS_HEAD if index == 0 else ROWS
-    spans = ((0, 16), (30, 33)) if index == 0 else ((15, 31),)
-    blocks = [block for first, last in spans for block in range(first, last)]
-
-    def fetch(rank, part):
-        first, last = spans[part]
-        span = pl.ds(first * 16, (last - first) * 16)
-        return pltpu.make_async_copy(recv_hbm.at[rank, span, :], recv.at[rank, span, :], recv_sems.at[part, rank])
-
-    def begin(rank):
-        for part in range(len(spans)):
-            fetch(rank, part).start()
-
-    loop(0, RANKS, begin)
-    others = start_all(sems, [(kl_hbm, kl), (mean_hbm, mean)])
+    def fetch(rank):
+        return pltpu.make_async_copy(recv_hbm.at[rank], recv.at[rank], recv_sems.at[rank])
+
+    loop(0, RANKS, lambda rank: fetch(rank).start())
+    fetch_kl = pltpu.make_async_copy(kl_hbm, kl, kl_sem)
+    fetch_kl.start()
 
     def clear(rank):
-        start = pl.multiple_of(rank * STRIDE, 8)
-        outs[pl.ds(start, rows), :] = jnp.zeros((rows, CZ), F32)
+        outs[pl.ds(pl.multiple_of(rank * STRIDE, 8), SENT), :] = jnp.zeros((SENT, CZ), F32)
 
     loop(0, RANKS, clear)
-    for copy in others:
-        copy.wait()
+    fetch_kl.wait()
     for larger in range(ORDER):
         root = float(np.sqrt(np.float32(larger + 1)).astype(jnp.bfloat16))
         for d in range(KL):
             weights[larger * KL + d] = root * kl[d]
 
     def spread(rank):
-        for part in range(len(spans)):
-            fetch(rank, part).wait()
-        unpack_rank(recv, rank, images, STRIDE, blocks)
+        fetch(rank).wait()
+        unpack_rank(recv, rank, images, STRIDE, range(SENT // 16))
 
     loop(0, RANKS, spread)
-    for i in range(VALID):
-        copy_share(ordered, i * FULL, images, places[i] + index * BODY)
-    for part in range(0, FULL, 8):
-        count = min(8, SHARE - part)
-        held = [weights[i, pl.ds(part, 8), :] for i in range(ORDER * KL)]
+
+    def one_field(index):
         for i in range(VALID):
-            total = None
-            for d, larger, other in NEIGHBOURS[i]:
-                term = held[(larger - 1) * KL + d] * ordered[pl.ds(other * FULL + part, 8), :]
-                total = term if total is None else total + term
-            outs[pl.ds(places[i] + part, count), :] = total[:count]
-    if index == 0:
-        start = places[OWNER]
-        known = images[pl.ds(start + SENT_HIGH, SHARE), :] + images[pl.ds(start + SENT_LOW, SHARE), :]
-        image = ordered[pl.ds(0, SHARE), :]
-        total = outs[pl.ds(places[0], SHARE), :]
-        here = mean[pl.ds(0, SHARE), :]
-        head = known - OMEGA * (here * image + total) / (6.0 * here)
-        top = rounded(head)
-        for rank in range(RANKS):
-            outs[pl.ds(rank * STRIDE + HIGH, SHARE), :] = top
-            outs[pl.ds(rank * STRIDE + LOW, SHARE), :] = head - top
+            copy_share(ordered, i * FULL, images, places[i] + index * BODY)
+        for part in range(0, FULL, 8):
+            count = min(8, SHARE - part)
+            held = [weights[i, pl.ds(part, 8), :] for i in range(ORDER * KL)]
+            for i in range(VALID):
+                total = None
+                for d, larger, other in NEIGHBOURS[i]:
+                    term = held[(larger - 1) * KL + d] * ordered[pl.ds(other * FULL + part, 8), :]
+                    total = term if total is None else total + term
+                outs[pl.ds(places[i] + index * BODY + part, count), :] = total[:count]
+
+    loop(0, 2, one_field)
 
     def send(rank):
         return pltpu.make_async_copy(strip.at[rank], send_hbm.at[rank], send_sems.at[rank])
 
     def go(rank):
-        pack_rank(outs, pl.multiple_of(rank * STRIDE, 8), strip, rank, rows // 16)
+        pack_rank(outs, pl.multiple_of(rank * STRIDE, 8), strip, rank, SENT // 16)
         send(rank).start()
 
     loop(0, RANKS, go)
     loop(0, RANKS, lambda rank: send(rank).wait())
 
 
-def result_kernel(index, recv_hbm, base_hbm, mean_hbm, out_hbm, *rest):
-    rows = ROWS if index else ROWS_HEAD
-    stride = rows + PAD
-    head_hbm = None if index else rest[0]
-    recv, base, mean, scale, sums, head, out, recv_sems, base_sems, sems, extra_sems = rest[0 if index else 1 :]
+def result_kernel(
+    recv_hbm, base_p_hbm, base_c_hbm, mean_hbm, out_p_hbm, out_c_hbm,
+    recv, base, mean, scale, sums, out, recv_sems, base_sems, mean_sem, sems,
+):
+    bases = (base_p_hbm, base_c_hbm)
+    outputs = (out_p_hbm, out_c_hbm)
 
     def fetch(rank):
         return pltpu.make_async_copy(recv_hbm.at[rank], recv.at[rank], recv_sems.at[rank])
 
-    def fetch_base(m):
-        target = base.at[pl.ds(pl.multiple_of(m * SPACED, 8), SLAB), :]
-        return pltpu.make_async_copy(base_hbm.at[m], target, base_sems.at[m])
-
-    def leave(m):
-        source = out.at[pl.ds(pl.multiple_of(m * SPACED, 8), SLAB), :]
-        return pltpu.make_async_copy(source, out_hbm.at[m], sems.at[m])
+    def rows_at(index, m):
+        return pl.ds(pl.multiple_of((index * MODES + m) * SPACED, 8), SLAB)
+
+    def fetch_base(index, m):
+        return pltpu.make_async_copy(bases[index].at[m], base.at[rows_at(index, m), :], base_sems.at[index, m])
+
+    def leave(index, m):
+        return pltpu.make_async_copy(out.at[rows_at(index, m), :], outputs[index].at[m], sems.at[index, m])
 
     loop(0, RANKS, lambda rank: fetch(rank).start())
-    loop(0, MODES, lambda m: fetch_base(m).start())
-    if index == 0:
-        fetch_mean = pltpu.make_async_copy(mean_hbm, mean, extra_sems.at[0])
-        fetch_mean.start()
+    fetch_mean = pltpu.make_async_copy(mean_hbm, mean, mean_sem)
+    fetch_mean.start()
+    for index in range(2):
+        loop(0, MODES, lambda m: fetch_base(index, m).start())
+    fetch_mean.wait()
+    scale[pl.ds(0, SLAB), :] = OMEGA / (6.0 * mean[...])
 
     def spread(rank):
         fetch(rank).wait()
-        unpack_rank(recv, rank, sums, stride, range(rows // 16))
+        unpack_rank(recv, rank, sums, STRIDE, range(SENT // 16))
 
     loop(0, RANKS, spread)
-    if index == 0:
-        fetch_mean.wait()
-        scale[pl.ds(0, SLAB), :] = OMEGA / (6.0 * mean[...])
-        for rank in range(RANKS):
-            for part in range(0, FULL, 8):
-                at = rank * stride + part
-                head[pl.ds(rank * SHARE + part, 8), :] = sums[pl.ds(at + HIGH, 8), :] + sums[pl.ds(at + LOW, 8), :]
-        head_out = pltpu.make_async_copy(head.at[pl.ds(0, SLAB), :], head_hbm, extra_sems.at[1])
-        head_out.start()
-
-    def one_mode(m):
-        fetch_base(m).wait()
-        for rank in range(RANKS):
-            for part in range(0, FULL, 8):
-                at = pl.ds(m * SPACED + rank * SHARE + part, 8)
-                factor = DISPERSION if index else scale[pl.ds(rank * SHARE + part, 8), :]
-                out[at, :] = base[at, :] - factor * sums[pl.ds(rank * stride + m * SHARE + part, 8), :]
-        leave(m).start()
-
-    loop(0, MODES, one_mode)
-    if index == 0:
-        head_out.wait()
-    loop(0, MODES, lambda m: leave(m).wait())
+    for index in range(2):
+
+        def one_mode(m):
+            fetch_base(index, m).wait()
+            for rank in range(RANKS):
+                for part in range(0, FULL, 8):
+                    at = pl.ds((index * MODES + m) * SPACED + rank * SHARE + part, 8)
+                    factor = DISPERSION if index else scale[pl.ds(rank * SHARE + part, 8), :]
+                    total = sums[pl.ds(rank * STRIDE + (index * MODES + m) * SHARE + part, 8), :]
+                    out[at, :] = base[at, :] - factor * total
+            leave(index, m).start()
+
+        loop(0, MODES, one_mode)
+    for index in range(2):
+        loop(0, MODES, lambda m: leave(index, m).wait())
 
 
 def advection_kernel(
@@ -504,14 +512,13 @@
     send, part = call(
         inner_kernel,
         (message(SENT), jax.ShapeDtypeStruct((4, SENT, CZ), F32)),
-        [vmem()] + [hbm()] * 4,
-        [rows_vmem(2 * MODES * SPACED + 2 * PAD), rows_vmem(SLAB), rows_vmem(SLAB)]
-        + [rows_vmem(SLAB + PAD)] * 3
-        + [rows_vmem(RANKS * STRIDE), message_vmem(SENT), dma((2, MODES)), dma((2,)), dma((RANKS,)), dma((4,))],
+        [hbm()] * 2,
+        [rows_vmem(2 * MODES * SPACED + 2 * PAD), rows_vmem(SLAB + PAD), rows_vmem(RANKS * STRIDE), message_vmem(SENT)]
+        + [dma((2, MODES)), dma((RANKS,)), dma((4,))],
         "inner_images",
         size * 20,
         size * 14,
-    )(table, mean_cond, pressure, source, concentration)
+    )(pressure, concentration)
     send = call(
         outer_kernel,
         message(SENT),
@@ -532,6 +539,27 @@
     )(part, low, high, send)
     recv = exchange(send)
 
+    own_rank = rank.reshape(1)
+    head = call(
+        head_kernel,
+        plane,
+        [smem(), smem()] + [hbm()] * 6,
+        [rows_vmem(SLAB + 2 * PAD)] + [rows_vmem(SLAB)] * 3
+        + [pltpu.VMEM((CY, CZ), BF16)] * 2 + [rows_vmem(SLAB)] * 2 + [dma((5,)), dma(()), dma(())],
+        "head_part",
+        size,
+        size,
+    )(own_rank, table, pressure, source, mean_cond, kl_cond, low, high)
+
+    def partner(rows, bits):
+        return lax.ppermute(rows, "mode", [(i, i ^ bits) for i in range(RANKS)])
+
+    core = rank % 2
+    half = SLAB // 2
+    kept = lax.dynamic_slice_in_dim(head, core * half, half, 0)
+    kept = kept + partner(lax.dynamic_slice_in_dim(head, (1 - core) * half, half, 0), 1)
+    kept = kept + partner(kept, 2)
+
     base_p, base_c = call(
         base_kernel,
         (field, field),
@@ -541,63 +569,45 @@
         "base",
         size * 60,
         size * 24,
-    )(rank.reshape(1), table, pressure, source, concentration, mean_cond, low, high)
-
-    recv, base_p, base_c = lax.optimization_barrier((recv, base_p, base_c))
+    )(own_rank, table, pressure, source, concentration, mean_cond, low, high)
+
+    recv, base_p, base_c, kept = lax.optimization_barrier((recv, base_p, base_c, kept))
 
     code = jnp.sum(table * POWERS.astype(np.int32)[:, None], axis=0)
     row = jnp.sum(jnp.where(code[None, :] == CODES[:, None], jnp.arange(ALL, dtype=jnp.int32)[None, :], 0), axis=1)
     places = row // MODES * STRIDE + row % MODES * SHARE
-    places = jnp.concatenate([places, row[:1] // MODES * STRIDE])
-
-    def share(rows):
-        rows = lax.dynamic_slice_in_dim(rows, rank * SHARE, SHARE, rows.ndim - 2)
-        return jnp.pad(rows, [(0, 0)] * (rows.ndim - 2) + [(0, FULL - SHARE), (0, 0)], constant_values=1.0)
-
-    own_kl, own_mean = share(kl_cond), share(mean_cond)
-
-    def contract(index):
-        rows = ROWS if index else ROWS_HEAD
-        return call(
-            functools.partial(contract_kernel, index),
-            message(rows),
-            [smem()] + [hbm()] * 3,
-            [
-                message_vmem(SENT),
-                pltpu.VMEM((KL, FULL, CZ), F32),
-                rows_vmem(FULL),
-                rows_vmem(RANKS * STRIDE),
-                rows_vmem(VALID * FULL),
-                pltpu.VMEM((ORDER * KL, FULL, CZ), F32),
-                rows_vmem(RANKS * STRIDE),
-                message_vmem(rows),
-                dma((2, RANKS)),
-                dma((2,)),
-                dma((RANKS,)),
-            ],
-            "contract_concentration" if index else "contract_pressure",
-            size * 40,
-            size * 8,
-        )(places, recv, own_kl, own_mean)
-
-    back_p = exchange(contract(0))
-    back_c = exchange(contract(1))
-
-    def result(index, received, base):
-        rows = ROWS if index else ROWS_HEAD
-        return call(
-            functools.partial(result_kernel, index),
-            field if index else (field, plane),
-            [hbm()] * 3,
-            [message_vmem(rows), rows_vmem(MODES * SPACED), rows_vmem(SLAB), rows_vmem(SLAB + PAD)]
-            + [rows_vmem(RANKS * (rows + PAD)), rows_vmem(SLAB + PAD), rows_vmem(MODES * SPACED)]
-            + [dma((RANKS,)), dma((MODES,)), dma((MODES,)), dma((2,))],
-            "concentration_result" if index else "pressure_result",
-            size * 4,
-            size * 10,
-        )(received, base, mean_cond)
-
-    pressure_next, head = result(0, back_p, base_p)
+
+    own_kl = lax.dynamic_slice_in_dim(kl_cond, rank * SHARE, SHARE, 1)
+    own_kl = jnp.pad(own_kl, ((0, 0), (0, FULL - SHARE), (0, 0)))
+
+    back = call(
+        contract_kernel,
+        message(SENT),
+        [smem()] + [hbm()] * 2,
+        [
+            message_vmem(SENT),
+            pltpu.VMEM((KL, FULL, CZ), F32),
+            rows_vmem(RANKS * STRIDE),
+            rows_vmem(VALID * FULL),
+            pltpu.VMEM((ORDER * KL, FULL, CZ), F32),
+            rows_vmem(RANKS * STRIDE),
+            message_vmem(SENT),
+            dma((RANKS,)),
+            dma(()),
+            dma((RANKS,)),
+        ],
+        "contract",
+        size * 80,
+        size * 16,
+    )(places, recv, own_kl)
+    kept = (kept + partner(kept, 4)) + (partner(kept, 8) + partner(kept, 12))
+    back, kept = lax.optimization_barrier((back, kept))
+    received = exchange(back)
+
+    other = partner(kept, 1)
+    first_half = jnp.where(core == 0, kept, other)
+    second_half = jnp.where(core == 0, other, kept)
+    head = jnp.concatenate([first_half, second_half], axis=0)
     head_low = lax.ppermute(head[-CY:], "space", up)
     head_high = lax.ppermute(head[:CY], "space", down)
     moved = call(
@@ -611,7 +621,17 @@
         size * 20,
         size * 12,
     )(concentration, low, high, base_c, mean_cond, head, head_low, head_high)
-    concentration_next = result(1, back_c, moved)
+    pressure_next, concentration_next = call(
+        result_kernel,
+        (field, field),
+        [hbm()] * 4,
+        [message_vmem(SENT), rows_vmem(2 * MODES * SPACED), rows_vmem(SLAB), rows_vmem(SLAB + PAD)]
+        + [rows_vmem(RANKS * STRIDE), rows_vmem(2 * MODES * SPACED)]
+        + [dma((RANKS,)), dma((2, MODES)), dma(()), dma((2, MODES))],
+        "result",
+        size * 8,
+        size * 20,
+    )(received, base_p, moved, mean_cond)
     return (pressure_next.reshape(shape), concentration_next.reshape(shape))
 
 

time: 119 us -> 109 us (0.916); the launches traced: 117 us -> 108 us
  waiting for transfers between devices: 36.5 us -> 25.9 us
  starting transfers between devices: 30.5 us -> 35.1 us
  between operations: 2.85 us -> 0.92 us
  other arithmetic: 0.95 us -> 2.56 us
  Pallas kernels: 40.4 us -> 38.9 us
    all_to_all x3 -> x2, waiting for transfers between devices: 30.7 us -> 12.2 us  [exchange(): return lax.all_to_all(rows_of_ranks, 'mode', 0, 0, tiled=True)]
    ppermute x0 -> x6, waiting for transfers between devices: none -> 13 us  [partner(): return lax.ppermute(rows, 'mode', [(i, i ^ bits) for i in range(RANKS)])]
    ppermute x0 -> x6, starting transfers between devices: none -> 6.58 us  [partner(): return lax.ppermute(rows, 'mode', [(i, i ^ bits) for i in range(RANKS)])]
    ppermute x1, waiting for transfers between devices: 5.79 us -> 0.01 us  [local(): head_low = lax.ppermute(head[-CY:], 'space', up)]
    all_to_all x3 -> x2, starting transfers between devices: 14.7 us -> 10.9 us  [exchange(): return lax.all_to_all(rows_of_ranks, 'mode', 0, 0, tiled=True)]
    ppermute x1, starting transfers between devices: 4.2 us -> 6.03 us  [local(): head_high = lax.ppermute(head[:CY], 'space', down)]
    pallas_call x4 -> x3, Pallas kernels: 15.9 us -> 15.1 us  [the longest x1 6.51 us: local(): call(contract_kernel, message(SENT), [smem()] + [hbm()] * 2, [message_vme...]
  transfers between devices with their start and end apart: 7 -> 12, of which waited for: 3 -> 5; matrix products, arithmetic and copies ran while one was open for 4% -> 5% of each run, Pallas kernels for 26% -> 29%
where the time goes in v3:
time: 109 us; the launch traced here: 108 us
  Pallas kernels  38.9 us (36%)
  starting transfers between devices  35.1 us (32%)
  waiting for transfers between devices  25.9 us (24%)
  local copies, waits for them, and re-layouts  5.09 us (5%)
  other arithmetic  2.56 us (2%)
    ppermute x6, waiting for transfers between devices, partner(): return lax.ppermute(rows, 'mode', [(i, i ^ bits) for i in range(RANKS)])  13 us
    all_to_all x2, waiting for transfers between devices, exchange(): return lax.all_to_all(rows_of_ranks, 'mode', 0, 0, tiled=True)  12.2 us
    all_to_all x2, starting transfers between devices, exchange(): return lax.all_to_all(rows_of_ranks, 'mode', 0, 0, tiled=True)  10.9 us
    pallas_call x1, Pallas kernels, local(): call(base_kernel, (field, field), [smem(), smem()] + [hbm()] * 6, [rows_v...  9.05 us
    pallas_call x1, Pallas kernels, local(): call(inner_kernel, (message(SENT), jax.ShapeDtypeStruct((4, SENT, CZ), F3...  6.91 us
    ppermute x6, starting transfers between devices, partner(): return lax.ppermute(rows, 'mode', [(i, i ^ bits) for i in range(RANKS)])  6.58 us
    pallas_call x1, Pallas kernels, local(): call(contract_kernel, message(SENT), [smem()] + [hbm()] * 2, [message_vme...  6.51 us
    ppermute x1, starting transfers between devices, local(): head_high = lax.ppermute(head[:CY], 'space', down)  6.03 us
  transfers between devices with their start and end apart: 12, of which 5 were waited for; matrix products, arithmetic and copies ran while one was open for 5% of the time, Pallas kernels for 29%

profile of v3, /device:TPU:2, one launch (start us, length us, event | category | flops | bytes accessed | tf_op | source)
XLA Modules:
  0.0 108.5 jit_solution(11345452531992718987)
XLA Ops:
  0.6 1.3 %slice_bitcast_fusion = (bf16[11,32,128]{2,1,0:T(8,128)(2,1)S(1)}, bf16[11,32,128]{2,1,0:T(8,128)(2,1)S(1)}, bf16[11,32,128]{2,1,0:T(8,128)(2,1)S(1)}, bf16[11,32,128]{2,1,0:T(8,128)(2,1)S(1)}) fusion(f32[11,11,32,128]{3,2,1,0:T(8,128)} %param.8, f32[11,11,32,128]{3,2,1,0:T(8,128)} %param.10), kind=kLoop, calls=%fused_computation.6 | loop fusion | bytes 720896 | tf_op jit(solution)/shard_map/squeeze | solution.py:485
  1.9 3.8 %collective-permute-start = (bf16[22,32,128]{2,1,0:T(8,128)(2,1)S(1)}, bf16[22,32,128]{2,1,0:T(8,128)(2,1)S(1)}, u32[]{:S(2)}, u32[]{:S(2)}) collective-permute-start(bf16[22,32,128]{2,1,0:T(8,128)(2,1)S(1)} %pad_maximum_fusion), channel_id=1, source_target_pairs={{0,16},{16,32},{32,48},{48,64},{64,80},{80,96},{96,112},{112,128},... | collective-permute-start | bytes 540680 | tf_op jit(solution)/shard_map/ppermute | solution.py:486
  5.8 5.8 %collective-permute-start.1 = (bf16[22,32,128]{2,1,0:T(8,128)(2,1)S(1)}, bf16[22,32,128]{2,1,0:T(8,128)(2,1)S(1)}, u32[]{:S(2)}, u32[]{:S(2)}) collective-permute-start(bf16[22,32,128]{2,1,0:T(8,128)(2,1)S(1)} %pad_maximum_fusion.1), channel_id=1, source_target_pairs={{16,0},{32,16},{48,32},{64,48},{80,64},{96,80},{112,96},{128,112},... | collective-permute-start | bytes 540680 | tf_op jit(solution)/shard_map/ppermute | solution.py:487
  11.6 6.9 %inner_images.1 = (bf16[16,496,128]{2,1,0:T(8,128)(2,1)}, f32[4,496,128]{2,1,0:T(8,128)}) custom-call(f32[11,352,128]{2,1,0:T(8,128)} %bitcast.18, f32[11,352,128]{2,1,0:T(8,128)} %bitcast.21), custom_call_target="tpu_custom_call" | custom-call | flops 9912320 | bytes 6938624 | tf_op jit(solution)/shard_map/inner_images/pallas_call | solution.py:512
  18.5 0.0 collective-permute-done.low_hbm
  18.5 0.0 copy-start
  18.6 0.0 collective-permute-done.1.high_hbm
  18.6 0.0 copy-start.1
  18.6 0.6 copy-done
  19.2 0.1 copy-done.1
  19.3 2.6 %outer_images.1 = bf16[16,496,128]{2,1,0:T(8,128)(2,1)} custom-call(f32[4,496,128]{2,1,0:T(8,128)} %get-tuple-element.14.part_hbm, bf16[22,32,128]{2,1,0:T(8,128)(2,1)} %copy-done, bf16[22,32,128]{2,1,0:T(8,128)(2,1)} %copy-done.1, bf16[16,496,128]{2,1,0:T(8,128)(2,1)} %get-tuple-element.15.send_in), custom_call_target="tpu_custom_call", output_to_operand_aliasing={{}: (3, {})} | custom-call | flops 495616 | bytes 495616 | tf_op jit(solution)/shard_map/outer_images/pallas_call | solution.py:522
  21.9 0.0 copy-start.2
  21.9 0.0 copy-start.6
  21.9 6.5 %all-to-all-start = ((bf16[16,496,128]{2,1,0:T(8,128)(2,1)}), bf16[16,496,128]{2,1,0:T(8,128)(2,1)}, u32[]{:S(2)}, u32[]{:S(2)}) async-start(bf16[16,496,128]{2,1,0:T(8,128)(2,1)} %outer_images.1), calls=%async_computation | async-start | bytes 4063232 | tf_op jit(solution)/shard_map/all_to_all | solution.py:510
  28.4 0.0 copy-done.2
  28.5 0.0 copy-done.6
  28.5 0.1 multiply_reduce_fusion
  28.6 0.0 copy-start.5
  28.6 4.1 %head_part.1 = f32[352,128]{1,0:T(8,128)} custom-call(s32[1]{0:T(128)} %bitcast.7.rank_ref, s32[8,176]{1,0:T(8,128)} %bitcast.32, f32[11,352,128]{2,1,0:T(8,128)} %bitcast.19, f32[11,352,128]{2,1,0:T(8,128)} %bitcast.24, f32[352,128]{1,0:T(8,128)} %bitcast.26, f32[8,352,128]{2,1,0:T(8,128)} %bitcast.30, bf16[22,32,128]{2,1,0:T(8,128)(2,1)} %copy-done, ...), custom_call_target="tpu_custom_call" | custom-call | flops 495616 | bytes 495616 | tf_op jit(solution)/shard_map/head_part/pallas_call | solution.py:543
  32.7 0.9 constant_dynamic-slice_fusion.1
  33.6 0.0 collective-permute-start.2
  33.6 0.0 copy-done.5
  33.6 0.2 select_reduce_fusion
  33.8 1.1 collective-permute-done.2
  34.8 0.9 dynamic-slice_add_fusion
  35.8 2.2 %collective-permute-start.3 = (f32[176,128]{1,0:T(8,128)S(1)}, f32[176,128]{1,0:T(8,128)S(1)}, u32[]{:S(2)}, u32[]{:S(2)}) collective-permute-start(f32[176,128]{1,0:T(8,128)S(1)} %dynamic-slice_add_fusion), channel_id=1, source_target_pairs={{0,2},{1,3},{2,0},{3,1},{4,6},{5,7},{6,4},{7,5},{8,10},{9,11},{10,... | collective-permute-start | bytes 270344 | tf_op jit(solution)/shard_map/ppermute | solution.py:555
  37.9 0.6 fusion.1.places
  38.5 9.0 %base.1 = (f32[11,352,128]{2,1,0:T(8,128)}, f32[11,352,128]{2,1,0:T(8,128)}) custom-call(s32[1]{0:T(128)} %bitcast.7.rank_ref, s32[8,176]{1,0:T(8,128)} %bitcast.33, f32[11,352,128]{2,1,0:T(8,128)} %bitcast.20, f32[11,352,128]{2,1,0:T(8,128)} %bitcast.25, f32[11,352,128]{2,1,0:T(8,128)} %bitcast.22, f32[352,128]{1,0:T(8,128)} %bitcast.27, ...), custom_call_target="tpu_custom_call" | custom-call | flops 29736960 | bytes 11894784 | tf_op jit(solution)/shard_map/base/pallas_call | solution.py:563
  47.6 10.7 %collective-permute-done.3 = f32[176,128]{1,0:T(8,128)S(1)} collective-permute-done((f32[176,128]{1,0:T(8,128)S(1)}, f32[176,128]{1,0:T(8,128)S(1)}, u32[]{:S(2)}, u32[]{:S(2)}) %collective-permute-start.3) | collective-permute-done | bytes 90144 | tf_op jit(solution)/shard_map/ppermute | solution.py:555
  58.3 0.0 all-to-all-done.recv_hbm
  58.3 1.5 %collective-permute-start.6 = (f32[176,128]{1,0:T(8,128)S(1)}, f32[176,128]{1,0:T(8,128)S(1)}, u32[]{:S(2)}, u32[]{:S(2)}) collective-permute-start(f32[176,128]{1,0:T(8,128)S(1)} %add.46), channel_id=1, source_target_pairs={{0,12},{1,13},{2,14},{3,15},{4,8},{5,9},{6,10},{7,11},{8,4},{9,5},... | collective-permute-start | bytes 270344 | tf_op jit(solution)/shard_map/ppermute | solution.py:555
  59.8 1.2 %collective-permute-start.5 = (f32[176,128]{1,0:T(8,128)S(1)}, f32[176,128]{1,0:T(8,128)S(1)}, u32[]{:S(2)}, u32[]{:S(2)}) collective-permute-start(f32[176,128]{1,0:T(8,128)S(1)} %add.46), channel_id=1, source_target_pairs={{0,8},{1,9},{2,10},{3,11},{4,12},{5,13},{6,14},{7,15},{8,0},{9,1},... | collective-permute-start | bytes 270344 | tf_op jit(solution)/shard_map/ppermute | solution.py:555
  61.0 1.5 %collective-permute-start.4 = (f32[176,128]{1,0:T(8,128)S(1)}, f32[176,128]{1,0:T(8,128)S(1)}, u32[]{:S(2)}, u32[]{:S(2)}) collective-permute-start(f32[176,128]{1,0:T(8,128)S(1)} %add.46), channel_id=1, source_target_pairs={{0,4},{1,5},{2,6},{3,7},{4,0},{5,1},{6,2},{7,3},{8,12},{9,13},{10,... | collective-permute-start | bytes 270344 | tf_op jit(solution)/shard_map/ppermute | solution.py:555
  62.5 0.9 constant_dynamic-slice_fusion
  63.4 0.7 pad.4.kl_hbm
  64.1 6.5 %contract.1 = bf16[16,496,128]{2,1,0:T(8,128)(2,1)} custom-call(s32[165]{0:T(256)} %fusion.1.places, bf16[16,496,128]{2,1,0:T(8,128)(2,1)} %all-to-all-done.recv_hbm, f32[8,24,128]{2,1,0:T(8,128)} %pad.4.kl_hbm), custom_call_target="tpu_custom_call" | custom-call | flops 39649280 | bytes 7929856 | tf_op jit(solution)/shard_map/contract/pallas_call | solution.py:583
  70.6 0.0 collective-permute-done.6
  70.6 0.0 collective-permute-done.5
  70.6 0.0 collective-permute-done.4
  70.7 4.4 %all-to-all-start.1 = ((bf16[16,496,128]{2,1,0:T(8,128)(2,1)}), bf16[16,496,128]{2,1,0:T(8,128)(2,1)}, u32[]{:S(2)}, u32[]{:S(2)}) async-start(bf16[16,496,128]{2,1,0:T(8,128)(2,1)} %contract.1), calls=%async_computation.1 | async-start | bytes 4063232 | tf_op jit(solution)/shard_map/all_to_all | solution.py:510
  75.1 0.2 collective-permute-start.7
  75.4 1.1 %collective-permute-done.7 = f32[176,128]{1,0:T(8,128)S(1)} collective-permute-done((f32[176,128]{1,0:T(8,128)S(1)}, f32[176,128]{1,0:T(8,128)S(1)}, u32[]{:S(2)}, u32[]{:S(2)}) %collective-permute-start.7) | collective-permute-done | bytes 90144 | tf_op jit(solution)/shard_map/ppermute | solution.py:555
  76.5 1.9 %collective-permute-start.8 = (f32[32,128]{1,0:T(8,128)S(1)}, f32[32,128]{1,0:T(8,128)S(1)}, u32[]{:S(2)}, u32[]{:S(2)}) collective-permute-start(f32[32,128]{1,0:T(8,128)S(1)} %slice.32), channel_id=1, source_target_pairs={{0,16},{16,32},{32,48},{48,64},{64,80},{80,96},{96,112},{112,128},... | collective-permute-start | bytes 49160 | tf_op jit(solution)/shard_map/ppermute | solution.py:611
  78.5 6.0 %collective-permute-start.9 = (f32[32,128]{1,0:T(8,128)S(1)}, f32[32,128]{1,0:T(8,128)S(1)}, u32[]{:S(2)}, u32[]{:S(2)}) collective-permute-start(f32[32,128]{1,0:T(8,128)S(1)} %slice.33), channel_id=1, source_target_pairs={{16,0},{32,16},{48,32},{64,48},{80,64},{96,80},{112,96},{128,112},... | collective-permute-start | bytes 49160 | tf_op jit(solution)/shard_map/ppermute | solution.py:612
  84.5 0.7 pad_maximum_fusion.2.head_hbm
  85.2 0.0 collective-permute-done.8.head_low_hbm
  85.2 0.0 copy-start.3
  85.2 0.7 collective-permute-done.9.head_high_hbm
  85.9 0.0 copy-done.3
  85.9 0.0 copy-start.4
  85.9 0.6 copy-done.4
  86.5 5.3 %advection.1.base_c_hbm = f32[11,352,128]{2,1,0:T(8,128)} custom-call(f32[11,352,128]{2,1,0:T(8,128)} %bitcast.23, bf16[22,32,128]{2,1,0:T(8,128)(2,1)} %copy-done, bf16[22,32,128]{2,1,0:T(8,128)(2,1)} %copy-done.1, f32[11,352,128]{2,1,0:T(8,128)} %get-tuple-element.22.base_hbm, f32[352,128]{1,0:T(8,128)} %bitcast.28, ...), custom_call_target="tpu_custom_call" | custom-call | flops 9912320 | bytes 5947392 | tf_op jit(solution)/shard_map/advection/pallas_call | solution.py:613
  91.8 12.2 %all-to-all-done.1.recv_hbm = bf16[16,496,128]{2,1,0:T(8,128)(2,1)} async-done(((bf16[16,496,128]{2,1,0:T(8,128)(2,1)}), bf16[16,496,128]{2,1,0:T(8,128)(2,1)}, u32[]{:S(2)}, u32[]{:S(2)}) %all-to-all-start.1) | async-done | bytes 2031648 | tf_op jit(solution)/shard_map/all_to_all | solution.py:510
  104.0 4.5 %result.1 = (f32[11,352,128]{2,1,0:T(8,128)}, f32[11,352,128]{2,1,0:T(8,128)}) custom-call(bf16[16,496,128]{2,1,0:T(8,128)(2,1)} %all-to-all-done.1.recv_hbm, f32[11,352,128]{2,1,0:T(8,128)} %get-tuple-element.21.base_p_hbm, f32[11,352,128]{2,1,0:T(8,128)} %advection.1.base_c_hbm, f32[352,128]{1,0:T(8,128)} %bitcast.29), custom_call_target="tpu_custom_call" | custom-call | flops 3964928 | bytes 9912320 | tf_op jit(solution)/shard_map/result/pallas_call | solution.py:624
  (7 shorter events, 0.1 us)
Async XLA Ops:
  1.9 16.6 %collective-permute-start = (bf16[22,32,128]{2,1,0:T(8,128)(2,1)S(1)}, bf16[22,32,128]{2,1,0:T(8,128)(2,1)S(1)}, u32[]{:S(2)}, u32[]{:S(2)}) collective-permute-start(bf16[22,32,128]{2,1,0:T(8,128)(2,1)S(1)} %pad_maximum_fusion), channel_id=1, source_target_pairs={{0,16},{16,32},{32,48},{48,64},{64,80},{80,96},{96,112},{112,128},... | collective-permute-start | bytes 540680 | tf_op jit(solution)/shard_map/ppermute | solution.py:486
  5.8 12.8 %collective-permute-start.1 = (bf16[22,32,128]{2,1,0:T(8,128)(2,1)S(1)}, bf16[22,32,128]{2,1,0:T(8,128)(2,1)S(1)}, u32[]{:S(2)}, u32[]{:S(2)}) collective-permute-start(bf16[22,32,128]{2,1,0:T(8,128)(2,1)S(1)} %pad_maximum_fusion.1), channel_id=1, source_target_pairs={{16,0},{32,16},{48,32},{64,48},{80,64},{96,80},{112,96},{128,112},... | collective-permute-start | bytes 540680 | tf_op jit(solution)/shard_map/ppermute | solution.py:487
  18.5 0.7 copy-start
  18.6 0.7 copy-start.1
  21.9 6.5 %copy-start.2 = (s32[176,8]{0,1:T(8,128)S(1)}, s32[176,8]{0,1:T(8,128)}, u32[]{:S(2)}) copy-start(s32[176,8]{0,1:T(8,128)} %param.13) | copy-start | bytes 16900
  21.9 6.5 %copy-start.6 = (s32[8]{0:T(128)S(1)}, s32[8]{0:T(128)}, u32[]{:S(2)}) copy-start(s32[8]{0:T(128)} %constant.61) | copy-start | bytes 100
  21.9 36.4 %all-to-all-start = ((bf16[16,496,128]{2,1,0:T(8,128)(2,1)}), bf16[16,496,128]{2,1,0:T(8,128)(2,1)}, u32[]{:S(2)}, u32[]{:S(2)}) async-start(bf16[16,496,128]{2,1,0:T(8,128)(2,1)} %outer_images.1), calls=%async_computation | async-start | bytes 4063232 | tf_op jit(solution)/shard_map/all_to_all | solution.py:510
  28.6 5.0 %copy-start.5 = (s32[165]{0:T(256)S(1)}, s32[165]{0:T(256)}, u32[]{:S(2)}) copy-start(s32[165]{0:T(256)} %constant.62) | copy-start | bytes 1984
  33.6 1.3 %collective-permute-start.2 = (f32[176,128]{1,0:T(8,128)S(1)}, f32[176,128]{1,0:T(8,128)S(1)}, u32[]{:S(2)}, u32[]{:S(2)}) collective-permute-start(f32[176,128]{1,0:T(8,128)S(1)} %constant_dynamic-slice_fusion.1), channel_id=1, source_target_pairs={{0,1},{1,0},{2,3},{3,2},{4,5},{5,4},{6,7},{7,6},{8,9},{9,8},{10,11... | collective-permute-start | bytes 270344 | tf_op jit(solution)/shard_map/ppermute | solution.py:555
  35.8 22.6 %collective-permute-start.3 = (f32[176,128]{1,0:T(8,128)S(1)}, f32[176,128]{1,0:T(8,128)S(1)}, u32[]{:S(2)}, u32[]{:S(2)}) collective-permute-start(f32[176,128]{1,0:T(8,128)S(1)} %dynamic-slice_add_fusion), channel_id=1, source_target_pairs={{0,2},{1,3},{2,0},{3,1},{4,6},{5,7},{6,4},{7,5},{8,10},{9,11},{10,... | collective-permute-start | bytes 270344 | tf_op jit(solution)/shard_map/ppermute | solution.py:555
  58.3 12.3 %collective-permute-start.6 = (f32[176,128]{1,0:T(8,128)S(1)}, f32[176,128]{1,0:T(8,128)S(1)}, u32[]{:S(2)}, u32[]{:S(2)}) collective-permute-start(f32[176,128]{1,0:T(8,128)S(1)} %add.46), channel_id=1, source_target_pairs={{0,12},{1,13},{2,14},{3,15},{4,8},{5,9},{6,10},{7,11},{8,4},{9,5},... | collective-permute-start | bytes 270344 | tf_op jit(solution)/shard_map/ppermute | solution.py:555
  59.8 10.8 %collective-permute-start.5 = (f32[176,128]{1,0:T(8,128)S(1)}, f32[176,128]{1,0:T(8,128)S(1)}, u32[]{:S(2)}, u32[]{:S(2)}) collective-permute-start(f32[176,128]{1,0:T(8,128)S(1)} %add.46), channel_id=1, source_target_pairs={{0,8},{1,9},{2,10},{3,11},{4,12},{5,13},{6,14},{7,15},{8,0},{9,1},... | collective-permute-start | bytes 270344 | tf_op jit(solution)/shard_map/ppermute | solution.py:555
  61.0 9.6 %collective-permute-start.4 = (f32[176,128]{1,0:T(8,128)S(1)}, f32[176,128]{1,0:T(8,128)S(1)}, u32[]{:S(2)}, u32[]{:S(2)}) collective-permute-start(f32[176,128]{1,0:T(8,128)S(1)} %add.46), channel_id=1, source_target_pairs={{0,4},{1,5},{2,6},{3,7},{4,0},{5,1},{6,2},{7,3},{8,12},{9,13},{10,... | collective-permute-start | bytes 270344 | tf_op jit(solution)/shard_map/ppermute | solution.py:555
  70.7 33.3 %all-to-all-start.1 = ((bf16[16,496,128]{2,1,0:T(8,128)(2,1)}), bf16[16,496,128]{2,1,0:T(8,128)(2,1)}, u32[]{:S(2)}, u32[]{:S(2)}) async-start(bf16[16,496,128]{2,1,0:T(8,128)(2,1)} %contract.1), calls=%async_computation.1 | async-start | bytes 4063232 | tf_op jit(solution)/shard_map/all_to_all | solution.py:510
  75.1 1.4 %collective-permute-start.7 = (f32[176,128]{1,0:T(8,128)S(1)}, f32[176,128]{1,0:T(8,128)S(1)}, u32[]{:S(2)}, u32[]{:S(2)}) collective-permute-start(f32[176,128]{1,0:T(8,128)S(1)} %add_add_fusion), channel_id=1, source_target_pairs={{0,1},{1,0},{2,3},{3,2},{4,5},{5,4},{6,7},{7,6},{8,9},{9,8},{10,11... | collective-permute-start | bytes 270344 | tf_op jit(solution)/shard_map/ppermute | solution.py:555
  76.5 8.7 %collective-permute-start.8 = (f32[32,128]{1,0:T(8,128)S(1)}, f32[32,128]{1,0:T(8,128)S(1)}, u32[]{:S(2)}, u32[]{:S(2)}) collective-permute-start(f32[32,128]{1,0:T(8,128)S(1)} %slice.32), channel_id=1, source_target_pairs={{0,16},{16,32},{32,48},{48,64},{64,80},{80,96},{96,112},{112,128},... | collective-permute-start | bytes 49160 | tf_op jit(solution)/shard_map/ppermute | solution.py:611
  78.5 7.5 %collective-permute-start.9 = (f32[32,128]{1,0:T(8,128)S(1)}, f32[32,128]{1,0:T(8,128)S(1)}, u32[]{:S(2)}, u32[]{:S(2)}) collective-permute-start(f32[32,128]{1,0:T(8,128)S(1)} %slice.33), channel_id=1, source_target_pairs={{16,0},{32,16},{48,32},{64,48},{80,64},{96,80},{112,96},{128,112},... | collective-permute-start | bytes 49160 | tf_op jit(solution)/shard_map/ppermute | solution.py:612
  85.2 0.7 copy-start.3
  85.9 0.6 copy-start.4

commit v4 on v3

--- a/solution.py
+++ b/solution.py
@@ -558,7 +558,7 @@
     half = SLAB // 2
     kept = lax.dynamic_slice_in_dim(head, core * half, half, 0)
     kept = kept + partner(lax.dynamic_slice_in_dim(head, (1 - core) * half, half, 0), 1)
-    kept = kept + partner(kept, 2)
+    kept = (kept + partner(kept, 4)) + (partner(kept, 8) + partner(kept, 12))
 
     base_p, base_c = call(
         base_kernel,
@@ -571,14 +571,16 @@
         size * 24,
     )(own_rank, table, pressure, source, concentration, mean_cond, low, high)
 
-    recv, base_p, base_c, kept = lax.optimization_barrier((recv, base_p, base_c, kept))
-
     code = jnp.sum(table * POWERS.astype(np.int32)[:, None], axis=0)
     row = jnp.sum(jnp.where(code[None, :] == CODES[:, None], jnp.arange(ALL, dtype=jnp.int32)[None, :], 0), axis=1)
     places = row // MODES * STRIDE + row % MODES * SHARE
 
     own_kl = lax.dynamic_slice_in_dim(kl_cond, rank * SHARE, SHARE, 1)
     own_kl = jnp.pad(own_kl, ((0, 0), (0, FULL - SHARE), (0, 0)))
+
+    recv, base_p, base_c, kept, places, own_kl = lax.optimization_barrier(
+        (recv, base_p, base_c, kept, places, own_kl)
+    )
 
     back = call(
         contract_kernel,
@@ -600,7 +602,7 @@
         size * 80,
         size * 16,
     )(places, recv, own_kl)
-    kept = (kept + partner(kept, 4)) + (partner(kept, 8) + partner(kept, 12))
+    kept = kept + partner(kept, 2)
     back, kept = lax.optimization_barrier((back, kept))
     received = exchange(back)
 

time: 109 us -> 107 us (0.982)
  waiting for transfers between devices: 25.9 us -> 21.1 us
  Pallas kernels: 38.9 us -> 40.2 us
    ppermute x6, waiting for transfers between devices: 13 us -> 8.17 us  [partner(): return lax.ppermute(rows, 'mode', [(i, i ^ bits) for i in range(RANKS)])]
    pallas_call x1, Pallas kernels: 4.08 us -> 5.36 us  [local(): call(head_kernel, plane, [smem(), smem()] + [hbm()] * 6, [rows_vmem(SLAB...]
  transfers between devices with their start and end apart: 12 -> 12, of which waited for: 5 -> 5; matrix products, arithmetic and copies ran while one was open for 5% -> 5% of each run, Pallas kernels for 29% -> 31%
where the time goes in v4:
time: 107 us; the launch traced here: 106 us
  Pallas kernels  40.2 us (38%)
  starting transfers between devices  36.1 us (34%)
  waiting for transfers between devices  21.1 us (20%)
  local copies, waits for them, and re-layouts  5.09 us (5%)
  other arithmetic  2.56 us (2%)
    all_to_all x2, waiting for transfers between devices, exchange(): return lax.all_to_all(rows_of_ranks, 'mode', 0, 0, tiled=True)  12.2 us
    all_to_all x2, starting transfers between devices, exchange(): return lax.all_to_all(rows_of_ranks, 'mode', 0, 0, tiled=True)  11.1 us
    pallas_call x1, Pallas kernels, local(): call(base_kernel, (field, field), [smem(), smem()] + [hbm()] * 6, [rows_v...  9.05 us
    ppermute x6, waiting for transfers between devices, partner(): return lax.ppermute(rows, 'mode', [(i, i ^ bits) for i in range(RANKS)])  8.17 us
    ppermute x6, starting transfers between devices, partner(): return lax.ppermute(rows, 'mode', [(i, i ^ bits) for i in range(RANKS)])  7.47 us
    pallas_call x1, Pallas kernels, local(): call(inner_kernel, (message(SENT), jax.ShapeDtypeStruct((4, SENT, CZ), F3...  6.91 us
    pallas_call x1, Pallas kernels, local(): call(contract_kernel, message(SENT), [smem()] + [hbm()] * 2, [message_vme...  6.51 us
    ppermute x1, starting transfers between devices, local(): head_high = lax.ppermute(head[:CY], 'space', down)  6.03 us
  transfers between devices with their start and end apart: 12, of which 5 were waited for; matrix products, arithmetic and copies ran while one was open for 5% of the time, Pallas kernels for 31%

profile of v4, /device:TPU:2, one launch (start us, length us, event | category | flops | bytes accessed | tf_op | source)
XLA Modules:
  0.0 106.0 jit_solution(6146889592530261900)
XLA Ops:
  0.6 1.3 %slice_bitcast_fusion = (bf16[11,32,128]{2,1,0:T(8,128)(2,1)S(1)}, bf16[11,32,128]{2,1,0:T(8,128)(2,1)S(1)}, bf16[11,32,128]{2,1,0:T(8,128)(2,1)S(1)}, bf16[11,32,128]{2,1,0:T(8,128)(2,1)S(1)}) fusion(f32[11,11,32,128]{3,2,1,0:T(8,128)} %param.8, f32[11,11,32,128]{3,2,1,0:T(8,128)} %param.10), kind=kLoop, calls=%fused_computation.6 | loop fusion | bytes 720896 | tf_op jit(solution)/shard_map/squeeze | solution.py:485
  1.9 3.8 %collective-permute-start = (bf16[22,32,128]{2,1,0:T(8,128)(2,1)S(1)}, bf16[22,32,128]{2,1,0:T(8,128)(2,1)S(1)}, u32[]{:S(2)}, u32[]{:S(2)}) collective-permute-start(bf16[22,32,128]{2,1,0:T(8,128)(2,1)S(1)} %pad_maximum_fusion), channel_id=1, source_target_pairs={{0,16},{16,32},{32,48},{48,64},{64,80},{80,96},{96,112},{112,128},... | collective-permute-start | bytes 540680 | tf_op jit(solution)/shard_map/ppermute | solution.py:486
  5.8 5.8 %collective-permute-start.1 = (bf16[22,32,128]{2,1,0:T(8,128)(2,1)S(1)}, bf16[22,32,128]{2,1,0:T(8,128)(2,1)S(1)}, u32[]{:S(2)}, u32[]{:S(2)}) collective-permute-start(bf16[22,32,128]{2,1,0:T(8,128)(2,1)S(1)} %pad_maximum_fusion.1), channel_id=1, source_target_pairs={{16,0},{32,16},{48,32},{64,48},{80,64},{96,80},{112,96},{128,112},... | collective-permute-start | bytes 540680 | tf_op jit(solution)/shard_map/ppermute | solution.py:487
  11.6 6.9 %inner_images.1 = (bf16[16,496,128]{2,1,0:T(8,128)(2,1)}, f32[4,496,128]{2,1,0:T(8,128)}) custom-call(f32[11,352,128]{2,1,0:T(8,128)} %bitcast.18, f32[11,352,128]{2,1,0:T(8,128)} %bitcast.21), custom_call_target="tpu_custom_call" | custom-call | flops 9912320 | bytes 6938624 | tf_op jit(solution)/shard_map/inner_images/pallas_call | solution.py:512
  18.5 0.0 collective-permute-done.low_hbm
  18.5 0.0 copy-start
  18.6 0.0 collective-permute-done.1.high_hbm
  18.6 0.0 copy-start.1
  18.6 0.6 copy-done
  19.2 0.1 copy-done.1
  19.3 2.6 %outer_images.1 = bf16[16,496,128]{2,1,0:T(8,128)(2,1)} custom-call(f32[4,496,128]{2,1,0:T(8,128)} %get-tuple-element.16.part_hbm, bf16[22,32,128]{2,1,0:T(8,128)(2,1)} %copy-done, bf16[22,32,128]{2,1,0:T(8,128)(2,1)} %copy-done.1, bf16[16,496,128]{2,1,0:T(8,128)(2,1)} %get-tuple-element.17.send_in), custom_call_target="tpu_custom_call", output_to_operand_aliasing={{}: (3, {})} | custom-call | flops 495616 | bytes 495616 | tf_op jit(solution)/shard_map/outer_images/pallas_call | solution.py:522
  21.9 0.0 copy-start.2
  21.9 0.0 copy-start.6
  21.9 0.0 copy-start.5
  21.9 6.6 %all-to-all-start = ((bf16[16,496,128]{2,1,0:T(8,128)(2,1)}), bf16[16,496,128]{2,1,0:T(8,128)(2,1)}, u32[]{:S(2)}, u32[]{:S(2)}) async-start(bf16[16,496,128]{2,1,0:T(8,128)(2,1)} %outer_images.1), calls=%async_computation | async-start | bytes 4063232 | tf_op jit(solution)/shard_map/all_to_all | solution.py:510
  28.6 0.0 copy-done.2
  28.6 0.0 copy-done.6
  28.6 0.1 multiply_reduce_fusion
  28.7 0.0 copy-done.5
  28.7 0.2 select_reduce_fusion
  28.9 5.4 %head_part.1 = f32[352,128]{1,0:T(8,128)} custom-call(s32[1]{0:T(128)} %bitcast.6.rank_ref, s32[8,176]{1,0:T(8,128)} %bitcast.32, f32[11,352,128]{2,1,0:T(8,128)} %bitcast.19, f32[11,352,128]{2,1,0:T(8,128)} %bitcast.24, f32[352,128]{1,0:T(8,128)} %bitcast.26, f32[8,352,128]{2,1,0:T(8,128)} %bitcast.30, bf16[22,32,128]{2,1,0:T(8,128)(2,1)} %copy-done, ...), custom_call_target="tpu_custom_call" | custom-call | flops 495616 | bytes 495616 | tf_op jit(solution)/shard_map/head_part/pallas_call | solution.py:543
  34.3 0.9 constant_dynamic-slice_fusion.1
  35.2 0.0 collective-permute-start.2
  35.2 0.6 fusion.1.places
  35.8 0.7 collective-permute-done.2
  36.5 0.9 dynamic-slice_add_fusion
  37.4 3.2 %collective-permute-start.5 = (f32[176,128]{1,0:T(8,128)S(1)}, f32[176,128]{1,0:T(8,128)S(1)}, u32[]{:S(2)}, u32[]{:S(2)}) collective-permute-start(f32[176,128]{1,0:T(8,128)S(1)} %dynamic-slice_add_fusion), channel_id=1, source_target_pairs={{0,12},{1,13},{2,14},{3,15},{4,8},{5,9},{6,10},{7,11},{8,4},{9,5},... | collective-permute-start | bytes 270344 | tf_op jit(solution)/shard_map/ppermute | solution.py:555
  40.5 0.0 collective-permute-start.4
  40.5 1.0 collective-permute-start.3
  41.5 0.9 constant_dynamic-slice_fusion
  42.5 0.7 pad.4.kl_hbm
  43.1 9.0 %base.1 = (f32[11,352,128]{2,1,0:T(8,128)}, f32[11,352,128]{2,1,0:T(8,128)}) custom-call(s32[1]{0:T(128)} %bitcast.6.rank_ref, s32[8,176]{1,0:T(8,128)} %bitcast.33, f32[11,352,128]{2,1,0:T(8,128)} %bitcast.20, f32[11,352,128]{2,1,0:T(8,128)} %bitcast.25, f32[11,352,128]{2,1,0:T(8,128)} %bitcast.22, f32[352,128]{1,0:T(8,128)} %bitcast.27, ...), custom_call_target="tpu_custom_call" | custom-call | flops 29736960 | bytes 11894784 | tf_op jit(solution)/shard_map/base/pallas_call | solution.py:563
  52.2 6.3 %collective-permute-done.5 = f32[176,128]{1,0:T(8,128)S(1)} collective-permute-done((f32[176,128]{1,0:T(8,128)S(1)}, f32[176,128]{1,0:T(8,128)S(1)}, u32[]{:S(2)}, u32[]{:S(2)}) %collective-permute-start.5) | collective-permute-done | bytes 90144 | tf_op jit(solution)/shard_map/ppermute | solution.py:555
  58.5 0.0 collective-permute-done.4
  58.5 0.0 collective-permute-done.3
  58.5 0.0 all-to-all-done.recv_hbm
  58.5 3.1 %collective-permute-start.6 = (f32[176,128]{1,0:T(8,128)S(1)}, f32[176,128]{1,0:T(8,128)S(1)}, u32[]{:S(2)}, u32[]{:S(2)}) collective-permute-start(f32[176,128]{1,0:T(8,128)S(1)} %add_add_fusion), channel_id=1, source_target_pairs={{0,2},{1,3},{2,0},{3,1},{4,6},{5,7},{6,4},{7,5},{8,10},{9,11},{10,... | collective-permute-start | bytes 270344 | tf_op jit(solution)/shard_map/ppermute | solution.py:555
  61.6 6.5 %contract.1 = bf16[16,496,128]{2,1,0:T(8,128)(2,1)} custom-call(s32[165]{0:T(256)} %fusion.1.places, bf16[16,496,128]{2,1,0:T(8,128)(2,1)} %all-to-all-done.recv_hbm, f32[8,24,128]{2,1,0:T(8,128)} %pad.4.kl_hbm), custom_call_target="tpu_custom_call" | custom-call | flops 39649280 | bytes 7929856 | tf_op jit(solution)/shard_map/contract/pallas_call | solution.py:585
  68.1 0.0 collective-permute-done.6
  68.2 4.4 %all-to-all-start.1 = ((bf16[16,496,128]{2,1,0:T(8,128)(2,1)}), bf16[16,496,128]{2,1,0:T(8,128)(2,1)}, u32[]{:S(2)}, u32[]{:S(2)}) async-start(bf16[16,496,128]{2,1,0:T(8,128)(2,1)} %contract.1), calls=%async_computation.1 | async-start | bytes 4063232 | tf_op jit(solution)/shard_map/all_to_all | solution.py:510
  72.6 0.2 collective-permute-start.7
  72.8 1.1 %collective-permute-done.7 = f32[176,128]{1,0:T(8,128)S(1)} collective-permute-done((f32[176,128]{1,0:T(8,128)S(1)}, f32[176,128]{1,0:T(8,128)S(1)}, u32[]{:S(2)}, u32[]{:S(2)}) %collective-permute-start.7) | collective-permute-done | bytes 90144 | tf_op jit(solution)/shard_map/ppermute | solution.py:555
  74.0 1.9 %collective-permute-start.8 = (f32[32,128]{1,0:T(8,128)S(1)}, f32[32,128]{1,0:T(8,128)S(1)}, u32[]{:S(2)}, u32[]{:S(2)}) collective-permute-start(f32[32,128]{1,0:T(8,128)S(1)} %slice.32), channel_id=1, source_target_pairs={{0,16},{16,32},{32,48},{48,64},{64,80},{80,96},{96,112},{112,128},... | collective-permute-start | bytes 49160 | tf_op jit(solution)/shard_map/ppermute | solution.py:613
  75.9 6.0 %collective-permute-start.9 = (f32[32,128]{1,0:T(8,128)S(1)}, f32[32,128]{1,0:T(8,128)S(1)}, u32[]{:S(2)}, u32[]{:S(2)}) collective-permute-start(f32[32,128]{1,0:T(8,128)S(1)} %slice.33), channel_id=1, source_target_pairs={{16,0},{32,16},{48,32},{64,48},{80,64},{96,80},{112,96},{128,112},... | collective-permute-start | bytes 49160 | tf_op jit(solution)/shard_map/ppermute | solution.py:614
  82.0 0.7 pad_maximum_fusion.2.head_hbm
  82.7 0.0 collective-permute-done.8.head_low_hbm
  82.7 0.0 copy-start.3
  82.7 0.7 collective-permute-done.9.head_high_hbm
  83.4 0.0 copy-done.3
  83.4 0.0 copy-start.4
  83.4 0.6 copy-done.4
  84.0 5.3 %advection.1.base_c_hbm = f32[11,352,128]{2,1,0:T(8,128)} custom-call(f32[11,352,128]{2,1,0:T(8,128)} %bitcast.23, bf16[22,32,128]{2,1,0:T(8,128)(2,1)} %copy-done, bf16[22,32,128]{2,1,0:T(8,128)(2,1)} %copy-done.1, f32[11,352,128]{2,1,0:T(8,128)} %get-tuple-element.26.base_hbm, f32[352,128]{1,0:T(8,128)} %bitcast.28, ...), custom_call_target="tpu_custom_call" | custom-call | flops 9912320 | bytes 5947392 | tf_op jit(solution)/shard_map/advection/pallas_call | solution.py:615
  89.3 12.2 %all-to-all-done.1.recv_hbm = bf16[16,496,128]{2,1,0:T(8,128)(2,1)} async-done(((bf16[16,496,128]{2,1,0:T(8,128)(2,1)}), bf16[16,496,128]{2,1,0:T(8,128)(2,1)}, u32[]{:S(2)}, u32[]{:S(2)}) %all-to-all-start.1) | async-done | bytes 2031648 | tf_op jit(solution)/shard_map/all_to_all | solution.py:510
  101.5 4.5 %result.1 = (f32[11,352,128]{2,1,0:T(8,128)}, f32[11,352,128]{2,1,0:T(8,128)}) custom-call(bf16[16,496,128]{2,1,0:T(8,128)(2,1)} %all-to-all-done.1.recv_hbm, f32[11,352,128]{2,1,0:T(8,128)} %get-tuple-element.25.base_p_hbm, f32[11,352,128]{2,1,0:T(8,128)} %advection.1.base_c_hbm, f32[352,128]{1,0:T(8,128)} %bitcast.29), custom_call_target="tpu_custom_call" | custom-call | flops 3964928 | bytes 9912320 | tf_op jit(solution)/shard_map/result/pallas_call | solution.py:626
  (7 shorter events, 0.1 us)
Async XLA Ops:
  1.9 16.6 %collective-permute-start = (bf16[22,32,128]{2,1,0:T(8,128)(2,1)S(1)}, bf16[22,32,128]{2,1,0:T(8,128)(2,1)S(1)}, u32[]{:S(2)}, u32[]{:S(2)}) collective-permute-start(bf16[22,32,128]{2,1,0:T(8,128)(2,1)S(1)} %pad_maximum_fusion), channel_id=1, source_target_pairs={{0,16},{16,32},{32,48},{48,64},{64,80},{80,96},{96,112},{112,128},... | collective-permute-start | bytes 540680 | tf_op jit(solution)/shard_map/ppermute | solution.py:486
  5.8 12.8 %collective-permute-start.1 = (bf16[22,32,128]{2,1,0:T(8,128)(2,1)S(1)}, bf16[22,32,128]{2,1,0:T(8,128)(2,1)S(1)}, u32[]{:S(2)}, u32[]{:S(2)}) collective-permute-start(bf16[22,32,128]{2,1,0:T(8,128)(2,1)S(1)} %pad_maximum_fusion.1), channel_id=1, source_target_pairs={{16,0},{32,16},{48,32},{64,48},{80,64},{96,80},{112,96},{128,112},... | collective-permute-start | bytes 540680 | tf_op jit(solution)/shard_map/ppermute | solution.py:487
  18.5 0.7 copy-start
  18.6 0.7 copy-start.1
  21.9 6.7 %copy-start.2 = (s32[176,8]{0,1:T(8,128)S(1)}, s32[176,8]{0,1:T(8,128)}, u32[]{:S(2)}) copy-start(s32[176,8]{0,1:T(8,128)} %param.13) | copy-start | bytes 16900
  21.9 6.7 %copy-start.6 = (s32[8]{0:T(128)S(1)}, s32[8]{0:T(128)}, u32[]{:S(2)}) copy-start(s32[8]{0:T(128)} %constant.61) | copy-start | bytes 100
  21.9 6.8 %copy-start.5 = (s32[165]{0:T(256)S(1)}, s32[165]{0:T(256)}, u32[]{:S(2)}) copy-start(s32[165]{0:T(256)} %constant.62) | copy-start | bytes 1984
  21.9 36.6 %all-to-all-start = ((bf16[16,496,128]{2,1,0:T(8,128)(2,1)}), bf16[16,496,128]{2,1,0:T(8,128)(2,1)}, u32[]{:S(2)}, u32[]{:S(2)}) async-start(bf16[16,496,128]{2,1,0:T(8,128)(2,1)} %outer_images.1), calls=%async_computation | async-start | bytes 4063232 | tf_op jit(solution)/shard_map/all_to_all | solution.py:510
  35.2 1.3 %collective-permute-start.2 = (f32[176,128]{1,0:T(8,128)S(1)}, f32[176,128]{1,0:T(8,128)S(1)}, u32[]{:S(2)}, u32[]{:S(2)}) collective-permute-start(f32[176,128]{1,0:T(8,128)S(1)} %constant_dynamic-slice_fusion.1), channel_id=1, source_target_pairs={{0,1},{1,0},{2,3},{3,2},{4,5},{5,4},{6,7},{7,6},{8,9},{9,8},{10,11... | collective-permute-start | bytes 270344 | tf_op jit(solution)/shard_map/ppermute | solution.py:555
  37.4 21.1 %collective-permute-start.5 = (f32[176,128]{1,0:T(8,128)S(1)}, f32[176,128]{1,0:T(8,128)S(1)}, u32[]{:S(2)}, u32[]{:S(2)}) collective-permute-start(f32[176,128]{1,0:T(8,128)S(1)} %dynamic-slice_add_fusion), channel_id=1, source_target_pairs={{0,12},{1,13},{2,14},{3,15},{4,8},{5,9},{6,10},{7,11},{8,4},{9,5},... | collective-permute-start | bytes 270344 | tf_op jit(solution)/shard_map/ppermute | solution.py:555
  40.5 18.0 %collective-permute-start.4 = (f32[176,128]{1,0:T(8,128)S(1)}, f32[176,128]{1,0:T(8,128)S(1)}, u32[]{:S(2)}, u32[]{:S(2)}) collective-permute-start(f32[176,128]{1,0:T(8,128)S(1)} %dynamic-slice_add_fusion), channel_id=1, source_target_pairs={{0,8},{1,9},{2,10},{3,11},{4,12},{5,13},{6,14},{7,15},{8,0},{9,1},... | collective-permute-start | bytes 270344 | tf_op jit(solution)/shard_map/ppermute | solution.py:555
  40.5 18.0 %collective-permute-start.3 = (f32[176,128]{1,0:T(8,128)S(1)}, f32[176,128]{1,0:T(8,128)S(1)}, u32[]{:S(2)}, u32[]{:S(2)}) collective-permute-start(f32[176,128]{1,0:T(8,128)S(1)} %dynamic-slice_add_fusion), channel_id=1, source_target_pairs={{0,4},{1,5},{2,6},{3,7},{4,0},{5,1},{6,2},{7,3},{8,12},{9,13},{10,... | collective-permute-start | bytes 270344 | tf_op jit(solution)/shard_map/ppermute | solution.py:555
  58.5 9.6 %collective-permute-start.6 = (f32[176,128]{1,0:T(8,128)S(1)}, f32[176,128]{1,0:T(8,128)S(1)}, u32[]{:S(2)}, u32[]{:S(2)}) collective-permute-start(f32[176,128]{1,0:T(8,128)S(1)} %add_add_fusion), channel_id=1, source_target_pairs={{0,2},{1,3},{2,0},{3,1},{4,6},{5,7},{6,4},{7,5},{8,10},{9,11},{10,... | collective-permute-start | bytes 270344 | tf_op jit(solution)/shard_map/ppermute | solution.py:555
  68.2 33.3 %all-to-all-start.1 = ((bf16[16,496,128]{2,1,0:T(8,128)(2,1)}), bf16[16,496,128]{2,1,0:T(8,128)(2,1)}, u32[]{:S(2)}, u32[]{:S(2)}) async-start(bf16[16,496,128]{2,1,0:T(8,128)(2,1)} %contract.1), calls=%async_computation.1 | async-start | bytes 4063232 | tf_op jit(solution)/shard_map/all_to_all | solution.py:510
  72.6 1.4 %collective-permute-start.7 = (f32[176,128]{1,0:T(8,128)S(1)}, f32[176,128]{1,0:T(8,128)S(1)}, u32[]{:S(2)}, u32[]{:S(2)}) collective-permute-start(f32[176,128]{1,0:T(8,128)S(1)} %add.50), channel_id=1, source_target_pairs={{0,1},{1,0},{2,3},{3,2},{4,5},{5,4},{6,7},{7,6},{8,9},{9,8},{10,11... | collective-permute-start | bytes 270344 | tf_op jit(solution)/shard_map/ppermute | solution.py:555
  74.0 8.7 %collective-permute-start.8 = (f32[32,128]{1,0:T(8,128)S(1)}, f32[32,128]{1,0:T(8,128)S(1)}, u32[]{:S(2)}, u32[]{:S(2)}) collective-permute-start(f32[32,128]{1,0:T(8,128)S(1)} %slice.32), channel_id=1, source_target_pairs={{0,16},{16,32},{32,48},{48,64},{64,80},{80,96},{96,112},{112,128},... | collective-permute-start | bytes 49160 | tf_op jit(solution)/shard_map/ppermute | solution.py:613
  75.9 7.5 %collective-permute-start.9 = (f32[32,128]{1,0:T(8,128)S(1)}, f32[32,128]{1,0:T(8,128)S(1)}, u32[]{:S(2)}, u32[]{:S(2)}) collective-permute-start(f32[32,128]{1,0:T(8,128)S(1)} %slice.33), channel_id=1, source_target_pairs={{16,0},{32,16},{48,32},{64,48},{80,64},{96,80},{112,96},{128,112},... | collective-permute-start | bytes 49160 | tf_op jit(solution)/shard_map/ppermute | solution.py:614
  82.7 0.7 copy-start.3
  83.4 0.6 copy-start.4

commit v5 on v4

--- a/solution.py
+++ b/solution.py
@@ -138,8 +138,15 @@
         target[pl.ds(to + part, 8), :] = source[pl.ds(start + part, 8), :]
 
 
+HALVES = ((0, BODY // 16), (BODY // 16, SENT // 16))
+
+
+def half_rows(half):
+    return pl.ds(half[0] * 16, (half[1] - half[0]) * 16)
+
+
 def pack_rank(scratch, start, out_ref, slot, blocks):
-    for block in range(blocks):
+    for block in blocks:
         out_ref[slot, pl.ds(block * 16, 16), :] = scratch[pl.ds(start + block * 16, 16), :].astype(BF16)
 
 
@@ -167,6 +174,10 @@
     for rank in range(RANKS):
         scratch[pl.ds(rank * STRIDE + 2 * BODY, SENT - 2 * BODY), :] = jnp.zeros((SENT - 2 * BODY, CZ), F32)
     masks = edge_masks()
+
+    def send(index, rank):
+        rows = half_rows(HALVES[index])
+        return pltpu.make_async_copy(strip.at[rank, rows, :], send_hbm.at[rank, rows, :], send_sems.at[index, rank])
 
     for index in range(2):
 
@@ -178,22 +189,21 @@
                 copy_share(scratch, rank * STRIDE + (index * MODES + m) * SHARE, image, rank * SHARE)
 
         loop(0, MODES, one_mode)
+
+        def go(rank):
+            pack_rank(scratch, pl.multiple_of(rank * STRIDE, 8), strip, rank, range(*HALVES[index]))
+            send(index, rank).start()
+
+        loop(2, RANKS - 2, go)
     parts = start_all(
         part_sems,
         [(scratch.at[pl.ds(rank * STRIDE, SENT), :], part_hbm.at[i]) for i, rank in enumerate(EDGE_RANKS)],
     )
 
-    def send(rank):
-        return pltpu.make_async_copy(strip.at[rank], send_hbm.at[rank], send_sems.at[rank])
-
-    def go(rank):
-        pack_rank(scratch, pl.multiple_of(rank * STRIDE, 8), strip, rank, SENT // 16)
-        send(rank).start()
-
-    loop(2, RANKS - 2, go)
     for copy in parts:
         copy.wait()
-    loop(2, RANKS - 2, lambda rank: send(rank).wait())
+    for index in range(2):
+        loop(2, RANKS - 2, lambda rank: send(index, rank).wait())
 
 
 def outer_kernel(part_hbm, low_hbm, high_hbm, send_in, send_hbm, part, low, high, halo, strip, sems, send_sems):
@@ -217,7 +227,7 @@
     loop(0, 2 * MODES, spread)
     sends = []
     for i, rank in enumerate(EDGE_RANKS):
-        pack_rank(part, i * STRIDE, strip, i, SENT // 16)
+        pack_rank(part, i * STRIDE, strip, i, range(SENT // 16))
         send = pltpu.make_async_copy(strip.at[i], send_hbm.at[rank], send_sems.at[i])
         send.start()
         sends.append(send)
@@ -345,6 +355,10 @@
 
     loop(0, RANKS, spread)
 
+    def send(index, rank):
+        rows = half_rows(HALVES[index])
+        return pltpu.make_async_copy(strip.at[rank, rows, :], send_hbm.at[rank, rows, :], send_sems.at[index, rank])
+
     def one_field(index):
         for i in range(VALID):
             copy_share(ordered, i * FULL, images, places[i] + index * BODY)
@@ -358,17 +372,16 @@
                     total = term if total is None else total + term
                 outs[pl.ds(places[i] + index * BODY + part, count), :] = total[:count]
 
-    loop(0, 2, one_field)
-
-    def send(rank):
-        return pltpu.make_async_copy(strip.at[rank], send_hbm.at[rank], send_sems.at[rank])
-
-    def go(rank):
-        pack_rank(outs, pl.multiple_of(rank * STRIDE, 8), strip, rank, SENT // 16)
-        send(rank).start()
-
-    loop(0, RANKS, go)
-    loop(0, RANKS, lambda rank: send(rank).wait())
+        def go(rank):
+            pack_rank(outs, pl.multiple_of(rank * STRIDE, 8), strip, rank, range(*HALVES[index]))
+            send(index, rank).start()
+
+        loop(0, RANKS, go)
+
+    for index in range(2):
+        one_field(index)
+    for index in range(2):
+        loop(0, RANKS, lambda rank: send(index, rank).wait())
 
 
 def result_kernel(
@@ -514,7 +527,7 @@
         (message(SENT), jax.ShapeDtypeStruct((4, SENT, CZ), F32)),
         [hbm()] * 2,
         [rows_vmem(2 * MODES * SPACED + 2 * PAD), rows_vmem(SLAB + PAD), rows_vmem(RANKS * STRIDE), message_vmem(SENT)]
-        + [dma((2, MODES)), dma((RANKS,)), dma((4,))],
+        + [dma((2, MODES)), dma((2, RANKS)), dma((4,))],
         "inner_images",
         size * 20,
         size * 14,
@@ -596,7 +609,7 @@
             message_vmem(SENT),
             dma((RANKS,)),
             dma(()),
-            dma((RANKS,)),
+            dma((2, RANKS)),
         ],
         "contract",
         size * 80,

time: 107 us -> 106 us (level)
  Pallas kernels: 40.2 us -> 36.9 us
  starting transfers between devices: 36.1 us -> 39 us
    ppermute x6, starting transfers between devices: 7.47 us -> 10.3 us  [partner(): return lax.ppermute(rows, 'mode', [(i, i ^ bits) for i in range(RANKS)])]
    pallas_call x1, Pallas kernels: 5.36 us -> 2.8 us  [local(): call(head_kernel, plane, [smem(), smem()] + [hbm()] * 6, [rows_vmem(SLAB...]
  transfers between devices with their start and end apart: 12 -> 12, of which waited for: 5 -> 5; matrix products, arithmetic and copies ran while one was open for 5% -> 5% of each run, Pallas kernels for 31% -> 28%
where the time goes in v5:
time: 106 us; the launch traced here: 105 us
  starting transfers between devices  39 us (37%)
  Pallas kernels  36.9 us (35%)
  waiting for transfers between devices  20.8 us (20%)
  local copies, waits for them, and re-layouts  5.09 us (5%)
  other arithmetic  2.55 us (2%)
    all_to_all x2, waiting for transfers between devices, exchange(): return lax.all_to_all(rows_of_ranks, 'mode', 0, 0, tiled=True)  12.2 us
    all_to_all x2, starting transfers between devices, exchange(): return lax.all_to_all(rows_of_ranks, 'mode', 0, 0, tiled=True)  11.1 us
    ppermute x6, starting transfers between devices, partner(): return lax.ppermute(rows, 'mode', [(i, i ^ bits) for i in range(RANKS)])  10.3 us
    pallas_call x1, Pallas kernels, local(): call(base_kernel, (field, field), [smem(), smem()] + [hbm()] * 6, [rows_v...  9.05 us
    ppermute x6, waiting for transfers between devices, partner(): return lax.ppermute(rows, 'mode', [(i, i ^ bits) for i in range(RANKS)])  7.89 us
    pallas_call x1, Pallas kernels, local(): call(inner_kernel, (message(SENT), jax.ShapeDtypeStruct((4, SENT, CZ), F3...  7.04 us
    ppermute x1, starting transfers between devices, local(): head_high = lax.ppermute(head[:CY], 'space', down)  6.03 us
    ppermute x1, starting transfers between devices, local(): high = lax.ppermute(first, 'space', down)  5.83 us
  transfers between devices with their start and end apart: 12, of which 5 were waited for; matrix products, arithmetic and copies ran while one was open for 5% of the time, Pallas kernels for 28%

profile of v5, /device:TPU:2, one launch (start us, length us, event | category | flops | bytes accessed | tf_op | source)
XLA Modules:
  0.0 105.2 jit_solution(15457056558632562025)
XLA Ops:
  0.6 1.3 %slice_bitcast_fusion = (bf16[11,32,128]{2,1,0:T(8,128)(2,1)S(1)}, bf16[11,32,128]{2,1,0:T(8,128)(2,1)S(1)}, bf16[11,32,128]{2,1,0:T(8,128)(2,1)S(1)}, bf16[11,32,128]{2,1,0:T(8,128)(2,1)S(1)}) fusion(f32[11,11,32,128]{3,2,1,0:T(8,128)} %param.8, f32[11,11,32,128]{3,2,1,0:T(8,128)} %param.10), kind=kLoop, calls=%fused_computation.6 | loop fusion | bytes 720896 | tf_op jit(solution)/shard_map/squeeze | solution.py:498
  1.9 3.8 %collective-permute-start = (bf16[22,32,128]{2,1,0:T(8,128)(2,1)S(1)}, bf16[22,32,128]{2,1,0:T(8,128)(2,1)S(1)}, u32[]{:S(2)}, u32[]{:S(2)}) collective-permute-start(bf16[22,32,128]{2,1,0:T(8,128)(2,1)S(1)} %pad_maximum_fusion), channel_id=1, source_target_pairs={{0,16},{16,32},{32,48},{48,64},{64,80},{80,96},{96,112},{112,128},... | collective-permute-start | bytes 540680 | tf_op jit(solution)/shard_map/ppermute | solution.py:499
  5.8 5.8 %collective-permute-start.1 = (bf16[22,32,128]{2,1,0:T(8,128)(2,1)S(1)}, bf16[22,32,128]{2,1,0:T(8,128)(2,1)S(1)}, u32[]{:S(2)}, u32[]{:S(2)}) collective-permute-start(bf16[22,32,128]{2,1,0:T(8,128)(2,1)S(1)} %pad_maximum_fusion.1), channel_id=1, source_target_pairs={{16,0},{32,16},{48,32},{64,48},{80,64},{96,80},{112,96},{128,112},... | collective-permute-start | bytes 540680 | tf_op jit(solution)/shard_map/ppermute | solution.py:500
  11.6 7.0 %inner_images.1 = (bf16[16,496,128]{2,1,0:T(8,128)(2,1)}, f32[4,496,128]{2,1,0:T(8,128)}) custom-call(f32[11,352,128]{2,1,0:T(8,128)} %bitcast.18, f32[11,352,128]{2,1,0:T(8,128)} %bitcast.21), custom_call_target="tpu_custom_call" | custom-call | flops 9912320 | bytes 6938624 | tf_op jit(solution)/shard_map/inner_images/pallas_call | solution.py:525
  18.7 0.0 collective-permute-done.low_hbm
  18.7 0.0 copy-start
  18.7 0.0 collective-permute-done.1.high_hbm
  18.7 0.0 copy-start.1
  18.7 0.6 copy-done
  19.4 0.1 copy-done.1
  19.4 2.6 %outer_images.1 = bf16[16,496,128]{2,1,0:T(8,128)(2,1)} custom-call(f32[4,496,128]{2,1,0:T(8,128)} %get-tuple-element.16.part_hbm, bf16[22,32,128]{2,1,0:T(8,128)(2,1)} %copy-done, bf16[22,32,128]{2,1,0:T(8,128)(2,1)} %copy-done.1, bf16[16,496,128]{2,1,0:T(8,128)(2,1)} %get-tuple-element.17.send_in), custom_call_target="tpu_custom_call", output_to_operand_aliasing={{}: (3, {})} | custom-call | flops 495616 | bytes 495616 | tf_op jit(solution)/shard_map/outer_images/pallas_call | solution.py:535
  22.0 0.0 copy-start.2
  22.0 0.0 copy-start.6
  22.1 0.0 copy-start.5
  22.1 6.6 %all-to-all-start = ((bf16[16,496,128]{2,1,0:T(8,128)(2,1)}), bf16[16,496,128]{2,1,0:T(8,128)(2,1)}, u32[]{:S(2)}, u32[]{:S(2)}) async-start(bf16[16,496,128]{2,1,0:T(8,128)(2,1)} %outer_images.1), calls=%async_computation | async-start | bytes 4063232 | tf_op jit(solution)/shard_map/all_to_all | solution.py:523
  28.7 0.0 copy-done.2
  28.7 0.0 copy-done.6
  28.7 0.1 multiply_reduce_fusion
  28.8 0.0 copy-done.5
  28.8 0.2 select_reduce_fusion
  29.0 2.8 %head_part.1 = f32[352,128]{1,0:T(8,128)} custom-call(s32[1]{0:T(128)} %bitcast.6.rank_ref, s32[8,176]{1,0:T(8,128)} %bitcast.32, f32[11,352,128]{2,1,0:T(8,128)} %bitcast.19, f32[11,352,128]{2,1,0:T(8,128)} %bitcast.24, f32[352,128]{1,0:T(8,128)} %bitcast.26, f32[8,352,128]{2,1,0:T(8,128)} %bitcast.30, bf16[22,32,128]{2,1,0:T(8,128)(2,1)} %copy-done, ...), custom_call_target="tpu_custom_call" | custom-call | flops 495616 | bytes 495616 | tf_op jit(solution)/shard_map/head_part/pallas_call | solution.py:556
  31.8 0.9 constant_dynamic-slice_fusion.1
  32.7 0.3 collective-permute-start.2
  33.1 0.6 fusion.1.places
  33.7 0.4 collective-permute-done.2
  34.0 0.9 dynamic-slice_add_fusion
  34.9 5.7 %collective-permute-start.5 = (f32[176,128]{1,0:T(8,128)S(1)}, f32[176,128]{1,0:T(8,128)S(1)}, u32[]{:S(2)}, u32[]{:S(2)}) collective-permute-start(f32[176,128]{1,0:T(8,128)S(1)} %dynamic-slice_add_fusion), channel_id=1, source_target_pairs={{0,12},{1,13},{2,14},{3,15},{4,8},{5,9},{6,10},{7,11},{8,4},{9,5},... | collective-permute-start | bytes 270344 | tf_op jit(solution)/shard_map/ppermute | solution.py:568
  40.7 0.0 collective-permute-start.4
  40.7 1.0 collective-permute-start.3
  41.6 0.9 constant_dynamic-slice_fusion
  42.5 0.7 pad.4.kl_hbm
  43.2 9.0 %base.1 = (f32[11,352,128]{2,1,0:T(8,128)}, f32[11,352,128]{2,1,0:T(8,128)}) custom-call(s32[1]{0:T(128)} %bitcast.6.rank_ref, s32[8,176]{1,0:T(8,128)} %bitcast.33, f32[11,352,128]{2,1,0:T(8,128)} %bitcast.20, f32[11,352,128]{2,1,0:T(8,128)} %bitcast.25, f32[11,352,128]{2,1,0:T(8,128)} %bitcast.22, f32[352,128]{1,0:T(8,128)} %bitcast.27, ...), custom_call_target="tpu_custom_call" | custom-call | flops 29736960 | bytes 11894784 | tf_op jit(solution)/shard_map/base/pallas_call | solution.py:576
  52.2 6.4 %collective-permute-done.5 = f32[176,128]{1,0:T(8,128)S(1)} collective-permute-done((f32[176,128]{1,0:T(8,128)S(1)}, f32[176,128]{1,0:T(8,128)S(1)}, u32[]{:S(2)}, u32[]{:S(2)}) %collective-permute-start.5) | collective-permute-done | bytes 90144 | tf_op jit(solution)/shard_map/ppermute | solution.py:568
  58.6 0.0 collective-permute-done.4
  58.6 0.0 collective-permute-done.3
  58.7 0.0 all-to-all-done.recv_hbm
  58.7 3.1 %collective-permute-start.6 = (f32[176,128]{1,0:T(8,128)S(1)}, f32[176,128]{1,0:T(8,128)S(1)}, u32[]{:S(2)}, u32[]{:S(2)}) collective-permute-start(f32[176,128]{1,0:T(8,128)S(1)} %add_add_fusion), channel_id=1, source_target_pairs={{0,2},{1,3},{2,0},{3,1},{4,6},{5,7},{6,4},{7,5},{8,10},{9,11},{10,... | collective-permute-start | bytes 270344 | tf_op jit(solution)/shard_map/ppermute | solution.py:568
  61.7 5.6 %contract.1 = bf16[16,496,128]{2,1,0:T(8,128)(2,1)} custom-call(s32[165]{0:T(256)} %fusion.1.places, bf16[16,496,128]{2,1,0:T(8,128)(2,1)} %all-to-all-done.recv_hbm, f32[8,24,128]{2,1,0:T(8,128)} %pad.4.kl_hbm), custom_call_target="tpu_custom_call" | custom-call | flops 39649280 | bytes 7929856 | tf_op jit(solution)/shard_map/contract/pallas_call | solution.py:598
  67.3 0.0 collective-permute-done.6
  67.4 4.4 %all-to-all-start.1 = ((bf16[16,496,128]{2,1,0:T(8,128)(2,1)}), bf16[16,496,128]{2,1,0:T(8,128)(2,1)}, u32[]{:S(2)}, u32[]{:S(2)}) async-start(bf16[16,496,128]{2,1,0:T(8,128)(2,1)} %contract.1), calls=%async_computation.1 | async-start | bytes 4063232 | tf_op jit(solution)/shard_map/all_to_all | solution.py:523
  71.8 0.2 collective-permute-start.7
  72.1 1.1 %collective-permute-done.7 = f32[176,128]{1,0:T(8,128)S(1)} collective-permute-done((f32[176,128]{1,0:T(8,128)S(1)}, f32[176,128]{1,0:T(8,128)S(1)}, u32[]{:S(2)}, u32[]{:S(2)}) %collective-permute-start.7) | collective-permute-done | bytes 90144 | tf_op jit(solution)/shard_map/ppermute | solution.py:568
  73.2 1.9 %collective-permute-start.8 = (f32[32,128]{1,0:T(8,128)S(1)}, f32[32,128]{1,0:T(8,128)S(1)}, u32[]{:S(2)}, u32[]{:S(2)}) collective-permute-start(f32[32,128]{1,0:T(8,128)S(1)} %slice.32), channel_id=1, source_target_pairs={{0,16},{16,32},{32,48},{48,64},{64,80},{80,96},{96,112},{112,128},... | collective-permute-start | bytes 49160 | tf_op jit(solution)/shard_map/ppermute | solution.py:626
  75.2 6.0 %collective-permute-start.9 = (f32[32,128]{1,0:T(8,128)S(1)}, f32[32,128]{1,0:T(8,128)S(1)}, u32[]{:S(2)}, u32[]{:S(2)}) collective-permute-start(f32[32,128]{1,0:T(8,128)S(1)} %slice.33), channel_id=1, source_target_pairs={{16,0},{32,16},{48,32},{64,48},{80,64},{96,80},{112,96},{128,112},... | collective-permute-start | bytes 49160 | tf_op jit(solution)/shard_map/ppermute | solution.py:627
  81.2 0.7 pad_maximum_fusion.2.head_hbm
  81.9 0.0 collective-permute-done.8.head_low_hbm
  81.9 0.0 copy-start.3
  81.9 0.7 collective-permute-done.9.head_high_hbm
  82.6 0.0 copy-done.3
  82.6 0.0 copy-start.4
  82.6 0.6 copy-done.4
  83.2 5.3 %advection.1.base_c_hbm = f32[11,352,128]{2,1,0:T(8,128)} custom-call(f32[11,352,128]{2,1,0:T(8,128)} %bitcast.23, bf16[22,32,128]{2,1,0:T(8,128)(2,1)} %copy-done, bf16[22,32,128]{2,1,0:T(8,128)(2,1)} %copy-done.1, f32[11,352,128]{2,1,0:T(8,128)} %get-tuple-element.26.base_hbm, f32[352,128]{1,0:T(8,128)} %bitcast.28, ...), custom_call_target="tpu_custom_call" | custom-call | flops 9912320 | bytes 5947392 | tf_op jit(solution)/shard_map/advection/pallas_call | solution.py:628
  88.5 12.2 %all-to-all-done.1.recv_hbm = bf16[16,496,128]{2,1,0:T(8,128)(2,1)} async-done(((bf16[16,496,128]{2,1,0:T(8,128)(2,1)}), bf16[16,496,128]{2,1,0:T(8,128)(2,1)}, u32[]{:S(2)}, u32[]{:S(2)}) %all-to-all-start.1) | async-done | bytes 2031648 | tf_op jit(solution)/shard_map/all_to_all | solution.py:523
  100.7 4.5 %result.1 = (f32[11,352,128]{2,1,0:T(8,128)}, f32[11,352,128]{2,1,0:T(8,128)}) custom-call(bf16[16,496,128]{2,1,0:T(8,128)(2,1)} %all-to-all-done.1.recv_hbm, f32[11,352,128]{2,1,0:T(8,128)} %get-tuple-element.25.base_p_hbm, f32[11,352,128]{2,1,0:T(8,128)} %advection.1.base_c_hbm, f32[352,128]{1,0:T(8,128)} %bitcast.29), custom_call_target="tpu_custom_call" | custom-call | flops 3964928 | bytes 9912320 | tf_op jit(solution)/shard_map/result/pallas_call | solution.py:639
  (7 shorter events, 0.1 us)
Async XLA Ops:
  1.9 16.7 %collective-permute-start = (bf16[22,32,128]{2,1,0:T(8,128)(2,1)S(1)}, bf16[22,32,128]{2,1,0:T(8,128)(2,1)S(1)}, u32[]{:S(2)}, u32[]{:S(2)}) collective-permute-start(bf16[22,32,128]{2,1,0:T(8,128)(2,1)S(1)} %pad_maximum_fusion), channel_id=1, source_target_pairs={{0,16},{16,32},{32,48},{48,64},{64,80},{80,96},{96,112},{112,128},... | collective-permute-start | bytes 540680 | tf_op jit(solution)/shard_map/ppermute | solution.py:499
  5.8 12.9 %collective-permute-start.1 = (bf16[22,32,128]{2,1,0:T(8,128)(2,1)S(1)}, bf16[22,32,128]{2,1,0:T(8,128)(2,1)S(1)}, u32[]{:S(2)}, u32[]{:S(2)}) collective-permute-start(bf16[22,32,128]{2,1,0:T(8,128)(2,1)S(1)} %pad_maximum_fusion.1), channel_id=1, source_target_pairs={{16,0},{32,16},{48,32},{64,48},{80,64},{96,80},{112,96},{128,112},... | collective-permute-start | bytes 540680 | tf_op jit(solution)/shard_map/ppermute | solution.py:500
  18.7 0.7 copy-start
  18.7 0.7 copy-start.1
  22.0 6.7 %copy-start.2 = (s32[176,8]{0,1:T(8,128)S(1)}, s32[176,8]{0,1:T(8,128)}, u32[]{:S(2)}) copy-start(s32[176,8]{0,1:T(8,128)} %param.13) | copy-start | bytes 16900
  22.0 6.7 %copy-start.6 = (s32[8]{0:T(128)S(1)}, s32[8]{0:T(128)}, u32[]{:S(2)}) copy-start(s32[8]{0:T(128)} %constant.61) | copy-start | bytes 100
  22.1 6.8 %copy-start.5 = (s32[165]{0:T(256)S(1)}, s32[165]{0:T(256)}, u32[]{:S(2)}) copy-start(s32[165]{0:T(256)} %constant.62) | copy-start | bytes 1984
  22.1 36.6 %all-to-all-start = ((bf16[16,496,128]{2,1,0:T(8,128)(2,1)}), bf16[16,496,128]{2,1,0:T(8,128)(2,1)}, u32[]{:S(2)}, u32[]{:S(2)}) async-start(bf16[16,496,128]{2,1,0:T(8,128)(2,1)} %outer_images.1), calls=%async_computation | async-start | bytes 4063232 | tf_op jit(solution)/shard_map/all_to_all | solution.py:523
  32.7 1.3 %collective-permute-start.2 = (f32[176,128]{1,0:T(8,128)S(1)}, f32[176,128]{1,0:T(8,128)S(1)}, u32[]{:S(2)}, u32[]{:S(2)}) collective-permute-start(f32[176,128]{1,0:T(8,128)S(1)} %constant_dynamic-slice_fusion.1), channel_id=1, source_target_pairs={{0,1},{1,0},{2,3},{3,2},{4,5},{5,4},{6,7},{7,6},{8,9},{9,8},{10,11... | collective-permute-start | bytes 270344 | tf_op jit(solution)/shard_map/ppermute | solution.py:568
  34.9 23.7 %collective-permute-start.5 = (f32[176,128]{1,0:T(8,128)S(1)}, f32[176,128]{1,0:T(8,128)S(1)}, u32[]{:S(2)}, u32[]{:S(2)}) collective-permute-start(f32[176,128]{1,0:T(8,128)S(1)} %dynamic-slice_add_fusion), channel_id=1, source_target_pairs={{0,12},{1,13},{2,14},{3,15},{4,8},{5,9},{6,10},{7,11},{8,4},{9,5},... | collective-permute-start | bytes 270344 | tf_op jit(solution)/shard_map/ppermute | solution.py:568
  40.7 18.0 %collective-permute-start.4 = (f32[176,128]{1,0:T(8,128)S(1)}, f32[176,128]{1,0:T(8,128)S(1)}, u32[]{:S(2)}, u32[]{:S(2)}) collective-permute-start(f32[176,128]{1,0:T(8,128)S(1)} %dynamic-slice_add_fusion), channel_id=1, source_target_pairs={{0,8},{1,9},{2,10},{3,11},{4,12},{5,13},{6,14},{7,15},{8,0},{9,1},... | collective-permute-start | bytes 270344 | tf_op jit(solution)/shard_map/ppermute | solution.py:568
  40.7 18.0 %collective-permute-start.3 = (f32[176,128]{1,0:T(8,128)S(1)}, f32[176,128]{1,0:T(8,128)S(1)}, u32[]{:S(2)}, u32[]{:S(2)}) collective-permute-start(f32[176,128]{1,0:T(8,128)S(1)} %dynamic-slice_add_fusion), channel_id=1, source_target_pairs={{0,4},{1,5},{2,6},{3,7},{4,0},{5,1},{6,2},{7,3},{8,12},{9,13},{10,... | collective-permute-start | bytes 270344 | tf_op jit(solution)/shard_map/ppermute | solution.py:568
  58.7 8.7 %collective-permute-start.6 = (f32[176,128]{1,0:T(8,128)S(1)}, f32[176,128]{1,0:T(8,128)S(1)}, u32[]{:S(2)}, u32[]{:S(2)}) collective-permute-start(f32[176,128]{1,0:T(8,128)S(1)} %add_add_fusion), channel_id=1, source_target_pairs={{0,2},{1,3},{2,0},{3,1},{4,6},{5,7},{6,4},{7,5},{8,10},{9,11},{10,... | collective-permute-start | bytes 270344 | tf_op jit(solution)/shard_map/ppermute | solution.py:568
  67.4 33.3 %all-to-all-start.1 = ((bf16[16,496,128]{2,1,0:T(8,128)(2,1)}), bf16[16,496,128]{2,1,0:T(8,128)(2,1)}, u32[]{:S(2)}, u32[]{:S(2)}) async-start(bf16[16,496,128]{2,1,0:T(8,128)(2,1)} %contract.1), calls=%async_computation.1 | async-start | bytes 4063232 | tf_op jit(solution)/shard_map/all_to_all | solution.py:523
  71.8 1.4 %collective-permute-start.7 = (f32[176,128]{1,0:T(8,128)S(1)}, f32[176,128]{1,0:T(8,128)S(1)}, u32[]{:S(2)}, u32[]{:S(2)}) collective-permute-start(f32[176,128]{1,0:T(8,128)S(1)} %add.50), channel_id=1, source_target_pairs={{0,1},{1,0},{2,3},{3,2},{4,5},{5,4},{6,7},{7,6},{8,9},{9,8},{10,11... | collective-permute-start | bytes 270344 | tf_op jit(solution)/shard_map/ppermute | solution.py:568
  73.2 8.7 %collective-permute-start.8 = (f32[32,128]{1,0:T(8,128)S(1)}, f32[32,128]{1,0:T(8,128)S(1)}, u32[]{:S(2)}, u32[]{:S(2)}) collective-permute-start(f32[32,128]{1,0:T(8,128)S(1)} %slice.32), channel_id=1, source_target_pairs={{0,16},{16,32},{32,48},{48,64},{64,80},{80,96},{96,112},{112,128},... | collective-permute-start | bytes 49160 | tf_op jit(solution)/shard_map/ppermute | solution.py:626
  75.2 7.5 %collective-permute-start.9 = (f32[32,128]{1,0:T(8,128)S(1)}, f32[32,128]{1,0:T(8,128)S(1)}, u32[]{:S(2)}, u32[]{:S(2)}) collective-permute-start(f32[32,128]{1,0:T(8,128)S(1)} %slice.33), channel_id=1, source_target_pairs={{16,0},{32,16},{48,32},{64,48},{80,64},{96,80},{112,96},{128,112},... | collective-permute-start | bytes 49160 | tf_op jit(solution)/shard_map/ppermute | solution.py:627
  81.9 0.7 copy-start.3
  82.6 0.6 copy-start.4

commit v6 on v5

--- a/solution.py
+++ b/solution.py
@@ -411,12 +411,12 @@
     fetch_mean.wait()
     scale[pl.ds(0, SLAB), :] = OMEGA / (6.0 * mean[...])
 
-    def spread(rank):
-        fetch(rank).wait()
-        unpack_rank(recv, rank, sums, STRIDE, range(SENT // 16))
-
-    loop(0, RANKS, spread)
-    for index in range(2):
+    loop(0, RANKS, lambda rank: fetch(rank).wait())
+    whole = (BODY + 15) // 16
+    for index, blocks in enumerate((range(whole), range(whole, SENT // 16))):
+
+        def spread(rank):
+            unpack_rank(recv, rank, sums, STRIDE, blocks)
 
         def one_mode(m):
             fetch_base(index, m).wait()
@@ -428,6 +428,7 @@
                     out[at, :] = base[at, :] - factor * total
             leave(index, m).start()
 
+        loop(0, RANKS, spread)
         loop(0, MODES, one_mode)
     for index in range(2):
         loop(0, MODES, lambda m: leave(index, m).wait())

time: 106 us -> 106 us (level)
  starting transfers between devices: 39 us -> 36.1 us
  Pallas kernels: 36.9 us -> 39.4 us
    ppermute x6, starting transfers between devices: 10.3 us -> 7.47 us  [partner(): return lax.ppermute(rows, 'mode', [(i, i ^ bits) for i in range(RANKS)])]
    pallas_call x1, Pallas kernels: 2.8 us -> 5.36 us  [local(): call(head_kernel, plane, [smem(), smem()] + [hbm()] * 6, [rows_vmem(SLAB...]
  transfers between devices with their start and end apart: 12 -> 12, of which waited for: 5 -> 5; matrix products, arithmetic and copies ran while one was open for 5% -> 5% of each run, Pallas kernels for 28% -> 31%
where the time goes in v6:
time: 106 us; the launch traced here: 105 us
  Pallas kernels  39.4 us (37%)
  starting transfers between devices  36.1 us (34%)
  waiting for transfers between devices  21.1 us (20%)
  local copies, waits for them, and re-layouts  5.09 us (5%)
  other arithmetic  2.56 us (2%)
    all_to_all x2, waiting for transfers between devices, exchange(): return lax.all_to_all(rows_of_ranks, 'mode', 0, 0, tiled=True)  12.2 us
    all_to_all x2, starting transfers between devices, exchange(): return lax.all_to_all(rows_of_ranks, 'mode', 0, 0, tiled=True)  11.1 us
    pallas_call x1, Pallas kernels, local(): call(base_kernel, (field, field), [smem(), smem()] + [hbm()] * 6, [rows_v...  9.05 us
    ppermute x6, waiting for transfers between devices, partner(): return lax.ppermute(rows, 'mode', [(i, i ^ bits) for i in range(RANKS)])  8.16 us
    ppermute x6, starting transfers between devices, partner(): return lax.ppermute(rows, 'mode', [(i, i ^ bits) for i in range(RANKS)])  7.47 us
    pallas_call x1, Pallas kernels, local(): call(inner_kernel, (message(SENT), jax.ShapeDtypeStruct((4, SENT, CZ), F3...  7.04 us
    ppermute x1, starting transfers between devices, local(): head_high = lax.ppermute(head[:CY], 'space', down)  6.03 us
    ppermute x1, starting transfers between devices, local(): high = lax.ppermute(first, 'space', down)  5.83 us
  transfers between devices with their start and end apart: 12, of which 5 were waited for; matrix products, arithmetic and copies ran while one was open for 5% of the time, Pallas kernels for 31%

profile of v6, /device:TPU:2, one launch (start us, length us, event | category | flops | bytes accessed | tf_op | source)
XLA Modules:
  0.0 105.2 jit_solution(4858186424335792877)
XLA Ops:
  0.6 1.3 %slice_bitcast_fusion = (bf16[11,32,128]{2,1,0:T(8,128)(2,1)S(1)}, bf16[11,32,128]{2,1,0:T(8,128)(2,1)S(1)}, bf16[11,32,128]{2,1,0:T(8,128)(2,1)S(1)}, bf16[11,32,128]{2,1,0:T(8,128)(2,1)S(1)}) fusion(f32[11,11,32,128]{3,2,1,0:T(8,128)} %param.8, f32[11,11,32,128]{3,2,1,0:T(8,128)} %param.10), kind=kLoop, calls=%fused_computation.6 | loop fusion | bytes 720896 | tf_op jit(solution)/shard_map/squeeze | solution.py:499
  1.9 3.8 %collective-permute-start = (bf16[22,32,128]{2,1,0:T(8,128)(2,1)S(1)}, bf16[22,32,128]{2,1,0:T(8,128)(2,1)S(1)}, u32[]{:S(2)}, u32[]{:S(2)}) collective-permute-start(bf16[22,32,128]{2,1,0:T(8,128)(2,1)S(1)} %pad_maximum_fusion), channel_id=1, source_target_pairs={{0,16},{16,32},{32,48},{48,64},{64,80},{80,96},{96,112},{112,128},... | collective-permute-start | bytes 540680 | tf_op jit(solution)/shard_map/ppermute | solution.py:500
  5.8 5.8 %collective-permute-start.1 = (bf16[22,32,128]{2,1,0:T(8,128)(2,1)S(1)}, bf16[22,32,128]{2,1,0:T(8,128)(2,1)S(1)}, u32[]{:S(2)}, u32[]{:S(2)}) collective-permute-start(bf16[22,32,128]{2,1,0:T(8,128)(2,1)S(1)} %pad_maximum_fusion.1), channel_id=1, source_target_pairs={{16,0},{32,16},{48,32},{64,48},{80,64},{96,80},{112,96},{128,112},... | collective-permute-start | bytes 540680 | tf_op jit(solution)/shard_map/ppermute | solution.py:501
  11.6 7.0 %inner_images.1 = (bf16[16,496,128]{2,1,0:T(8,128)(2,1)}, f32[4,496,128]{2,1,0:T(8,128)}) custom-call(f32[11,352,128]{2,1,0:T(8,128)} %bitcast.18, f32[11,352,128]{2,1,0:T(8,128)} %bitcast.21), custom_call_target="tpu_custom_call" | custom-call | flops 9912320 | bytes 6938624 | tf_op jit(solution)/shard_map/inner_images/pallas_call | solution.py:526
  18.7 0.0 collective-permute-done.low_hbm
  18.7 0.0 copy-start
  18.7 0.0 collective-permute-done.1.high_hbm
  18.7 0.0 copy-start.1
  18.7 0.6 copy-done
  19.4 0.1 copy-done.1
  19.4 2.6 %outer_images.1 = bf16[16,496,128]{2,1,0:T(8,128)(2,1)} custom-call(f32[4,496,128]{2,1,0:T(8,128)} %get-tuple-element.16.part_hbm, bf16[22,32,128]{2,1,0:T(8,128)(2,1)} %copy-done, bf16[22,32,128]{2,1,0:T(8,128)(2,1)} %copy-done.1, bf16[16,496,128]{2,1,0:T(8,128)(2,1)} %get-tuple-element.17.send_in), custom_call_target="tpu_custom_call", output_to_operand_aliasing={{}: (3, {})} | custom-call | flops 495616 | bytes 495616 | tf_op jit(solution)/shard_map/outer_images/pallas_call | solution.py:536
  22.0 0.0 copy-start.2
  22.0 0.0 copy-start.6
  22.1 0.0 copy-start.5
  22.1 6.6 %all-to-all-start = ((bf16[16,496,128]{2,1,0:T(8,128)(2,1)}), bf16[16,496,128]{2,1,0:T(8,128)(2,1)}, u32[]{:S(2)}, u32[]{:S(2)}) async-start(bf16[16,496,128]{2,1,0:T(8,128)(2,1)} %outer_images.1), calls=%async_computation | async-start | bytes 4063232 | tf_op jit(solution)/shard_map/all_to_all | solution.py:524
  28.7 0.0 copy-done.2
  28.7 0.0 copy-done.6
  28.7 0.1 multiply_reduce_fusion
  28.8 0.0 copy-done.5
  28.8 0.2 select_reduce_fusion
  29.0 5.4 %head_part.1 = f32[352,128]{1,0:T(8,128)} custom-call(s32[1]{0:T(128)} %bitcast.6.rank_ref, s32[8,176]{1,0:T(8,128)} %bitcast.32, f32[11,352,128]{2,1,0:T(8,128)} %bitcast.19, f32[11,352,128]{2,1,0:T(8,128)} %bitcast.24, f32[352,128]{1,0:T(8,128)} %bitcast.26, f32[8,352,128]{2,1,0:T(8,128)} %bitcast.30, bf16[22,32,128]{2,1,0:T(8,128)(2,1)} %copy-done, ...), custom_call_target="tpu_custom_call" | custom-call | flops 495616 | bytes 495616 | tf_op jit(solution)/shard_map/head_part/pallas_call | solution.py:557
  34.4 0.9 constant_dynamic-slice_fusion.1
  35.3 0.0 collective-permute-start.2
  35.3 0.6 fusion.1.places
  35.9 0.7 collective-permute-done.2
  36.6 0.9 dynamic-slice_add_fusion
  37.5 3.2 %collective-permute-start.5 = (f32[176,128]{1,0:T(8,128)S(1)}, f32[176,128]{1,0:T(8,128)S(1)}, u32[]{:S(2)}, u32[]{:S(2)}) collective-permute-start(f32[176,128]{1,0:T(8,128)S(1)} %dynamic-slice_add_fusion), channel_id=1, source_target_pairs={{0,12},{1,13},{2,14},{3,15},{4,8},{5,9},{6,10},{7,11},{8,4},{9,5},... | collective-permute-start | bytes 270344 | tf_op jit(solution)/shard_map/ppermute | solution.py:569
  40.7 0.0 collective-permute-start.4
  40.7 1.0 collective-permute-start.3
  41.7 0.9 constant_dynamic-slice_fusion
  42.6 0.7 pad.4.kl_hbm
  43.2 9.0 %base.1 = (f32[11,352,128]{2,1,0:T(8,128)}, f32[11,352,128]{2,1,0:T(8,128)}) custom-call(s32[1]{0:T(128)} %bitcast.6.rank_ref, s32[8,176]{1,0:T(8,128)} %bitcast.33, f32[11,352,128]{2,1,0:T(8,128)} %bitcast.20, f32[11,352,128]{2,1,0:T(8,128)} %bitcast.25, f32[11,352,128]{2,1,0:T(8,128)} %bitcast.22, f32[352,128]{1,0:T(8,128)} %bitcast.27, ...), custom_call_target="tpu_custom_call" | custom-call | flops 29736960 | bytes 11894784 | tf_op jit(solution)/shard_map/base/pallas_call | solution.py:577
  52.3 6.3 %collective-permute-done.5 = f32[176,128]{1,0:T(8,128)S(1)} collective-permute-done((f32[176,128]{1,0:T(8,128)S(1)}, f32[176,128]{1,0:T(8,128)S(1)}, u32[]{:S(2)}, u32[]{:S(2)}) %collective-permute-start.5) | collective-permute-done | bytes 90144 | tf_op jit(solution)/shard_map/ppermute | solution.py:569
  58.6 0.0 collective-permute-done.4
  58.6 0.0 collective-permute-done.3
  58.7 0.0 all-to-all-done.recv_hbm
  58.7 3.1 %collective-permute-start.6 = (f32[176,128]{1,0:T(8,128)S(1)}, f32[176,128]{1,0:T(8,128)S(1)}, u32[]{:S(2)}, u32[]{:S(2)}) collective-permute-start(f32[176,128]{1,0:T(8,128)S(1)} %add_add_fusion), channel_id=1, source_target_pairs={{0,2},{1,3},{2,0},{3,1},{4,6},{5,7},{6,4},{7,5},{8,10},{9,11},{10,... | collective-permute-start | bytes 270344 | tf_op jit(solution)/shard_map/ppermute | solution.py:569
  61.7 5.6 %contract.1 = bf16[16,496,128]{2,1,0:T(8,128)(2,1)} custom-call(s32[165]{0:T(256)} %fusion.1.places, bf16[16,496,128]{2,1,0:T(8,128)(2,1)} %all-to-all-done.recv_hbm, f32[8,24,128]{2,1,0:T(8,128)} %pad.4.kl_hbm), custom_call_target="tpu_custom_call" | custom-call | flops 39649280 | bytes 7929856 | tf_op jit(solution)/shard_map/contract/pallas_call | solution.py:599
  67.3 0.0 collective-permute-done.6
  67.3 4.4 %all-to-all-start.1 = ((bf16[16,496,128]{2,1,0:T(8,128)(2,1)}), bf16[16,496,128]{2,1,0:T(8,128)(2,1)}, u32[]{:S(2)}, u32[]{:S(2)}) async-start(bf16[16,496,128]{2,1,0:T(8,128)(2,1)} %contract.1), calls=%async_computation.1 | async-start | bytes 4063232 | tf_op jit(solution)/shard_map/all_to_all | solution.py:524
  71.8 0.2 collective-permute-start.7
  72.0 1.1 %collective-permute-done.7 = f32[176,128]{1,0:T(8,128)S(1)} collective-permute-done((f32[176,128]{1,0:T(8,128)S(1)}, f32[176,128]{1,0:T(8,128)S(1)}, u32[]{:S(2)}, u32[]{:S(2)}) %collective-permute-start.7) | collective-permute-done | bytes 90144 | tf_op jit(solution)/shard_map/ppermute | solution.py:569
  73.2 1.9 %collective-permute-start.8 = (f32[32,128]{1,0:T(8,128)S(1)}, f32[32,128]{1,0:T(8,128)S(1)}, u32[]{:S(2)}, u32[]{:S(2)}) collective-permute-start(f32[32,128]{1,0:T(8,128)S(1)} %slice.32), channel_id=1, source_target_pairs={{0,16},{16,32},{32,48},{48,64},{64,80},{80,96},{96,112},{112,128},... | collective-permute-start | bytes 49160 | tf_op jit(solution)/shard_map/ppermute | solution.py:627
  75.1 6.0 %collective-permute-start.9 = (f32[32,128]{1,0:T(8,128)S(1)}, f32[32,128]{1,0:T(8,128)S(1)}, u32[]{:S(2)}, u32[]{:S(2)}) collective-permute-start(f32[32,128]{1,0:T(8,128)S(1)} %slice.33), channel_id=1, source_target_pairs={{16,0},{32,16},{48,32},{64,48},{80,64},{96,80},{112,96},{128,112},... | collective-permute-start | bytes 49160 | tf_op jit(solution)/shard_map/ppermute | solution.py:628
  81.2 0.7 pad_maximum_fusion.2.head_hbm
  81.9 0.0 collective-permute-done.8.head_low_hbm
  81.9 0.0 copy-start.3
  81.9 0.7 collective-permute-done.9.head_high_hbm
  82.6 0.0 copy-done.3
  82.6 0.0 copy-start.4
  82.6 0.6 copy-done.4
  83.2 5.3 %advection.1.base_c_hbm = f32[11,352,128]{2,1,0:T(8,128)} custom-call(f32[11,352,128]{2,1,0:T(8,128)} %bitcast.23, bf16[22,32,128]{2,1,0:T(8,128)(2,1)} %copy-done, bf16[22,32,128]{2,1,0:T(8,128)(2,1)} %copy-done.1, f32[11,352,128]{2,1,0:T(8,128)} %get-tuple-element.26.base_hbm, f32[352,128]{1,0:T(8,128)} %bitcast.28, ...), custom_call_target="tpu_custom_call" | custom-call | flops 9912320 | bytes 5947392 | tf_op jit(solution)/shard_map/advection/pallas_call | solution.py:629
  88.5 12.2 %all-to-all-done.1.recv_hbm = bf16[16,496,128]{2,1,0:T(8,128)(2,1)} async-done(((bf16[16,496,128]{2,1,0:T(8,128)(2,1)}), bf16[16,496,128]{2,1,0:T(8,128)(2,1)}, u32[]{:S(2)}, u32[]{:S(2)}) %all-to-all-start.1) | async-done | bytes 2031648 | tf_op jit(solution)/shard_map/all_to_all | solution.py:524
  100.7 4.5 %result.1 = (f32[11,352,128]{2,1,0:T(8,128)}, f32[11,352,128]{2,1,0:T(8,128)}) custom-call(bf16[16,496,128]{2,1,0:T(8,128)(2,1)} %all-to-all-done.1.recv_hbm, f32[11,352,128]{2,1,0:T(8,128)} %get-tuple-element.25.base_p_hbm, f32[11,352,128]{2,1,0:T(8,128)} %advection.1.base_c_hbm, f32[352,128]{1,0:T(8,128)} %bitcast.29), custom_call_target="tpu_custom_call" | custom-call | flops 3964928 | bytes 9912320 | tf_op jit(solution)/shard_map/result/pallas_call | solution.py:640
  (7 shorter events, 0.1 us)
Async XLA Ops:
  1.9 16.7 %collective-permute-start = (bf16[22,32,128]{2,1,0:T(8,128)(2,1)S(1)}, bf16[22,32,128]{2,1,0:T(8,128)(2,1)S(1)}, u32[]{:S(2)}, u32[]{:S(2)}) collective-permute-start(bf16[22,32,128]{2,1,0:T(8,128)(2,1)S(1)} %pad_maximum_fusion), channel_id=1, source_target_pairs={{0,16},{16,32},{32,48},{48,64},{64,80},{80,96},{96,112},{112,128},... | collective-permute-start | bytes 540680 | tf_op jit(solution)/shard_map/ppermute | solution.py:500
  5.8 12.9 %collective-permute-start.1 = (bf16[22,32,128]{2,1,0:T(8,128)(2,1)S(1)}, bf16[22,32,128]{2,1,0:T(8,128)(2,1)S(1)}, u32[]{:S(2)}, u32[]{:S(2)}) collective-permute-start(bf16[22,32,128]{2,1,0:T(8,128)(2,1)S(1)} %pad_maximum_fusion.1), channel_id=1, source_target_pairs={{16,0},{32,16},{48,32},{64,48},{80,64},{96,80},{112,96},{128,112},... | collective-permute-start | bytes 540680 | tf_op jit(solution)/shard_map/ppermute | solution.py:501
  18.7 0.7 copy-start
  18.7 0.7 copy-start.1
  22.0 6.7 %copy-start.2 = (s32[176,8]{0,1:T(8,128)S(1)}, s32[176,8]{0,1:T(8,128)}, u32[]{:S(2)}) copy-start(s32[176,8]{0,1:T(8,128)} %param.13) | copy-start | bytes 16900
  22.0 6.7 %copy-start.6 = (s32[8]{0:T(128)S(1)}, s32[8]{0:T(128)}, u32[]{:S(2)}) copy-start(s32[8]{0:T(128)} %constant.61) | copy-start | bytes 100
  22.1 6.8 %copy-start.5 = (s32[165]{0:T(256)S(1)}, s32[165]{0:T(256)}, u32[]{:S(2)}) copy-start(s32[165]{0:T(256)} %constant.62) | copy-start | bytes 1984
  22.1 36.6 %all-to-all-start = ((bf16[16,496,128]{2,1,0:T(8,128)(2,1)}), bf16[16,496,128]{2,1,0:T(8,128)(2,1)}, u32[]{:S(2)}, u32[]{:S(2)}) async-start(bf16[16,496,128]{2,1,0:T(8,128)(2,1)} %outer_images.1), calls=%async_computation | async-start | bytes 4063232 | tf_op jit(solution)/shard_map/all_to_all | solution.py:524
  35.3 1.3 %collective-permute-start.2 = (f32[176,128]{1,0:T(8,128)S(1)}, f32[176,128]{1,0:T(8,128)S(1)}, u32[]{:S(2)}, u32[]{:S(2)}) collective-permute-start(f32[176,128]{1,0:T(8,128)S(1)} %constant_dynamic-slice_fusion.1), channel_id=1, source_target_pairs={{0,1},{1,0},{2,3},{3,2},{4,5},{5,4},{6,7},{7,6},{8,9},{9,8},{10,11... | collective-permute-start | bytes 270344 | tf_op jit(solution)/shard_map/ppermute | solution.py:569
  37.5 21.1 %collective-permute-start.5 = (f32[176,128]{1,0:T(8,128)S(1)}, f32[176,128]{1,0:T(8,128)S(1)}, u32[]{:S(2)}, u32[]{:S(2)}) collective-permute-start(f32[176,128]{1,0:T(8,128)S(1)} %dynamic-slice_add_fusion), channel_id=1, source_target_pairs={{0,12},{1,13},{2,14},{3,15},{4,8},{5,9},{6,10},{7,11},{8,4},{9,5},... | collective-permute-start | bytes 270344 | tf_op jit(solution)/shard_map/ppermute | solution.py:569
  40.7 18.0 %collective-permute-start.4 = (f32[176,128]{1,0:T(8,128)S(1)}, f32[176,128]{1,0:T(8,128)S(1)}, u32[]{:S(2)}, u32[]{:S(2)}) collective-permute-start(f32[176,128]{1,0:T(8,128)S(1)} %dynamic-slice_add_fusion), channel_id=1, source_target_pairs={{0,8},{1,9},{2,10},{3,11},{4,12},{5,13},{6,14},{7,15},{8,0},{9,1},... | collective-permute-start | bytes 270344 | tf_op jit(solution)/shard_map/ppermute | solution.py:569
  40.7 18.0 %collective-permute-start.3 = (f32[176,128]{1,0:T(8,128)S(1)}, f32[176,128]{1,0:T(8,128)S(1)}, u32[]{:S(2)}, u32[]{:S(2)}) collective-permute-start(f32[176,128]{1,0:T(8,128)S(1)} %dynamic-slice_add_fusion), channel_id=1, source_target_pairs={{0,4},{1,5},{2,6},{3,7},{4,0},{5,1},{6,2},{7,3},{8,12},{9,13},{10,... | collective-permute-start | bytes 270344 | tf_op jit(solution)/shard_map/ppermute | solution.py:569
  58.7 8.6 %collective-permute-start.6 = (f32[176,128]{1,0:T(8,128)S(1)}, f32[176,128]{1,0:T(8,128)S(1)}, u32[]{:S(2)}, u32[]{:S(2)}) collective-permute-start(f32[176,128]{1,0:T(8,128)S(1)} %add_add_fusion), channel_id=1, source_target_pairs={{0,2},{1,3},{2,0},{3,1},{4,6},{5,7},{6,4},{7,5},{8,10},{9,11},{10,... | collective-permute-start | bytes 270344 | tf_op jit(solution)/shard_map/ppermute | solution.py:569
  67.3 33.3 %all-to-all-start.1 = ((bf16[16,496,128]{2,1,0:T(8,128)(2,1)}), bf16[16,496,128]{2,1,0:T(8,128)(2,1)}, u32[]{:S(2)}, u32[]{:S(2)}) async-start(bf16[16,496,128]{2,1,0:T(8,128)(2,1)} %contract.1), calls=%async_computation.1 | async-start | bytes 4063232 | tf_op jit(solution)/shard_map/all_to_all | solution.py:524
  71.8 1.4 %collective-permute-start.7 = (f32[176,128]{1,0:T(8,128)S(1)}, f32[176,128]{1,0:T(8,128)S(1)}, u32[]{:S(2)}, u32[]{:S(2)}) collective-permute-start(f32[176,128]{1,0:T(8,128)S(1)} %add.50), channel_id=1, source_target_pairs={{0,1},{1,0},{2,3},{3,2},{4,5},{5,4},{6,7},{7,6},{8,9},{9,8},{10,11... | collective-permute-start | bytes 270344 | tf_op jit(solution)/shard_map/ppermute | solution.py:569
  73.2 8.7 %collective-permute-start.8 = (f32[32,128]{1,0:T(8,128)S(1)}, f32[32,128]{1,0:T(8,128)S(1)}, u32[]{:S(2)}, u32[]{:S(2)}) collective-permute-start(f32[32,128]{1,0:T(8,128)S(1)} %slice.32), channel_id=1, source_target_pairs={{0,16},{16,32},{32,48},{48,64},{64,80},{80,96},{96,112},{112,128},... | collective-permute-start | bytes 49160 | tf_op jit(solution)/shard_map/ppermute | solution.py:627
  75.1 7.5 %collective-permute-start.9 = (f32[32,128]{1,0:T(8,128)S(1)}, f32[32,128]{1,0:T(8,128)S(1)}, u32[]{:S(2)}, u32[]{:S(2)}) collective-permute-start(f32[32,128]{1,0:T(8,128)S(1)} %slice.33), channel_id=1, source_target_pairs={{16,0},{32,16},{48,32},{64,48},{80,64},{96,80},{112,96},{128,112},... | collective-permute-start | bytes 49160 | tf_op jit(solution)/shard_map/ppermute | solution.py:628
  81.9 0.7 copy-start.3
  82.6 0.6 copy-start.4
